TPU v7x, 256 devices: a whole 4x4x8 slice. The times are simulated.
256 devices in a mesh: dom: 64 (over z, y, core), hid: 4 (over x).
Axes of the slice: x: 4, y: 4, z: 8, core: 2. Of those that a mesh axis runs over, the one named last changes fastest.
Arguments:
- node_features: bfloat16 [262144, 512], P('dom', 'hid'), may hold values from -6 to 6
- weight: bfloat16 [512, 512], P(None, 'hid'), may hold values from -0.25 to 0.25
- adjacency_tiles: bfloat16 [11264, 128, 128], P('dom'), may hold values from -0.25 to 0.25
- tile_rows: int32 [64, 176], P('dom'), may hold values from 0 to 31, as said below
- tile_cols: int32 [64, 176], P('dom'), may hold values from 0 to 95, as said below
- tile_count: int32 [64], P('dom'), may hold values from 33 to 176
- send_blocks: int32 [64, 64], P('dom'), may hold values from 0 to 31
- activation_bits: int32 [262144, 32], P('dom', 'hid'), may hold values from 0 to 65535, as said below
- out_cotangent: bfloat16 [262144, 512], P('dom', 'hid'), may hold values from -6 to 6
Outputs:
- out_act: bfloat16 [262144, 512], P('dom', 'hid')
- input_grad: bfloat16 [262144, 512], P('dom', 'hid')
- weight_grad: float32 [512, 512], P(None, 'hid')
Inputs may be any that keep to these rules, and one draw needn't show every extreme that they name: `tile_rows`: the first 32 tiles of every partition have row block i and source i, for i below 32. `tile_cols`: no tile of partition p names 32 + p. `activation_bits`: every word holds 16 independent bits.
All inputs are finite; a program needn't handle non-finite values.
Results may differ from a plain program's by a relative error of at most 0.005.
Values may be sent and summed in bfloat16 or wider, within the bound.
No kernel may reach another device: no remote copies, remote signals or barrier semaphores. Data moves between devices by JAX's collectives and lax.ppermute only.
A program may use at most 128 MiB of HBM per device.

v0:
```python
import jax
import jax.numpy as jnp
from jax import lax
from jax.sharding import PartitionSpec as P


def unpack_bits(packed):
    shifts = jnp.arange(16, dtype=jnp.int32)
    bit_flags = jnp.right_shift(packed[:, :, None], shifts) & 1
    return bit_flags.reshape(packed.shape[0], packed.shape[1] * 16) > 0


def per_device(
    node_features,
    weight,
    adjacency_tiles,
    tile_rows,
    tile_cols,
    tile_count,
    send_blocks,
    activation_bits,
    out_cotangent,
):
    partitions = lax.axis_size("dom")
    tile_size = adjacency_tiles.shape[1]
    local_width = weight.shape[1]
    feature_all = lax.all_gather(node_features, "hid", axis=1, tiled=True)
    hidden = jnp.dot(feature_all, weight, preferred_element_type=jnp.float32).astype(jnp.bfloat16)
    row_blocks = hidden.shape[0] // tile_size
    hidden_blocks = hidden.reshape(row_blocks, tile_size, local_width)
    tile_row = tile_rows[0]
    tile_col = tile_cols[0]
    outgoing = send_blocks[0]
    in_list = (jnp.arange(tile_row.shape[0], dtype=jnp.int32) < tile_count[0]).astype(jnp.float32)[
        :, None, None
    ]
    incoming = lax.all_to_all(
        hidden_blocks[outgoing], "dom", split_axis=0, concat_axis=0, tiled=True
    )
    sources = jnp.concatenate([hidden_blocks, incoming], 0)
    products = (
        jnp.einsum(
            "tij,tjk->tik", adjacency_tiles, sources[tile_col], preferred_element_type=jnp.float32
        )
        * in_list
    )
    aggregated = jax.ops.segment_sum(products, tile_row, num_segments=row_blocks).reshape(
        -1, local_width
    )
    active = unpack_bits(activation_bits)
    out_act = jnp.where(active, aggregated, jnp.float32(0.0)).astype(jnp.bfloat16)
    d_aggregated = jnp.where(active, out_cotangent, jnp.zeros_like(out_cotangent))
    d_blocks = d_aggregated.reshape(row_blocks, tile_size, local_width)
    back_terms = (
        jnp.einsum(
            "tji,tjk->tik", adjacency_tiles, d_blocks[tile_row], preferred_element_type=jnp.float32
        )
        * in_list
    )
    slot_sums = jax.ops.segment_sum(back_terms, tile_col, num_segments=row_blocks + partitions)
    returned = lax.all_to_all(
        slot_sums[row_blocks:], "dom", split_axis=0, concat_axis=0, tiled=True
    )
    d_sums = slot_sums[:row_blocks] + jax.ops.segment_sum(
        returned, outgoing, num_segments=row_blocks
    )
    d_hidden = d_sums.reshape(-1, local_width).astype(jnp.bfloat16)
    weight_terms = jnp.einsum(
        "nd,nk->dk", feature_all, d_hidden, preferred_element_type=jnp.float32
    )
    weight_grad = lax.psum(weight_terms, "dom")
    partial_terms = jnp.einsum("nk,dk->nd", d_hidden, weight, preferred_element_type=jnp.float32)
    input_grad = lax.psum_scatter(partial_terms, "hid", scatter_dimension=1, tiled=True).astype(
        jnp.bfloat16
    )
    return (out_act, input_grad, weight_grad)


def solution(mesh):
    placed = (
        P("dom", "hid"),
        P(None, "hid"),
        P("dom", None, None),
        P("dom", None),
        P("dom", None),
        P("dom"),
        P("dom", None),
        P("dom", "hid"),
        P("dom", "hid"),
    )
    return jax.shard_map(
        per_device,
        mesh=mesh,
        in_specs=placed,
        out_specs=(P("dom", "hid"), P("dom", "hid"), P(None, "hid")),
        check_vma=False,
    )
```

profile of v0, /device:TPU:6, one launch (start us, length us, event | category | flops | bytes accessed | tf_op | source)
XLA Modules:
  0.0 649.2 jit_solution(336017460157297907)
XLA Ops:
  7.2 0.0 copy-start
  7.2 0.0 all-gather.2.cloned.1.call-start
  7.2 0.7 all-gather.2.cloned.1.call-update
  7.9 0.7 fusion.3
  8.6 58.0 %all-gather.2.cloned.1.call-done = bf16[4096,512]{1,0:T(8,128)(2,1)} async-done(((bf16[4096,128]{1,0:T(8,128)(2,1)}), bf16[4096,512]{1,0:T(8,128)(2,1)}) %all-gather.2.cloned.1.call-update) | async-done | bytes 4194320 | tf_op jit(solution)/shard_map/all_gather | solution.py:27
  66.6 3.4 convolution_convert_fusion
  70.0 0.0 copy-start.1
  70.1 0.0 copy-start.3
  70.1 0.0 copy-start.6
  70.1 0.0 copy-start.5
  70.1 2.1 gather_fusion
  72.2 10.9 %all-to-all-start = ((bf16[64,128,128]{2,1,0:T(8,128)(2,1)}), bf16[64,128,128]{2,1,0:T(8,128)(2,1)}, u32[]{:S(2)}, u32[]{:S(2)}) async-start(bf16[64,128,128]{2,1,0:T(8,128)(2,1)} %gather_fusion), calls=%async_computation | async-start | bytes 4194304 | tf_op jit(solution)/shard_map/all_to_all | solution.py:37
  83.8 1.3 copy.19
  85.2 0.1 shift_right_arithmetic.23
  85.3 48.9 %all-to-all-done = bf16[64,128,128]{2,1,0:T(8,128)(2,1)} async-done(((bf16[64,128,128]{2,1,0:T(8,128)(2,1)}), bf16[64,128,128]{2,1,0:T(8,128)(2,1)}, u32[]{:S(2)}, u32[]{:S(2)}) %all-to-all-start) | async-done | bytes 2097184 | tf_op jit(solution)/shard_map/all_to_all | solution.py:37
  134.2 2.1 pad_maximum_fusion
  136.3 7.8 %gather_fusion.1 = bf16[176,128,128]{2,1,0:T(8,128)(2,1)} fusion(bf16[96,128,128]{2,1,0:T(8,128)(2,1)S(1)} %pad_maximum_fusion, s32[1024]{0:T(1024)S(1)} %pad_clamp_fusion.1), kind=kCustom, calls=%fused_computation.1 | custom fusion | bytes 11535040 | tf_op jit(solution)/shard_map/gather | solution.py:43
  144.2 12.9 %multiply_bitcast_fusion.1 = f32[176,128,128]{1,2,0:T(8,128)} fusion(f32[176]{0:T(256)S(1)} %compare_convert_fusion, bf16[176,128,128]{2,1,0:T(8,128)(2,1)} %gather_fusion.1, bf16[176,128,128]{2,1,0:T(8,128)(2,1)} %param.11), kind=kOutput, calls=%fused_computation.7 | convolution fusion | flops 741081088 | bytes 23069376 | tf_op jit(solution)/shard_map/tij,tjk->tik/dot_general | solution.py:42
  157.1 11.9 %copy.17 = f32[176,128,128]{2,1,0:T(8,128)} copy(f32[176,128,128]{1,2,0:T(8,128)} %multiply_bitcast_fusion.1) | data formatting | bytes 23068672 | tf_op jit(solution)/shard_map/mul | solution.py:42
  169.0 0.2 broadcast.59
  169.2 0.0 copy-start.4
  169.2 23.3 %scatter_fusion = f32[32,128,128]{2,1,0:T(8,128)S(1)} fusion(f32[32,128,128]{2,1,0:T(8,128)S(1)} %broadcast.59, s32[176]{0:T(256)S(1)} %bitcast.51, f32[176,128,128]{2,1,0:T(8,128)} %copy.17), kind=kCustom, calls=%fused_computation.3 | custom fusion | flops 2883584 | bytes 34603712 | tf_op jit(solution)/shard_map/scatter-add | solution.py:47
  192.5 0.6 copy.18
  193.1 2.8 fusion.2
  196.0 0.7 copy.20
  196.6 7.9 %gather_fusion.2 = bf16[176,128,128]{2,1,0:T(8,128)(2,1)} fusion(bf16[32,128,128]{2,1,0:T(8,128)(2,1)S(1)} %bitcast.46, s32[1024]{0:T(1024)S(1)} %pad_clamp_fusion), kind=kCustom, calls=%fused_computation.2 | custom fusion | bytes 11535040 | tf_op jit(solution)/shard_map/gather | solution.py:56
  204.5 11.3 %multiply_bitcast_fusion = f32[176,128,128]{1,2,0:T(8,128)} fusion(f32[176]{0:T(256)S(1)} %compare_convert_fusion, bf16[176,128,128]{2,1,0:T(8,128)(2,1)} %gather_fusion.2, bf16[176,128,128]{2,1,0:T(8,128)(2,1)} %param.11), kind=kOutput, calls=%fused_computation.6 | convolution fusion | flops 741081088 | bytes 23069376 | tf_op jit(solution)/shard_map/tji,tjk->tik/dot_general | solution.py:55
  215.7 12.0 %copy.22 = f32[176,128,128]{2,1,0:T(8,128)} copy(f32[176,128,128]{1,2,0:T(8,128)} %multiply_bitcast_fusion) | data formatting | bytes 23068672 | tf_op jit(solution)/shard_map/mul | solution.py:55
  227.7 3.4 broadcast_in_dim.9
  231.1 36.3 %scatter_fusion.1 = f32[96,128,128]{2,1,0:T(8,128)} fusion(f32[96,128,128]{2,1,0:T(8,128)} %broadcast_in_dim.9, s32[176]{0:T(256)S(1)} %bitcast.52, f32[176,128,128]{2,1,0:T(8,128)} %copy.22), kind=kCustom, calls=%fused_computation.4 | custom fusion | flops 2883584 | bytes 34603712 | tf_op jit(solution)/shard_map/scatter-add | solution.py:60
  267.4 4.6 slice.15
  272.1 5.9 all-to-all-start.1
  278.0 0.0 all-reduce.2.cloned.1.call-start
  278.1 1.7 slice.14
  279.8 94.4 %all-to-all-done.1 = f32[64,128,128]{2,1,0:T(8,128)} async-done(((f32[64,128,128]{2,1,0:T(8,128)}), f32[64,128,128]{2,1,0:T(8,128)}, u32[]{:S(2)}, u32[]{:S(2)}) %all-to-all-start.1) | async-done | bytes 4194336 | tf_op jit(solution)/shard_map/all_to_all | solution.py:61
  374.2 8.8 %scatter_fusion.2 = f32[32,128,128]{2,1,0:T(8,128)S(1)} fusion(f32[32,128,128]{2,1,0:T(8,128)S(1)} %slice.14, s32[64]{0:T(128)S(1)} %bitcast.55, f32[64,128,128]{2,1,0:T(8,128)} %all-to-all-done.1), kind=kCustom, calls=%fused_computation.5 | custom fusion | flops 1048576 | bytes 12583168 | tf_op jit(solution)/shard_map/scatter-add | solution.py:64
  383.0 0.2 convert_element_type.25
  383.2 3.6 convolution_bitcast_fusion
  386.9 0.0 all-reduce.2.cloned.1.call-update
  386.9 0.0 reduce-scatter.2.cloned.1.call-start
  386.9 4.5 fusion.4
  391.4 0.0 reduce-scatter.2.cloned.1.call-update
  391.4 1.2 copy-done.2
  392.6 1.3 copy.23
  393.9 163.3 %all-reduce.2.cloned.1.call-done = f32[512,128]{0,1:T(8,128)} async-done(((f32[512,128]{0,1:T(8,128)}), f32[512,128]{0,1:T(8,128)}) %all-reduce.2.cloned.1.call-update) | async-done | bytes 262160 | tf_op jit(solution)/shard_map/psum | solution.py:71
  557.3 1.8 copy.24
  559.1 80.9 %reduce-scatter.2.cloned.1.call-done = f32[4096,128]{1,0:T(8,128)} async-done(((f32[4096,512]{1,0:T(8,128)}), f32[4096,128]{1,0:T(8,128)}) %reduce-scatter.2.cloned.1.call-update) | async-done | bytes 2097168 | tf_op jit(solution)/shard_map/reduce_scatter | solution.py:73
  640.0 2.7 convert_element_type.27
  (16 shorter events, 0.1 us)
Async XLA Ops:
  7.2 59.4 %copy-start = (bf16[512,128]{1,0:T(8,128)(2,1)S(1)}, bf16[512,128]{1,0:T(8,128)(2,1)}, u32[]{:S(2)}) copy-start(bf16[512,128]{1,0:T(8,128)(2,1)} %param.10) | copy-start | bytes 393220
  7.2 59.4 %all-gather.2.cloned.1.call-start = ((), (), s32[]{:S(2)}) async-start(), calls=%async_computation.3 | async-start | bytes 5242880 | tf_op jit(solution)/shard_map/all_gather | solution.py:27
  70.0 15.3 %copy-start.1 = (bf16[4096,128]{1,0:T(8,128)(2,1)}, bf16[4096,128]{1,0:T(8,128)(2,1)S(1)}, u32[]{:S(2)}) copy-start(bf16[4096,128]{1,0:T(8,128)(2,1)S(1)} %convolution_convert_fusion) | copy-start | bytes 3145732
  70.1 13.8 %copy-start.3 = (bf16[4096,128]{1,0:T(8,128)(2,1)S(1)}, bf16[4096,128]{1,0:T(8,128)(2,1)}, u32[]{:S(2)}) copy-start(bf16[4096,128]{1,0:T(8,128)(2,1)} %param.17) | copy-start | bytes 3145732
  70.1 15.2 %copy-start.6 = (s32[1,176]{1,0:T(1,128)S(1)}, s32[1,176]{1,0:T(1,128)}, u32[]{:S(2)}) copy-start(s32[1,176]{1,0:T(1,128)} %param.13) | copy-start | bytes 2116
  70.1 15.2 %copy-start.5 = (s32[1,176]{1,0:T(1,128)S(1)}, s32[1,176]{1,0:T(1,128)}, u32[]{:S(2)}) copy-start(s32[1,176]{1,0:T(1,128)} %param.12) | copy-start | bytes 2116
  72.2 62.0 %all-to-all-start = ((bf16[64,128,128]{2,1,0:T(8,128)(2,1)}), bf16[64,128,128]{2,1,0:T(8,128)(2,1)}, u32[]{:S(2)}, u32[]{:S(2)}) async-start(bf16[64,128,128]{2,1,0:T(8,128)(2,1)} %gather_fusion), calls=%async_computation | async-start | bytes 4194304 | tf_op jit(solution)/shard_map/all_to_all | solution.py:37
  169.2 23.9 %copy-start.4 = (s32[4096,8]{0,1:T(8,128)S(1)}, s32[4096,8]{0,1:T(8,128)}, u32[]{:S(2)}) copy-start(s32[4096,8]{0,1:T(8,128)} %param.16) | copy-start | bytes 393220
  272.1 102.2 %copy-start.7 = (s32[1,64]{1,0:T(1,128)S(1)}, s32[1,64]{1,0:T(1,128)}, u32[]{:S(2)}) copy-start(s32[1,64]{1,0:T(1,128)} %param.15) | copy-start | bytes 772
  272.1 102.2 %all-to-all-start.1 = ((f32[64,128,128]{2,1,0:T(8,128)}), f32[64,128,128]{2,1,0:T(8,128)}, u32[]{:S(2)}, u32[]{:S(2)}) async-start(f32[64,128,128]{2,1,0:T(8,128)} %slice.15), calls=%async_computation.1 | async-start | bytes 8388608 | tf_op jit(solution)/shard_map/all_to_all | solution.py:61
  278.0 279.3 %all-reduce.2.cloned.1.call-start = ((), (), s32[]{:S(2)}) async-start(), calls=%async_computation.5 | async-start | bytes 524288 | tf_op jit(solution)/shard_map/psum | solution.py:71
  386.9 253.1 %reduce-scatter.2.cloned.1.call-start = ((), (), s32[]{:S(2)}) async-start(), calls=%async_computation.4 | async-start | bytes 10485760 | tf_op jit(solution)/shard_map/reduce_scatter | solution.py:73
  391.4 1.2 copy-start.2
Sparse Core Ops, SparseCore 0:
  9.8 56.7 all-gather.1
  387.0 170.2 all-reduce.1
  560.1 79.8 reduce-scatter.1
where the time goes:
time: 654 us; the launch traced here: 649 us
  waiting for transfers between devices  446 us (68%)
  other arithmetic  76.8 us (12%)
  local copies, waits for them, and re-layouts  58.7 us (9%)
  matrix products  35.7 us (5%)
  starting transfers between devices  17 us (3%)
  between operations  14.6 us (2%)
    psum x1, waiting for transfers between devices, per_device(): weight_grad = lax.psum(weight_terms, 'dom')  163 us
    all_to_all x1, waiting for transfers between devices, per_device(): lax.all_to_all(slot_sums[row_blocks:], 'dom', split_axis=0, concat_axis=0...  94.4 us
    reduce_scatter x1, waiting for transfers between devices, per_device(): lax.psum_scatter(partial_terms, 'hid', scatter_dimension=1, tiled=True)  80.9 us
    all_gather x1, waiting for transfers between devices, per_device(): feature_all = lax.all_gather(node_features, 'hid', axis=1, tiled=True)  58 us
    all_to_all x1, waiting for transfers between devices, per_device(): lax.all_to_all(hidden_blocks[outgoing], 'dom', split_axis=0, concat_axis=...  48.9 us
    scatter-add x1, other arithmetic, per_device(): jax.ops.segment_sum(back_terms, tile_col, num_segments=row_blocks + parti...  36.3 us
    scatter-add x1, other arithmetic, per_device(): jax.ops.segment_sum(products, tile_row, num_segments=row_blocks)  23.3 us
  transfers between devices with their start and end apart: 5, of which 5 were waited for; matrix products, arithmetic and copies ran while one was open for 2% of the time, Pallas kernels for 0%

commit v1 on v0

v1 whole, which is shorter than its diff:
```python
import functools

import jax
import jax.numpy as jnp
from jax import lax
from jax.experimental import pallas as pl
from jax.experimental.pallas import tpu as pltpu
from jax.sharding import PartitionSpec as P

B = 128
RB = 32
HID = 4
CHUNK = RB // HID
F32 = jnp.float32
BF16 = jnp.bfloat16
LIMIT = 60 * 1024 * 1024

VMEM = pl.BlockSpec(memory_space=pltpu.VMEM)
SMEM = pl.BlockSpec(memory_space=pltpu.SMEM)
ANY = pl.BlockSpec(memory_space=pl.ANY)
HBM = pl.BlockSpec(memory_space=pltpu.HBM)


def params():
    return pltpu.CompilerParams(vmem_limit_bytes=LIMIT)


def cost(flops, nbytes):
    return pl.CostEstimate(flops=flops, bytes_accessed=nbytes, transcendentals=0)


def dot(a, b, dims=((1,), (0,))):
    return lax.dot_general(a, b, (dims, ((), ())), preferred_element_type=F32)


def rel(me, shift):
    return lax.rem(me + shift + HID, HID)


def bit_mask(words):
    halves = jnp.concatenate([words & 255, words >> 8], 0).astype(F32).astype(BF16)
    row = lax.broadcasted_iota(jnp.int32, (16, B), 0)
    unit = lax.broadcasted_iota(jnp.int32, (16, B), 1)
    byte_row = (unit // 16) + 8 * ((unit % 16) // 8)
    scale = lax.div(jnp.ones((16, B), F32), (1 << (unit % 8)).astype(F32))
    spread = jnp.where(row == byte_row, scale, 0.0).astype(BF16)
    shifted = dot(halves, spread, ((0,), (0,)))
    return (shifted.astype(jnp.int32) & 1) == 1


STEP = 256
TILES = 176
PIECES = 4
PIECE = TILES // PIECES
INNER = PIECE // 4


def tile_copies(tiles_hbm, tiles, sems):
    return [
        pltpu.make_async_copy(
            tiles_hbm.at[pl.ds(k * PIECE, PIECE)], tiles.at[pl.ds(k * PIECE, PIECE)], sems.at[k]
        )
        for k in range(PIECES)
    ]


def tiles_bwd_kernel(count_ref, rows_ref, cols_ref, bits_hbm, cot_hbm, tiles_hbm, own_hbm,
                     slot_hbm, tiles, bits, cot, d_t, acc, slots, sems, out_sems):
    count = count_ref[0]
    bits_in = pltpu.make_async_copy(bits_hbm, bits, sems.at[PIECES])
    cot_in = pltpu.make_async_copy(cot_hbm, cot, sems.at[PIECES + 1])
    bits_in.start()
    cot_in.start()
    copies = tile_copies(tiles_hbm, tiles, sems)
    for c in copies:
        c.start()
    acc[...] = jnp.zeros_like(acc)
    bits_in.wait()
    cot_in.wait()

    def mask(i, carry):
        at = pl.multiple_of(i * STEP, STEP)
        active = bit_mask(bits[:, pl.ds(at, STEP)])
        v = jnp.where(active, cot[pl.ds(at, STEP), :].astype(F32), 0.0)
        for j in range(STEP // B):
            d_t[i * (STEP // B) + j] = v[j * B : (j + 1) * B].T.astype(BF16)
        return carry

    lax.fori_loop(0, 4096 // STEP, mask, 0)
    for k in range(PIECES):
        copies[k].wait()

        def body(i, carry, k=k):
            for j in range(INNER):
                t = k * PIECE + i * INNER + j
                s = jnp.where(t < count, cols_ref[0, t], RB + 64)
                acc[s] += dot(d_t[rows_ref[0, t]], tiles[t])
            return carry

        lax.fori_loop(0, 4, body, 0)
    outs = []
    for k in range(4):
        at = pl.ds(k * 16, 16)
        slots[at] = acc[RB + k * 16 : RB + (k + 1) * 16].astype(BF16)
        outs.append(pltpu.make_async_copy(slots.at[at], slot_hbm.at[at], out_sems.at[k]))
        outs[-1].start()
    outs.append(pltpu.make_async_copy(acc.at[pl.ds(0, RB)], own_hbm, out_sems.at[4]))
    outs[-1].start()
    for c in outs:
        c.wait()


def tiles_bwd_call(count, rows, cols, bits_t, cot, tiles):
    return pl.pallas_call(
        tiles_bwd_kernel,
        out_shape=[
            jax.ShapeDtypeStruct((RB, B, B), F32),
            jax.ShapeDtypeStruct((64, B, B), BF16),
        ],
        in_specs=[SMEM] * 3 + [ANY] * 3,
        out_specs=[HBM] * 2,
        scratch_shapes=[
            pltpu.VMEM((TILES, B, B), BF16),
            pltpu.VMEM((8, 4096), jnp.int32),
            pltpu.VMEM((4096, B), BF16),
            pltpu.VMEM((RB, B, B), BF16),
            pltpu.VMEM((RB + 65, B, B), F32),
            pltpu.VMEM((64, B, B), BF16),
            pltpu.SemaphoreType.DMA((PIECES + 2,)),
            pltpu.SemaphoreType.DMA((5,)),
        ],
        compiler_params=params(),
        cost_estimate=cost(2 * TILES * B * B * B, 30 << 20),
        name="tiles_bwd",
    )(count, rows, cols, bits_t, cot, tiles)


def tiles_fwd_kernel(count_ref, rows_ref, cols_ref, bits_ref, own_hbm, recv_hbm, tiles_hbm,
                     after, out_ref, tiles, src, acc, sems):
    count = count_ref[0]
    own = pltpu.make_async_copy(own_hbm, src.at[pl.ds(0, RB)], sems.at[PIECES])
    got = pltpu.make_async_copy(recv_hbm, src.at[pl.ds(RB, 64)], sems.at[PIECES + 1])
    own.start()
    got.start()
    copies = tile_copies(tiles_hbm, tiles, sems)
    for c in copies:
        c.start()
    acc[...] = jnp.zeros_like(acc)
    own.wait()
    got.wait()
    for k in range(PIECES):
        copies[k].wait()

        def body(i, carry, k=k):
            for j in range(INNER):
                t = k * PIECE + i * INNER + j
                r = jnp.where(t < count, rows_ref[0, t], RB)
                acc[r] += dot(tiles[t], src[cols_ref[0, t]])
            return carry

        lax.fori_loop(0, 4, body, 0)

    def mask(i, carry):
        at = pl.multiple_of(i * STEP, STEP)
        active = bit_mask(bits_ref[:, pl.ds(at, STEP)])
        for j in range(STEP // B):
            b = i * (STEP // B) + j
            out_ref[b] = jnp.where(active[j * B : (j + 1) * B], acc[b], 0.0).astype(BF16)
        return carry

    lax.fori_loop(0, 4096 // STEP, mask, 0)


def tiles_fwd_call(count, rows, cols, bits_t, own, recv, tiles, after):
    return pl.pallas_call(
        tiles_fwd_kernel,
        out_shape=jax.ShapeDtypeStruct((RB, B, B), BF16),
        in_specs=[SMEM] * 3 + [VMEM] + [ANY] * 4,
        out_specs=VMEM,
        scratch_shapes=[
            pltpu.VMEM((TILES, B, B), BF16),
            pltpu.VMEM((RB + 64, B, B), BF16),
            pltpu.VMEM((RB + 1, B, B), F32),
            pltpu.SemaphoreType.DMA((PIECES + 2,)),
        ],
        compiler_params=params(),
        cost_estimate=cost(2 * TILES * B * B * B, 30 << 20),
        name="tiles_fwd",
    )(count, rows, cols, bits_t, own, recv, tiles, after)


def hidden_kernel(me_ref, send_ref, x0, x1, x2a, x2b, x3, w_ref, w1, w2, w3, hid_hbm, out_hbm, hid, sems):
    me = me_ref[0]
    rhs = jnp.concatenate(
        [w_ref[pl.ds(pl.multiple_of(rel(me, -s) * B, B), B), :] for s in range(HID)], 0
    )
    for n in range(4096 // STEP):
        half, at = (x2a, n * STEP) if n < 2048 // STEP else (x2b, n * STEP - 2048)
        here = slice(n * STEP, (n + 1) * STEP)
        lhs = jnp.concatenate([x0[here, :], x1[here, :], half[at : at + STEP, :], x3[here, :]], 1)
        r = dot(lhs, rhs).astype(BF16)
        for j in range(STEP // B):
            hid[n * (STEP // B) + j] = r[j * B : (j + 1) * B]
    copies = [
        pltpu.make_async_copy(hid.at[send_ref[0, q]], out_hbm.at[q], sems.at[q]) for q in range(64)
    ]
    copies.append(pltpu.make_async_copy(hid, hid_hbm, sems.at[64]))
    for c in copies:
        c.start()
    for c in copies:
        c.wait()


def hidden_call(me, send, xs, w, ws):
    return pl.pallas_call(
        hidden_kernel,
        out_shape=[
            jax.ShapeDtypeStruct((RB, B, B), BF16),
            jax.ShapeDtypeStruct((64, B, B), BF16),
        ],
        in_specs=[SMEM] * 2 + [VMEM] * 6 + [ANY] * 3,
        out_specs=[HBM] * 2,
        scratch_shapes=[pltpu.VMEM((RB, B, B), BF16), pltpu.SemaphoreType.DMA((65,))],
        compiler_params=params(),
        cost_estimate=cost(2 * 4096 * 512 * 128, 10 << 20),
        name="hidden",
    )(me, send, *xs, w, *ws[1:])


def sum_kernel(me_ref, send_ref, own_hbm, got_hbm, x0, x1, x2a, x2b, x3, after, terms_hbm, d_hbm,
               acc, got, xv, flat, dv, terms, sems, out_sems):
    me, y = me_ref[0], me_ref[1]
    ins = [
        pltpu.make_async_copy(own_hbm, acc, sems.at[0]),
        pltpu.make_async_copy(got_hbm, got, sems.at[1]),
        pltpu.make_async_copy(x0, xv.at[0], sems.at[2]),
        pltpu.make_async_copy(x1, xv.at[1], sems.at[3]),
        pltpu.make_async_copy(x2a, xv.at[2, pl.ds(0, 2048)], sems.at[4]),
        pltpu.make_async_copy(x2b, xv.at[2, pl.ds(2048, 2048)], sems.at[5]),
        pltpu.make_async_copy(x3, xv.at[3], sems.at[6]),
    ]
    for i in ins:
        i.start()
    ins[0].wait()
    ins[1].wait()

    def body(i, carry):
        for j in range(8):
            q = i * 8 + j
            acc[send_ref[0, q]] += got[q].astype(F32)
        return carry

    lax.fori_loop(0, 8, body, 0)
    outs = []

    def flip(i, carry):
        for j in range(4):
            dv[i * 4 + j] = acc[i * 4 + j].T.astype(BF16)
        return carry

    for k in range(4):
        at = pl.ds(k * CHUNK, CHUNK)
        lax.fori_loop(2 * k, 2 * k + 2, flip, 0)
        outs.append(pltpu.make_async_copy(dv.at[at], d_hbm.at[at], out_sems.at[k]))
        outs[-1].start()
    for b in range(RB):
        flat[:, b * B : (b + 1) * B] = acc[b].astype(BF16)
    for i in ins[2:]:
        i.wait()
    for s in range(HID):
        r = dot(flat[...], xv[s]).T
        terms[pl.ds(pl.multiple_of(rel(me, -s) * B, B), B), :] = r
    for k in range(4):
        at = pl.multiple_of(lax.rem(y + k, 4) * B, B)
        outs.append(
            pltpu.make_async_copy(
                terms.at[pl.ds(at, B)], terms_hbm.at[pl.ds(k * B, B)], out_sems.at[4 + k]
            )
        )
        outs[-1].start()
    for o in outs:
        o.wait()


def sum_call(me, send, own, got, xs, after):
    return pl.pallas_call(
        sum_kernel,
        out_shape=[jax.ShapeDtypeStruct((512, B), F32)]
        + [jax.ShapeDtypeStruct((RB, B, B), BF16)],
        in_specs=[SMEM] * 2 + [ANY] * 8,
        out_specs=[HBM] * 2,
        scratch_shapes=[
            pltpu.VMEM((RB, B, B), F32),
            pltpu.VMEM((64, B, B), BF16),
            pltpu.VMEM((HID, 4096, B), BF16),
            pltpu.VMEM((B, 4096), BF16),
            pltpu.VMEM((RB, B, B), BF16),
            pltpu.VMEM((512, B), F32),
            pltpu.SemaphoreType.DMA((7,)),
            pltpu.SemaphoreType.DMA((8,)),
        ],
        compiler_params=params(),
        cost_estimate=cost(2 * 4096 * 512 * 128, 12 << 20),
        name="sum_returned",
    )(me, send, own, got, *xs, after)


def add_kernel(a, b, c, d, out):
    out[...] = ((a[...] + b[...]) + (c[...] + d[...])).astype(BF16)


def add_call(parts):
    return pl.pallas_call(
        add_kernel,
        out_shape=jax.ShapeDtypeStruct((B, B), BF16),
        in_specs=[VMEM] * 4,
        out_specs=VMEM,
        compiler_params=params(),
        cost_estimate=cost(4 * B * B, 1 << 18),
        name="add_y",
    )(*parts)


def add_z_kernel(me_ref, *refs):
    parts, out, by_z = refs[:8], refs[8], refs[9]
    z = me_ref[2]
    for k in range(8):
        by_z[lax.rem(z + 8 - k, 8)] = parts[k][...].astype(F32)
    total = by_z[0]
    for k in range(1, 8):
        total = total + by_z[k]
    out[...] = total


def add_z_call(me, parts):
    return pl.pallas_call(
        add_z_kernel,
        out_shape=jax.ShapeDtypeStruct((B, B), F32),
        in_specs=[SMEM] + [VMEM] * 8,
        out_specs=VMEM,
        scratch_shapes=[pltpu.VMEM((8, B, B), F32)],
        compiler_params=params(),
        cost_estimate=cost(8 * B * B, 1 << 19),
        name="add_z",
    )(me, *parts)


def round_y_kernel(me_ref, t0, t1, t2, t3, after, out):
    for k, t in enumerate((t0, t1, t2, t3)):
        out[pl.ds(pl.multiple_of(rel(me_ref[1], -k) * B, B), B), :] = t[...]


def round_y_call(me, parts, after):
    return pl.pallas_call(
        round_y_kernel,
        out_shape=jax.ShapeDtypeStruct((512, B), F32),
        in_specs=[SMEM] + [VMEM] * 4 + [ANY],
        out_specs=VMEM,
        compiler_params=params(),
        cost_estimate=cost(512 * B, 1 << 19),
        name="round_y",
    )(me, *parts, after)


def back_kernel(d0, d1, d2a, d2b, d3, w0, w1, w2, w3, after, out_hbm, d, out, sems, out_sems):
    parts = [pl.ds(k * 1024, 1024) for k in range(4)]
    ins = []
    for k, p in enumerate(parts):
        half = pl.ds((k % 2) * 1024, 1024)
        for s, v in enumerate((d0.at[p], d1.at[p], (d2a, d2b)[k // 2].at[half], d3.at[p])):
            ins.append(pltpu.make_async_copy(v, d.at[s, p], sems.at[len(ins)]))
    outs = [
        pltpu.make_async_copy(out.at[p], out_hbm.at[p], out_sems.at[k])
        for k, p in enumerate(parts)
    ]
    for c in ins:
        c.start()
    rhs = jnp.concatenate([w0[...], w1[...], w2[...], w3[...]], 1)
    for k in range(4):
        for c in ins[4 * k : 4 * k + 4]:
            c.wait()
        for n in range(1024 // STEP):
            at = slice(k * 1024 + n * STEP, k * 1024 + (n + 1) * STEP)
            lhs = jnp.concatenate([d[s, at, :] for s in range(HID)], 1)
            out[at, :] = dot(lhs, rhs, ((1,), (1,))).astype(BF16)
        outs[k].start()
    for c in outs:
        c.wait()


def back_call(ds, ws, after):
    return pl.pallas_call(
        back_kernel,
        out_shape=jax.ShapeDtypeStruct((4096, B), BF16),
        in_specs=[ANY] * 5 + [VMEM] * HID + [ANY],
        out_specs=HBM,
        scratch_shapes=[
            pltpu.VMEM((HID, 4096, B), BF16),
            pltpu.VMEM((4096, B), BF16),
            pltpu.SemaphoreType.DMA((16,)),
            pltpu.SemaphoreType.DMA((4,)),
        ],
        compiler_params=params(),
        cost_estimate=cost(2 * 4096 * 512 * 128, 5 << 20),
        name="d_times_wt",
    )(*ds, *ws, after)


def shift_hid(v, s):
    return lax.ppermute(v, "hid", [(i, (i + s) % HID) for i in range(HID)])


def split_kernel(v1, v3, after, low, high):
    low[...] = v1[...]
    high[...] = v3[...]


def split_call(v1, v3, after):
    half = jax.ShapeDtypeStruct((2048, B), BF16)
    return pl.pallas_call(
        split_kernel,
        out_shape=[half] * 2,
        grid=(1,),
        in_specs=[
            pl.BlockSpec((2048, B), lambda i: (0, 0)),
            pl.BlockSpec((2048, B), lambda i: (1, 0)),
            ANY,
        ],
        out_specs=[pl.BlockSpec((2048, B), lambda i: (0, 0))] * 2,
        compiler_params=params(),
        cost_estimate=cost(1000, 2 << 20),
        name="halves",
    )(v1, v3, after)


def gather_hid(v, after):
    v1, v3 = shift_hid(v, 1), shift_hid(v, 3)
    low, high = split_call(v1, v3, after)
    return v, v1, shift_hid(low, 1), shift_hid(high, 3), v3


def shift_dom(v, dz, dy, dc):
    pairs = [
        ((z * 4 + y) * 2 + c, (((z + dz) % 8) * 4 + (y + dy) % 4) * 2 + (c ^ dc))
        for z in range(8)
        for y in range(4)
        for c in range(2)
    ]
    return lax.ppermute(v, "dom", pairs)


def all_to_all(v):
    return lax.all_to_all(v, "dom", split_axis=0, concat_axis=0, tiled=True)


def per_device(x, w, tiles, rows, cols, count, send, bits, cot):
    hid = lax.axis_index("hid").astype(jnp.int32)
    dom = lax.axis_index("dom").astype(jnp.int32)
    z, y = dom // 8, (dom // 2) % 4
    me = jnp.stack([hid, y, z])
    bits_t = bits.T

    own, slots = tiles_bwd_call(count, rows, cols, bits_t, cot, tiles)
    returned = all_to_all(slots)

    xs = gather_hid(x, slots)
    ws = [lax.dynamic_slice_in_dim(w, ((hid + s) % HID) * B, B) for s in range(HID)]
    ws = [ws[0]] + [shift_hid(ws[s], s) for s in range(1, HID)]
    hidden, outgoing = hidden_call(me, send, xs, w, ws)
    incoming = all_to_all(outgoing)

    terms, d = sum_call(me, send, own, returned, xs, outgoing)
    terms = (terms + shift_dom(terms, 0, 0, 1)).reshape(4, B, B)
    terms = [terms[0]] + [shift_dom(terms[k], 0, k, 0) for k in (1, 3, 2)]
    part = add_call(terms)
    ds = gather_hid(d.reshape(4096, B), part)
    total = add_z_call(me, [part] + [shift_dom(part, k, 0, 0) for k in range(1, 8)])
    out_act = tiles_fwd_call(count, rows, cols, bits_t, hidden, incoming, tiles, total)
    input_grad = back_call(ds, ws, out_act)
    total = [total] + [shift_dom(total, 0, k, 0) for k in range(1, 4)]
    weight_grad = round_y_call(me, total, out_act)
    return out_act.reshape(4096, B), input_grad, weight_grad


def solution(mesh):
    placed = (
        P("dom", "hid"),
        P(None, "hid"),
        P("dom", None, None),
        P("dom", None),
        P("dom", None),
        P("dom"),
        P("dom", None),
        P("dom", "hid"),
        P("dom", "hid"),
    )
    return jax.shard_map(
        per_device,
        mesh=mesh,
        in_specs=placed,
        out_specs=(P("dom", "hid"), P("dom", "hid"), P(None, "hid")),
        check_vma=False,
    )
```

time: 654 us -> 185 us (0.28)
  waiting for transfers between devices: 446 us -> 56.6 us
  other arithmetic: 76.8 us -> 1.6 us
  Pallas kernels: 0 us -> 51.3 us
  local copies, waits for them, and re-layouts: 58.7 us -> 10.7 us
  starting transfers between devices: 17 us -> 61.7 us
  matrix products: 35.7 us -> 0 us
  between operations: 14.6 us -> 1.71 us
    psum x1 -> x0, waiting for transfers between devices: 163 us -> none  [per_device(): weight_grad = lax.psum(weight_terms, 'dom')]
    all_to_all x2, waiting for transfers between devices: 143 us -> 0.01 us  [all_to_all(): return lax.all_to_all(v, 'dom', split_axis=0, concat_axis=0, tiled=True)]
    reduce_scatter x1 -> x0, waiting for transfers between devices: 80.9 us -> none  [per_device(): lax.psum_scatter(partial_terms, 'hid', scatter_dimension=1, tiled=True)]
    scatter-add x3 -> x0, other arithmetic: 68.3 us -> none  [the longest x1 36.3 us: per_device(): jax.ops.segment_sum(back_terms, tile_col, num_segments=row_blocks + parti...]
    all_gather x1 -> x0, waiting for transfers between devices: 58 us -> none  [per_device(): feature_all = lax.all_gather(node_features, 'hid', axis=1, tiled=True)]
    ppermute x0 -> x25, waiting for transfers between devices: none -> 56.6 us  [the longest x11 39.2 us: shift_hid(): return lax.ppermute(v, 'hid', [(i, (i + s) % HID) for i in range(HID)])]
    pallas_call x0 -> x10, Pallas kernels: none -> 51.3 us  [the longest x1 13.2 us: tiles_bwd_call(): pl.pallas_call(tiles_bwd_kernel, out_shape=[jax.ShapeDtypeStruct((RB, B,...]
    ppermute x0 -> x25, starting transfers between devices: none -> 38.5 us  [the longest x14 23.1 us: shift_dom(): return lax.ppermute(v, 'dom', pairs)]
  transfers between devices with their start and end apart: 5 -> 27, of which waited for: 5 -> 11; matrix products, arithmetic and copies ran while one was open for 2% -> 2% of each run, Pallas kernels for 0% -> 18%
where the time goes in v1:
time: 185 us; the launch traced here: 184 us
  starting transfers between devices  61.7 us (33%)
  waiting for transfers between devices  56.6 us (31%)
  Pallas kernels  51.3 us (28%)
  local copies, waits for them, and re-layouts  10.7 us (6%)
    ppermute x11, waiting for transfers between devices, shift_hid(): return lax.ppermute(v, 'hid', [(i, (i + s) % HID) for i in range(HID)])  39.2 us
    all_to_all x2, starting transfers between devices, all_to_all(): return lax.all_to_all(v, 'dom', split_axis=0, concat_axis=0, tiled=True)  23.3 us
    ppermute x14, starting transfers between devices, shift_dom(): return lax.ppermute(v, 'dom', pairs)  23.1 us
    ppermute x14, waiting for transfers between devices, shift_dom(): return lax.ppermute(v, 'dom', pairs)  17.4 us
    ppermute x11, starting transfers between devices, shift_hid(): return lax.ppermute(v, 'hid', [(i, (i + s) % HID) for i in range(HID)])  15.4 us
    pallas_call x1, Pallas kernels, tiles_bwd_call(): pl.pallas_call(tiles_bwd_kernel, out_shape=[jax.ShapeDtypeStruct((RB, B,...  13.2 us
    pallas_call x1, Pallas kernels, tiles_fwd_call(): pl.pallas_call(tiles_fwd_kernel, out_shape=jax.ShapeDtypeStruct((RB, B, B...  11.9 us
    unnamed x54, local copies, waits for them, and re-layouts  9.45 us
  transfers between devices with their start and end apart: 27, of which 11 were waited for; matrix products, arithmetic and copies ran while one was open for 2% of the time, Pallas kernels for 18%

profile of v1, /device:TPU:6, one launch (start us, length us, event | category | flops | bytes accessed | tf_op | source)
XLA Modules:
  0.0 183.6 jit_solution(18108168476373638604)
XLA Ops:
  1.3 13.2 %tiles_bwd.1 = (f32[32,128,128]{2,1,0:T(8,128)}, bf16[64,128,128]{2,1,0:T(8,128)(2,1)}) custom-call(s32[1]{0:T(128)S(6)} %copy.12.count_ref, s32[1,176]{1,0:T(1,128)} %rows_ref.3, s32[1,176]{1,0:T(1,128)} %cols_ref.3, s32[8,4096]{1,0:T(8,128)} %bitcast.10, bf16[4096,128]{1,0:T(8,128)(2,1)} %cot_hbm.1, bf16[176,128,128]{2,1,0:T(8,128)(2,1)} %tiles_hbm.3), custom_call_target="tpu_custom_call" | custom-call | flops 738197504 | bytes 31457280 | tf_op jit(solution)/shard_map/tiles_bwd/pallas_call | solution.py:114
  14.5 12.5 %all-to-all-start.1 = ((bf16[64,128,128]{2,1,0:T(8,128)(2,1)}), bf16[64,128,128]{2,1,0:T(8,128)(2,1)}, u32[]{:S(2)}, u32[]{:S(2)}) async-start(bf16[64,128,128]{2,1,0:T(8,128)(2,1)} %get-tuple-element.13.after), calls=%async_computation.1 | async-start | bytes 4194304 | tf_op jit(solution)/shard_map/all_to_all | solution.py:453
  27.0 0.9 collective-permute-start.1
  27.9 2.4 %collective-permute-start = (bf16[4096,128]{1,0:T(8,128)(2,1)S(1)}, bf16[4096,128]{1,0:T(8,128)(2,1)S(1)}, u32[]{:S(2)}, u32[]{:S(2)}) collective-permute-start(bf16[4096,128]{1,0:T(8,128)(2,1)S(1)} %copy-done.4), channel_id=1, source_target_pairs={{0,1},{1,2},{2,3},{3,0},{4,5},{5,6},{6,7},{7,4},{8,9},{9,10},{10,1... | collective-permute-start | bytes 3145736 | tf_op jit(solution)/shard_map/ppermute | solution.py:410
  30.3 23.0 %collective-permute-done.1.v3.x3 = bf16[4096,128]{1,0:T(8,128)(2,1)S(1)} collective-permute-done((bf16[4096,128]{1,0:T(8,128)(2,1)S(1)}, bf16[4096,128]{1,0:T(8,128)(2,1)S(1)}, u32[]{:S(2)}, u32[]{:S(2)}) %collective-permute-start.1) | collective-permute-done | bytes 1048608 | tf_op jit(solution)/shard_map/ppermute | solution.py:410
  53.4 1.0 copy-done
  54.3 1.0 copy-done.1
  55.3 2.2 %halves.2 = (bf16[2048,128]{1,0:T(8,128)(2,1)}, bf16[2048,128]{1,0:T(8,128)(2,1)}) custom-call(bf16[4096,128]{1,0:T(8,128)(2,1)} %copy-done.1, bf16[4096,128]{1,0:T(8,128)(2,1)} %copy-done, bf16[64,128,128]{2,1,0:T(8,128)(2,1)} %get-tuple-element.13.after), custom_call_target="tpu_custom_call" | custom-call | flops 1000 | bytes 2097152 | tf_op jit(solution)/shard_map/halves/pallas_call | solution.py:420
  57.5 2.0 %collective-permute-start.2 = (bf16[2048,128]{1,0:T(8,128)(2,1)}, bf16[2048,128]{1,0:T(8,128)(2,1)S(1)}, u32[]{:S(2)}, u32[]{:S(2)}) collective-permute-start(bf16[2048,128]{1,0:T(8,128)(2,1)} %get-tuple-element.14), channel_id=1, source_target_pairs={{0,1},{1,2},{2,3},{3,0},{4,5},{5,6},{6,7},{7,4},{8,9},{9,10},{10,1... | collective-permute-start | bytes 1572872 | tf_op jit(solution)/shard_map/ppermute | solution.py:410
  60.2 4.7 %collective-permute-start.5 = (bf16[128,128]{1,0:T(8,128)(2,1)S(1)}, bf16[128,128]{1,0:T(8,128)(2,1)S(1)}, u32[]{:S(2)}, u32[]{:S(2)}) collective-permute-start(bf16[128,128]{1,0:T(8,128)(2,1)S(1)} %get-tuple-element.29), channel_id=1, source_target_pairs={{0,2},{1,3},{2,0},{3,1},{4,6},{5,7},{6,4},{7,5},{8,10},{9,11},{10,... | collective-permute-start | bytes 98312 | tf_op jit(solution)/shard_map/ppermute | solution.py:410
  65.5 9.3 %collective-permute-done.6.w3 = bf16[128,128]{1,0:T(8,128)(2,1)S(1)} collective-permute-done((bf16[128,128]{1,0:T(8,128)(2,1)S(1)}, bf16[128,128]{1,0:T(8,128)(2,1)S(1)}, u32[]{:S(2)}, u32[]{:S(2)}) %collective-permute-start.6) | collective-permute-done | bytes 32800 | tf_op jit(solution)/shard_map/ppermute | solution.py:410
  75.7 0.8 copy-done.6
  76.5 5.7 %hidden.1 = (bf16[32,128,128]{2,1,0:T(8,128)(2,1)}, bf16[64,128,128]{2,1,0:T(8,128)(2,1)}) custom-call(s32[3]{0:T(128)} %pad_add_fusion.me_ref, s32[1,64]{1,0:T(1,128)} %send_ref.3, bf16[4096,128]{1,0:T(8,128)(2,1)} %x0.3, bf16[4096,128]{1,0:T(8,128)(2,1)} %copy-done.1, bf16[2048,128]{1,0:T(8,128)(2,1)} %copy-done.5, bf16[2048,128]{1,0:T(8,128)(2,1)} %copy-done.6, ...), custom_call_target="tpu_custom_call" | custom-call | flops 536870912 | bytes 10485760 | tf_op jit(solution)/shard_map/hidden/pallas_call | solution.py:215
  82.2 10.8 %all-to-all-start = ((bf16[64,128,128]{2,1,0:T(8,128)(2,1)}), bf16[64,128,128]{2,1,0:T(8,128)(2,1)S(1)}, u32[]{:S(2)}, u32[]{:S(2)}) async-start(bf16[64,128,128]{2,1,0:T(8,128)(2,1)} %get-tuple-element.17.after), calls=%async_computation | async-start | bytes 4194304 | tf_op jit(solution)/shard_map/all_to_all | solution.py:453
  93.0 6.5 %sum_returned.1 = (f32[512,128]{1,0:T(8,128)}, bf16[32,128,128]{2,1,0:T(8,128)(2,1)}) custom-call(s32[3]{0:T(128)} %pad_add_fusion.me_ref, s32[1,64]{1,0:T(1,128)} %send_ref.3, f32[32,128,128]{2,1,0:T(8,128)} %get-tuple-element.18.own_hbm, bf16[64,128,128]{2,1,0:T(8,128)(2,1)} %all-to-all-done.1.got_hbm, bf16[4096,128]{1,0:T(8,128)(2,1)} %x0.3, ...), custom_call_target="tpu_custom_call" | custom-call | flops 536870912 | bytes 12582912 | tf_op jit(solution)/shard_map/sum_returned/pallas_call | solution.py:286
  99.6 3.2 %collective-permute-start.18 = (bf16[4096,128]{1,0:T(8,128)(2,1)}, bf16[4096,128]{1,0:T(8,128)(2,1)}, u32[]{:S(2)}, u32[]{:S(2)}) collective-permute-start(bf16[4096,128]{1,0:T(8,128)(2,1)} %bitcast.8), channel_id=1, source_target_pairs={{0,1},{1,2},{2,3},{3,0},{4,5},{5,6},{6,7},{7,4},{8,9},{9,10},{10,1... | collective-permute-start | bytes 3145736 | tf_op jit(solution)/shard_map/ppermute | solution.py:410
  102.8 1.7 collective-permute-done.7
  104.6 1.0 add.52
  105.5 0.6 fusion
  106.2 2.9 %collective-permute-start.10 = (f32[128,128]{1,0:T(8,128)S(1)}, f32[128,128]{1,0:T(8,128)S(1)}, u32[]{:S(2)}, u32[]{:S(2)}) collective-permute-start(f32[128,128]{1,0:T(8,128)S(1)} %get-tuple-element.23), channel_id=1, source_target_pairs={{0,16},{4,20},{8,24},{12,28},{16,0},{20,4},{24,8},{28,12},{32,48},... | collective-permute-start | bytes 196616 | tf_op jit(solution)/shard_map/ppermute | solution.py:449
  109.1 1.2 collective-permute-start.9
  110.3 0.9 collective-permute-start.8
  111.1 2.7 %collective-permute-done.10.d = f32[128,128]{1,0:T(8,128)S(1)} collective-permute-done((f32[128,128]{1,0:T(8,128)S(1)}, f32[128,128]{1,0:T(8,128)S(1)}, u32[]{:S(2)}, u32[]{:S(2)}) %collective-permute-start.10) | collective-permute-done | bytes 65568 | tf_op jit(solution)/shard_map/ppermute | solution.py:449
  113.8 1.6 collective-permute-done.9.c
  115.4 1.5 collective-permute-done.8.b
  117.6 1.6 add_y.1.refs_0_.after
  119.1 6.8 %collective-permute-done.19.v3.d3 = bf16[4096,128]{1,0:T(8,128)(2,1)S(1)} collective-permute-done((bf16[4096,128]{1,0:T(8,128)(2,1)}, bf16[4096,128]{1,0:T(8,128)(2,1)S(1)}, u32[]{:S(2)}, u32[]{:S(2)}) %collective-permute-start.19) | collective-permute-done | bytes 1048608 | tf_op jit(solution)/shard_map/ppermute | solution.py:410
  125.9 1.0 copy-done.3
  126.9 2.3 %halves.3 = (bf16[2048,128]{1,0:T(8,128)(2,1)}, bf16[2048,128]{1,0:T(8,128)(2,1)}) custom-call(bf16[4096,128]{1,0:T(8,128)(2,1)} %collective-permute-done.18.v1.d1, bf16[4096,128]{1,0:T(8,128)(2,1)} %copy-done.3, bf16[128,128]{1,0:T(8,128)(2,1)} %add_y.1.refs_0_.after), custom_call_target="tpu_custom_call" | custom-call | flops 1000 | bytes 2097152 | tf_op jit(solution)/shard_map/halves/pallas_call | solution.py:420
  129.2 2.1 %collective-permute-start.20 = (bf16[2048,128]{1,0:T(8,128)(2,1)}, bf16[2048,128]{1,0:T(8,128)(2,1)S(1)}, u32[]{:S(2)}, u32[]{:S(2)}) collective-permute-start(bf16[2048,128]{1,0:T(8,128)(2,1)} %get-tuple-element.21), channel_id=1, source_target_pairs={{0,1},{1,2},{2,3},{3,0},{4,5},{5,6},{6,7},{7,4},{8,9},{9,10},{10,1... | collective-permute-start | bytes 1572872 | tf_op jit(solution)/shard_map/ppermute | solution.py:410
  131.3 3.1 %collective-permute-start.17 = (bf16[128,128]{1,0:T(8,128)(2,1)S(1)}, bf16[128,128]{1,0:T(8,128)(2,1)S(1)}, u32[]{:S(2)}, u32[]{:S(2)}) collective-permute-start(bf16[128,128]{1,0:T(8,128)(2,1)S(1)} %copy-done.10), channel_id=1, source_target_pairs={{0,224},{4,228},{8,232},{12,236},{16,240},{20,244},{24,248},{28,25... | collective-permute-start | bytes 98312 | tf_op jit(solution)/shard_map/ppermute | solution.py:449
  134.4 2.2 %collective-permute-start.16 = (bf16[128,128]{1,0:T(8,128)(2,1)S(1)}, bf16[128,128]{1,0:T(8,128)(2,1)S(1)}, u32[]{:S(2)}, u32[]{:S(2)}) collective-permute-start(bf16[128,128]{1,0:T(8,128)(2,1)S(1)} %copy-done.10), channel_id=1, source_target_pairs={{0,192},{4,196},{8,200},{12,204},{16,208},{20,212},{24,216},{28,22... | collective-permute-start | bytes 98312 | tf_op jit(solution)/shard_map/ppermute | solution.py:449
  136.7 1.3 collective-permute-start.15
  138.0 4.0 %collective-permute-done.17.refs_7_ = bf16[128,128]{1,0:T(8,128)(2,1)S(1)} collective-permute-done((bf16[128,128]{1,0:T(8,128)(2,1)S(1)}, bf16[128,128]{1,0:T(8,128)(2,1)S(1)}, u32[]{:S(2)}, u32[]{:S(2)}) %collective-permute-start.17) | collective-permute-done | bytes 32800 | tf_op jit(solution)/shard_map/ppermute | solution.py:449
  142.0 4.1 %collective-permute-start.14 = (bf16[128,128]{1,0:T(8,128)(2,1)S(1)}, bf16[128,128]{1,0:T(8,128)(2,1)S(1)}, u32[]{:S(2)}, u32[]{:S(2)}) collective-permute-start(bf16[128,128]{1,0:T(8,128)(2,1)S(1)} %copy-done.10), channel_id=1, source_target_pairs={{0,128},{4,132},{8,136},{12,140},{16,144},{20,148},{24,152},{28,15... | collective-permute-start | bytes 98312 | tf_op jit(solution)/shard_map/ppermute | solution.py:449
  146.1 1.1 collective-permute-start.13
  147.2 1.9 %collective-permute-start.12 = (bf16[128,128]{1,0:T(8,128)(2,1)S(1)}, bf16[128,128]{1,0:T(8,128)(2,1)S(1)}, u32[]{:S(2)}, u32[]{:S(2)}) collective-permute-start(bf16[128,128]{1,0:T(8,128)(2,1)S(1)} %copy-done.10), channel_id=1, source_target_pairs={{0,64},{4,68},{8,72},{12,76},{16,80},{20,84},{24,88},{28,92},{32,9... | collective-permute-start | bytes 98312 | tf_op jit(solution)/shard_map/ppermute | solution.py:449
  149.1 0.8 collective-permute-done.14.refs_4_
  150.1 4.1 %collective-permute-done.13.refs_3_ = bf16[128,128]{1,0:T(8,128)(2,1)S(1)} collective-permute-done((bf16[128,128]{1,0:T(8,128)(2,1)S(1)}, bf16[128,128]{1,0:T(8,128)(2,1)S(1)}, u32[]{:S(2)}, u32[]{:S(2)}) %collective-permute-start.13) | collective-permute-done | bytes 32800 | tf_op jit(solution)/shard_map/ppermute | solution.py:449
  154.2 0.9 collective-permute-done.11.refs_1_
  155.7 1.6 add_z.1.after.t0
  157.3 2.6 %collective-permute-start.24 = (f32[128,128]{1,0:T(8,128)}, f32[128,128]{1,0:T(8,128)S(1)}, u32[]{:S(2)}, u32[]{:S(2)}) collective-permute-start(f32[128,128]{1,0:T(8,128)} %add_z.1.after.t0), channel_id=1, source_target_pairs={{0,24},{4,28},{8,0},{12,4},{16,8},{20,12},{24,16},{28,20},{32,56},... | collective-permute-start | bytes 196616 | tf_op jit(solution)/shard_map/ppermute | solution.py:449
  159.9 1.4 collective-permute-start.23
  161.5 1.4 copy-done.2
  162.9 11.9 %tiles_fwd.1.after = bf16[32,128,128]{2,1,0:T(8,128)(2,1)} custom-call(s32[1]{0:T(128)S(6)} %copy.12.count_ref, s32[1,176]{1,0:T(1,128)} %rows_ref.3, s32[1,176]{1,0:T(1,128)} %cols_ref.3, s32[8,4096]{1,0:T(8,128)} %bitcast.11, bf16[32,128,128]{2,1,0:T(8,128)(2,1)} %get-tuple-element.16.own_hbm, bf16[64,128,128]{2,1,0:T(8,128)(2,1)} %copy-done.2, ...), custom_call_target="tpu_custom_call" | custom-call | flops 738197504 | bytes 31457280 | tf_op jit(solution)/shard_map/tiles_fwd/pallas_call | solution.py:175
  176.1 1.7 round_y.1
  177.8 0.8 copy-done.7
  178.8 4.6 %d_times_wt.1 = bf16[4096,128]{1,0:T(8,128)(2,1)} custom-call(bf16[4096,128]{1,0:T(8,128)(2,1)} %bitcast.9, bf16[4096,128]{1,0:T(8,128)(2,1)} %collective-permute-done.18.v1.d1, bf16[2048,128]{1,0:T(8,128)(2,1)} %copy-done.7, bf16[2048,128]{1,0:T(8,128)(2,1)} %copy-done.8, bf16[4096,128]{1,0:T(8,128)(2,1)} %copy-done.3, ...), custom_call_target="tpu_custom_call" | custom-call | flops 536870912 | bytes 5242880 | tf_op jit(solution)/shard_map/d_times_wt/pallas_call | solution.py:392
  (74 shorter events, 5.3 us)
Async XLA Ops:
  14.5 12.5 %copy-start.4 = (bf16[4096,128]{1,0:T(8,128)(2,1)S(1)}, bf16[4096,128]{1,0:T(8,128)(2,1)}, u32[]{:S(2)}) copy-start(bf16[4096,128]{1,0:T(8,128)(2,1)} %x0.3) | copy-start | bytes 3145732
  14.5 67.7 %all-to-all-start.1 = ((bf16[64,128,128]{2,1,0:T(8,128)(2,1)}), bf16[64,128,128]{2,1,0:T(8,128)(2,1)}, u32[]{:S(2)}, u32[]{:S(2)}) async-start(bf16[64,128,128]{2,1,0:T(8,128)(2,1)} %get-tuple-element.13.after), calls=%async_computation.1 | async-start | bytes 4194304 | tf_op jit(solution)/shard_map/all_to_all | solution.py:453
  27.0 32.6 %copy-start.9 = (bf16[512,128]{1,0:T(8,128)(2,1)S(1)}, bf16[512,128]{1,0:T(8,128)(2,1)}, u32[]{:S(2)}) copy-start(bf16[512,128]{1,0:T(8,128)(2,1)} %w_ref.1) | copy-start | bytes 393220
  27.0 26.3 %collective-permute-start.1 = (bf16[4096,128]{1,0:T(8,128)(2,1)S(1)}, bf16[4096,128]{1,0:T(8,128)(2,1)S(1)}, u32[]{:S(2)}, u32[]{:S(2)}) collective-permute-start(bf16[4096,128]{1,0:T(8,128)(2,1)S(1)} %copy-done.4), channel_id=1, source_target_pairs={{0,3},{1,0},{2,1},{3,2},{4,7},{5,4},{6,5},{7,6},{8,11},{9,8},{10,9... | collective-permute-start | bytes 3145736 | tf_op jit(solution)/shard_map/ppermute | solution.py:410
  27.9 25.4 %collective-permute-start = (bf16[4096,128]{1,0:T(8,128)(2,1)S(1)}, bf16[4096,128]{1,0:T(8,128)(2,1)S(1)}, u32[]{:S(2)}, u32[]{:S(2)}) collective-permute-start(bf16[4096,128]{1,0:T(8,128)(2,1)S(1)} %copy-done.4), channel_id=1, source_target_pairs={{0,1},{1,2},{2,3},{3,0},{4,5},{5,6},{6,7},{7,4},{8,9},{9,10},{10,1... | collective-permute-start | bytes 3145736 | tf_op jit(solution)/shard_map/ppermute | solution.py:410
  53.4 1.0 copy-start
  54.3 1.0 copy-start.1
  57.5 17.3 %collective-permute-start.2 = (bf16[2048,128]{1,0:T(8,128)(2,1)}, bf16[2048,128]{1,0:T(8,128)(2,1)S(1)}, u32[]{:S(2)}, u32[]{:S(2)}) collective-permute-start(bf16[2048,128]{1,0:T(8,128)(2,1)} %get-tuple-element.14), channel_id=1, source_target_pairs={{0,1},{1,2},{2,3},{3,0},{4,5},{5,6},{6,7},{7,4},{8,9},{9,10},{10,1... | collective-permute-start | bytes 1572872 | tf_op jit(solution)/shard_map/ppermute | solution.py:410
  59.5 15.3 %collective-permute-start.3 = (bf16[2048,128]{1,0:T(8,128)(2,1)}, bf16[2048,128]{1,0:T(8,128)(2,1)S(1)}, u32[]{:S(2)}, u32[]{:S(2)}) collective-permute-start(bf16[2048,128]{1,0:T(8,128)(2,1)} %get-tuple-element.15), channel_id=1, source_target_pairs={{0,3},{1,0},{2,1},{3,2},{4,7},{5,4},{6,5},{7,6},{8,11},{9,8},{10,9... | collective-permute-start | bytes 1572872 | tf_op jit(solution)/shard_map/ppermute | solution.py:410
  60.2 14.6 %collective-permute-start.6 = (bf16[128,128]{1,0:T(8,128)(2,1)S(1)}, bf16[128,128]{1,0:T(8,128)(2,1)S(1)}, u32[]{:S(2)}, u32[]{:S(2)}) collective-permute-start(bf16[128,128]{1,0:T(8,128)(2,1)S(1)} %get-tuple-element.28), channel_id=1, source_target_pairs={{0,3},{1,0},{2,1},{3,2},{4,7},{5,4},{6,5},{7,6},{8,11},{9,8},{10,9... | collective-permute-start | bytes 98312 | tf_op jit(solution)/shard_map/ppermute | solution.py:410
  60.2 14.6 %collective-permute-start.5 = (bf16[128,128]{1,0:T(8,128)(2,1)S(1)}, bf16[128,128]{1,0:T(8,128)(2,1)S(1)}, u32[]{:S(2)}, u32[]{:S(2)}) collective-permute-start(bf16[128,128]{1,0:T(8,128)(2,1)S(1)} %get-tuple-element.29), channel_id=1, source_target_pairs={{0,2},{1,3},{2,0},{3,1},{4,6},{5,7},{6,4},{7,5},{8,10},{9,11},{10,... | collective-permute-start | bytes 98312 | tf_op jit(solution)/shard_map/ppermute | solution.py:410
  64.8 10.0 %collective-permute-start.4 = (bf16[128,128]{1,0:T(8,128)(2,1)S(1)}, bf16[128,128]{1,0:T(8,128)(2,1)S(1)}, u32[]{:S(2)}, u32[]{:S(2)}) collective-permute-start(bf16[128,128]{1,0:T(8,128)(2,1)S(1)} %get-tuple-element.30), channel_id=1, source_target_pairs={{0,1},{1,2},{2,3},{3,0},{4,5},{5,6},{6,7},{7,4},{8,9},{9,10},{10,1... | collective-permute-start | bytes 98312 | tf_op jit(solution)/shard_map/ppermute | solution.py:410
  74.8 0.6 copy-start.13
  74.8 0.8 copy-start.5
  75.7 0.8 copy-start.6
  82.2 79.3 %all-to-all-start = ((bf16[64,128,128]{2,1,0:T(8,128)(2,1)}), bf16[64,128,128]{2,1,0:T(8,128)(2,1)S(1)}, u32[]{:S(2)}, u32[]{:S(2)}) async-start(bf16[64,128,128]{2,1,0:T(8,128)(2,1)} %get-tuple-element.17.after), calls=%async_computation | async-start | bytes 4194304 | tf_op jit(solution)/shard_map/all_to_all | solution.py:453
  99.5 26.4 %collective-permute-start.19 = (bf16[4096,128]{1,0:T(8,128)(2,1)}, bf16[4096,128]{1,0:T(8,128)(2,1)S(1)}, u32[]{:S(2)}, u32[]{:S(2)}) collective-permute-start(bf16[4096,128]{1,0:T(8,128)(2,1)} %bitcast.7), channel_id=1, source_target_pairs={{0,3},{1,0},{2,1},{3,2},{4,7},{5,4},{6,5},{7,6},{8,11},{9,8},{10,9... | collective-permute-start | bytes 3145736 | tf_op jit(solution)/shard_map/ppermute | solution.py:410
  99.6 26.4 %collective-permute-start.18 = (bf16[4096,128]{1,0:T(8,128)(2,1)}, bf16[4096,128]{1,0:T(8,128)(2,1)}, u32[]{:S(2)}, u32[]{:S(2)}) collective-permute-start(bf16[4096,128]{1,0:T(8,128)(2,1)} %bitcast.8), channel_id=1, source_target_pairs={{0,1},{1,2},{2,3},{3,0},{4,5},{5,6},{6,7},{7,4},{8,9},{9,10},{10,1... | collective-permute-start | bytes 3145736 | tf_op jit(solution)/shard_map/ppermute | solution.py:410
  102.8 1.7 collective-permute-start.7
  106.2 7.6 %collective-permute-start.10 = (f32[128,128]{1,0:T(8,128)S(1)}, f32[128,128]{1,0:T(8,128)S(1)}, u32[]{:S(2)}, u32[]{:S(2)}) collective-permute-start(f32[128,128]{1,0:T(8,128)S(1)} %get-tuple-element.23), channel_id=1, source_target_pairs={{0,16},{4,20},{8,24},{12,28},{16,0},{20,4},{24,8},{28,12},{32,48},... | collective-permute-start | bytes 196616 | tf_op jit(solution)/shard_map/ppermute | solution.py:449
  109.1 6.3 %collective-permute-start.9 = (f32[128,128]{1,0:T(8,128)S(1)}, f32[128,128]{1,0:T(8,128)S(1)}, u32[]{:S(2)}, u32[]{:S(2)}) collective-permute-start(f32[128,128]{1,0:T(8,128)S(1)} %get-tuple-element.24), channel_id=1, source_target_pairs={{0,24},{4,28},{8,0},{12,4},{16,8},{20,12},{24,16},{28,20},{32,56},... | collective-permute-start | bytes 196616 | tf_op jit(solution)/shard_map/ppermute | solution.py:449
  110.3 6.7 %collective-permute-start.8 = (f32[128,128]{1,0:T(8,128)S(1)}, f32[128,128]{1,0:T(8,128)S(1)}, u32[]{:S(2)}, u32[]{:S(2)}) collective-permute-start(f32[128,128]{1,0:T(8,128)S(1)} %get-tuple-element.25), channel_id=1, source_target_pairs={{0,8},{4,12},{8,16},{12,20},{16,24},{20,28},{24,0},{28,4},{32,40},... | collective-permute-start | bytes 196616 | tf_op jit(solution)/shard_map/ppermute | solution.py:449
  113.8 3.1 %copy-start.17 = (f32[128,128]{1,0:T(8,128)}, f32[128,128]{1,0:T(8,128)S(1)}, u32[]{:S(2)}) copy-start(f32[128,128]{1,0:T(8,128)S(1)} %collective-permute-done.10.d) | copy-start | bytes 196612
  115.4 1.5 copy-start.18
  119.1 12.1 %copy-start.10 = (bf16[128,128]{1,0:T(8,128)(2,1)S(1)}, bf16[128,128]{1,0:T(8,128)(2,1)}, u32[]{:S(2)}) copy-start(bf16[128,128]{1,0:T(8,128)(2,1)} %add_y.1.refs_0_.after) | copy-start | bytes 98308
  125.9 1.0 copy-start.3
  129.2 48.6 %collective-permute-start.20 = (bf16[2048,128]{1,0:T(8,128)(2,1)}, bf16[2048,128]{1,0:T(8,128)(2,1)S(1)}, u32[]{:S(2)}, u32[]{:S(2)}) collective-permute-start(bf16[2048,128]{1,0:T(8,128)(2,1)} %get-tuple-element.21), channel_id=1, source_target_pairs={{0,1},{1,2},{2,3},{3,0},{4,5},{5,6},{6,7},{7,4},{8,9},{9,10},{10,1... | collective-permute-start | bytes 1572872 | tf_op jit(solution)/shard_map/ppermute | solution.py:410
  131.3 46.5 %collective-permute-start.21 = (bf16[2048,128]{1,0:T(8,128)(2,1)}, bf16[2048,128]{1,0:T(8,128)(2,1)S(1)}, u32[]{:S(2)}, u32[]{:S(2)}) collective-permute-start(bf16[2048,128]{1,0:T(8,128)(2,1)} %get-tuple-element.22), channel_id=1, source_target_pairs={{0,3},{1,0},{2,1},{3,2},{4,7},{5,4},{6,5},{7,6},{8,11},{9,8},{10,9... | collective-permute-start | bytes 1572872 | tf_op jit(solution)/shard_map/ppermute | solution.py:410
  131.3 10.7 %collective-permute-start.17 = (bf16[128,128]{1,0:T(8,128)(2,1)S(1)}, bf16[128,128]{1,0:T(8,128)(2,1)S(1)}, u32[]{:S(2)}, u32[]{:S(2)}) collective-permute-start(bf16[128,128]{1,0:T(8,128)(2,1)S(1)} %copy-done.10), channel_id=1, source_target_pairs={{0,224},{4,228},{8,232},{12,236},{16,240},{20,244},{24,248},{28,25... | collective-permute-start | bytes 98312 | tf_op jit(solution)/shard_map/ppermute | solution.py:449
  134.4 11.7 %collective-permute-start.16 = (bf16[128,128]{1,0:T(8,128)(2,1)S(1)}, bf16[128,128]{1,0:T(8,128)(2,1)S(1)}, u32[]{:S(2)}, u32[]{:S(2)}) collective-permute-start(bf16[128,128]{1,0:T(8,128)(2,1)S(1)} %copy-done.10), channel_id=1, source_target_pairs={{0,192},{4,196},{8,200},{12,204},{16,208},{20,212},{24,216},{28,22... | collective-permute-start | bytes 98312 | tf_op jit(solution)/shard_map/ppermute | solution.py:449
  136.7 10.6 %collective-permute-start.15 = (bf16[128,128]{1,0:T(8,128)(2,1)S(1)}, bf16[128,128]{1,0:T(8,128)(2,1)S(1)}, u32[]{:S(2)}, u32[]{:S(2)}) collective-permute-start(bf16[128,128]{1,0:T(8,128)(2,1)S(1)} %copy-done.10), channel_id=1, source_target_pairs={{0,160},{4,164},{8,168},{12,172},{16,176},{20,180},{24,184},{28,18... | collective-permute-start | bytes 98312 | tf_op jit(solution)/shard_map/ppermute | solution.py:449
  142.0 13.1 %copy-start.20 = (bf16[128,128]{1,0:T(8,128)(2,1)}, bf16[128,128]{1,0:T(8,128)(2,1)S(1)}, u32[]{:S(2)}) copy-start(bf16[128,128]{1,0:T(8,128)(2,1)S(1)} %collective-permute-done.17.refs_7_) | copy-start | bytes 98308
  142.0 7.9 %collective-permute-start.14 = (bf16[128,128]{1,0:T(8,128)(2,1)S(1)}, bf16[128,128]{1,0:T(8,128)(2,1)S(1)}, u32[]{:S(2)}, u32[]{:S(2)}) collective-permute-start(bf16[128,128]{1,0:T(8,128)(2,1)S(1)} %copy-done.10), channel_id=1, source_target_pairs={{0,128},{4,132},{8,136},{12,140},{16,144},{20,148},{24,152},{28,15... | collective-permute-start | bytes 98312 | tf_op jit(solution)/shard_map/ppermute | solution.py:449
  146.1 9.0 %copy-start.21 = (bf16[128,128]{1,0:T(8,128)(2,1)}, bf16[128,128]{1,0:T(8,128)(2,1)S(1)}, u32[]{:S(2)}) copy-start(bf16[128,128]{1,0:T(8,128)(2,1)S(1)} %collective-permute-done.16.refs_6_) | copy-start | bytes 98308
  146.1 8.1 %collective-permute-start.13 = (bf16[128,128]{1,0:T(8,128)(2,1)S(1)}, bf16[128,128]{1,0:T(8,128)(2,1)S(1)}, u32[]{:S(2)}, u32[]{:S(2)}) collective-permute-start(bf16[128,128]{1,0:T(8,128)(2,1)S(1)} %copy-done.10), channel_id=1, source_target_pairs={{0,96},{4,100},{8,104},{12,108},{16,112},{20,116},{24,120},{28,124... | collective-permute-start | bytes 98312 | tf_op jit(solution)/shard_map/ppermute | solution.py:449
  147.2 7.8 %copy-start.22 = (bf16[128,128]{1,0:T(8,128)(2,1)}, bf16[128,128]{1,0:T(8,128)(2,1)S(1)}, u32[]{:S(2)}) copy-start(bf16[128,128]{1,0:T(8,128)(2,1)S(1)} %collective-permute-done.15.refs_5_) | copy-start | bytes 98308
  147.2 6.9 %collective-permute-start.12 = (bf16[128,128]{1,0:T(8,128)(2,1)S(1)}, bf16[128,128]{1,0:T(8,128)(2,1)S(1)}, u32[]{:S(2)}, u32[]{:S(2)}) collective-permute-start(bf16[128,128]{1,0:T(8,128)(2,1)S(1)} %copy-done.10), channel_id=1, source_target_pairs={{0,64},{4,68},{8,72},{12,76},{16,80},{20,84},{24,88},{28,92},{32,9... | collective-permute-start | bytes 98312 | tf_op jit(solution)/shard_map/ppermute | solution.py:449
  149.9 5.1 %copy-start.23 = (bf16[128,128]{1,0:T(8,128)(2,1)}, bf16[128,128]{1,0:T(8,128)(2,1)S(1)}, u32[]{:S(2)}) copy-start(bf16[128,128]{1,0:T(8,128)(2,1)S(1)} %collective-permute-done.14.refs_4_) | copy-start | bytes 98308
  149.9 5.1 %collective-permute-start.11 = (bf16[128,128]{1,0:T(8,128)(2,1)S(1)}, bf16[128,128]{1,0:T(8,128)(2,1)S(1)}, u32[]{:S(2)}, u32[]{:S(2)}) collective-permute-start(bf16[128,128]{1,0:T(8,128)(2,1)S(1)} %copy-done.10), channel_id=1, source_target_pairs={{0,32},{4,36},{8,40},{12,44},{16,48},{20,52},{24,56},{28,60},{32,6... | collective-permute-start | bytes 98312 | tf_op jit(solution)/shard_map/ppermute | solution.py:449
  154.2 0.9 copy-start.24
  154.2 0.9 copy-start.25
  157.3 17.5 %collective-permute-start.24 = (f32[128,128]{1,0:T(8,128)}, f32[128,128]{1,0:T(8,128)S(1)}, u32[]{:S(2)}, u32[]{:S(2)}) collective-permute-start(f32[128,128]{1,0:T(8,128)} %add_z.1.after.t0), channel_id=1, source_target_pairs={{0,24},{4,28},{8,0},{12,4},{16,8},{20,12},{24,16},{28,20},{32,56},... | collective-permute-start | bytes 196616 | tf_op jit(solution)/shard_map/ppermute | solution.py:449
  159.9 14.9 %collective-permute-start.23 = (f32[128,128]{1,0:T(8,128)}, f32[128,128]{1,0:T(8,128)S(1)}, u32[]{:S(2)}, u32[]{:S(2)}) collective-permute-start(f32[128,128]{1,0:T(8,128)} %add_z.1.after.t0), channel_id=1, source_target_pairs={{0,16},{4,20},{8,24},{12,28},{16,0},{20,4},{24,8},{28,12},{32,48},... | collective-permute-start | bytes 196616 | tf_op jit(solution)/shard_map/ppermute | solution.py:449
  161.3 13.6 %collective-permute-start.22 = (f32[128,128]{1,0:T(8,128)}, f32[128,128]{1,0:T(8,128)S(1)}, u32[]{:S(2)}, u32[]{:S(2)}) collective-permute-start(f32[128,128]{1,0:T(8,128)} %add_z.1.after.t0), channel_id=1, source_target_pairs={{0,8},{4,12},{8,16},{12,20},{16,24},{20,28},{24,0},{28,4},{32,40},... | collective-permute-start | bytes 196616 | tf_op jit(solution)/shard_map/ppermute | solution.py:449
  161.5 1.4 copy-start.2
  174.9 0.6 copy-start.15
  177.8 0.8 copy-start.7
  177.8 1.0 copy-start.8
  (6 other events, 3.7 us)

commit v2 on v1

v2 whole, which is shorter than its diff:
```python
import functools

import jax
import jax.numpy as jnp
from jax import lax
from jax.experimental import pallas as pl
from jax.experimental.pallas import tpu as pltpu
from jax.sharding import PartitionSpec as P

B = 128
RB = 32
HID = 4
CHUNK = RB // HID
F32 = jnp.float32
BF16 = jnp.bfloat16
MIB = 1024 * 1024

VMEM = pl.BlockSpec(memory_space=pltpu.VMEM)
SMEM = pl.BlockSpec(memory_space=pltpu.SMEM)
ANY = pl.BlockSpec(memory_space=pl.ANY)
HBM = pl.BlockSpec(memory_space=pltpu.HBM)


def params(mib=60):
    return pltpu.CompilerParams(vmem_limit_bytes=mib * MIB)


def cost(flops, nbytes):
    return pl.CostEstimate(flops=flops, bytes_accessed=nbytes, transcendentals=0)


def dot(a, b, dims=((1,), (0,))):
    return lax.dot_general(a, b, (dims, ((), ())), preferred_element_type=F32)


def rel(me, shift):
    return lax.rem(me + shift + HID, HID)


def bit_mask(words):
    halves = jnp.concatenate([words & 255, words >> 8], 0).astype(F32).astype(BF16)
    row = lax.broadcasted_iota(jnp.int32, (16, B), 0)
    unit = lax.broadcasted_iota(jnp.int32, (16, B), 1)
    byte_row = (unit // 16) + 8 * ((unit % 16) // 8)
    scale = lax.div(jnp.ones((16, B), F32), (1 << (unit % 8)).astype(F32))
    spread = jnp.where(row == byte_row, scale, 0.0).astype(BF16)
    shifted = dot(halves, spread, ((0,), (0,)))
    return (shifted.astype(jnp.int32) & 1) == 1


STEP = 256
MASK_STEP = 1024
TILES = 176
PIECES = 4
PIECE = TILES // PIECES


def tile_copies(tiles_hbm, tiles, sems):
    return [
        pltpu.make_async_copy(
            tiles_hbm.at[pl.ds(k * PIECE, PIECE)], tiles.at[pl.ds(k * PIECE, PIECE)], sems.at[k]
        )
        for k in range(PIECES)
    ]


def tiles_bwd_kernel(count_ref, rows_ref, cols_ref, bits_hbm, cot_hbm, tiles_hbm, own_hbm,
                     slot_hbm, tiles, bits, cot, d_t, acc, slots, sems, out_sems):
    count = count_ref[0]
    bits_in = pltpu.make_async_copy(bits_hbm, bits, sems.at[PIECES])
    cot_in = pltpu.make_async_copy(cot_hbm, cot, sems.at[PIECES + 1])
    bits_in.start()
    cot_in.start()
    copies = tile_copies(tiles_hbm, tiles, sems)
    for c in copies:
        c.start()
    acc[...] = jnp.zeros_like(acc)
    bits_in.wait()
    cot_in.wait()

    def mask(i, carry):
        at = pl.multiple_of(i * MASK_STEP, MASK_STEP)
        active = bit_mask(bits[:, pl.ds(at, MASK_STEP)])
        v = jnp.where(active, cot[pl.ds(at, MASK_STEP), :].astype(F32), 0.0)
        for j in range(MASK_STEP // B):
            d_t[i * (MASK_STEP // B) + j] = v[j * B : (j + 1) * B].T.astype(BF16)
        return carry

    lax.fori_loop(0, 4096 // MASK_STEP, mask, 0)
    for k in range(PIECES):
        copies[k].wait()

        for t in range(k * PIECE, (k + 1) * PIECE):
            s = jnp.where(t < count, cols_ref[0, t], RB + 64)
            acc[s] += dot(d_t[rows_ref[0, t]], tiles[t])
    outs = []
    for k in range(4):
        at = pl.ds(k * 16, 16)
        slots[at] = acc[RB + k * 16 : RB + (k + 1) * 16].astype(BF16)
        outs.append(pltpu.make_async_copy(slots.at[at], slot_hbm.at[at], out_sems.at[k]))
        outs[-1].start()
    outs.append(pltpu.make_async_copy(acc.at[pl.ds(0, RB)], own_hbm, out_sems.at[4]))
    outs[-1].start()
    for c in outs:
        c.wait()


def tiles_bwd_call(count, rows, cols, bits_t, cot, tiles):
    return pl.pallas_call(
        tiles_bwd_kernel,
        out_shape=[
            jax.ShapeDtypeStruct((RB, B, B), F32),
            jax.ShapeDtypeStruct((64, B, B), BF16),
        ],
        in_specs=[SMEM] * 3 + [ANY] * 3,
        out_specs=[HBM] * 2,
        scratch_shapes=[
            pltpu.VMEM((TILES, B, B), BF16),
            pltpu.VMEM((8, 4096), jnp.int32),
            pltpu.VMEM((4096, B), BF16),
            pltpu.VMEM((RB, B, B), BF16),
            pltpu.VMEM((RB + 65, B, B), F32),
            pltpu.VMEM((64, B, B), BF16),
            pltpu.SemaphoreType.DMA((PIECES + 2,)),
            pltpu.SemaphoreType.DMA((5,)),
        ],
        compiler_params=params(),
        cost_estimate=cost(2 * TILES * B * B * B, 30 << 20),
        name="tiles_bwd",
    )(count, rows, cols, bits_t, cot, tiles)


def tiles_fwd_kernel(count_ref, rows_ref, cols_ref, bits_hbm, own_hbm, recv_hbm, tiles_hbm,
                     out_ref, token, tiles, src, acc, bits, sems):
    count = count_ref[0]
    own = pltpu.make_async_copy(own_hbm, src.at[pl.ds(0, RB)], sems.at[PIECES])
    got = pltpu.make_async_copy(recv_hbm, src.at[pl.ds(RB, 64)], sems.at[PIECES + 1])
    bits_in = pltpu.make_async_copy(bits_hbm, bits, sems.at[PIECES + 2])
    own.start()
    got.start()
    copies = tile_copies(tiles_hbm, tiles, sems)
    for c in copies:
        c.start()
    bits_in.start()
    acc[...] = jnp.zeros_like(acc)
    own.wait()
    got.wait()
    for k in range(PIECES):
        copies[k].wait()

        for t in range(k * PIECE, (k + 1) * PIECE):
            r = jnp.where(t < count, rows_ref[0, t], RB)
            acc[r] += dot(tiles[t], src[cols_ref[0, t]])

    token[...] = jnp.zeros_like(token)
    bits_in.wait()

    def mask(i, carry):
        at = pl.multiple_of(i * MASK_STEP, MASK_STEP)
        active = bit_mask(bits[:, pl.ds(at, MASK_STEP)])
        for j in range(MASK_STEP // B):
            b = i * (MASK_STEP // B) + j
            out_ref[b] = jnp.where(active[j * B : (j + 1) * B], acc[b], 0.0).astype(BF16)
        return carry

    lax.fori_loop(0, 4096 // MASK_STEP, mask, 0)


def tiles_fwd_call(count, rows, cols, bits_t, own, recv, tiles):
    return pl.pallas_call(
        tiles_fwd_kernel,
        out_shape=[jax.ShapeDtypeStruct((RB, B, B), BF16), jax.ShapeDtypeStruct((8, B), F32)],
        in_specs=[SMEM] * 3 + [ANY] * 4,
        out_specs=[VMEM] * 2,
        scratch_shapes=[
            pltpu.VMEM((TILES, B, B), BF16),
            pltpu.VMEM((RB + 64, B, B), BF16),
            pltpu.VMEM((RB + 1, B, B), F32),
            pltpu.VMEM((8, 4096), jnp.int32),
            pltpu.SemaphoreType.DMA((PIECES + 3,)),
        ],
        compiler_params=params(58),
        cost_estimate=cost(2 * TILES * B * B * B, 30 << 20),
        name="tiles_fwd",
    )(count, rows, cols, bits_t, own, recv, tiles)


def hidden_kernel(me_ref, send_ref, x0, x1, x2a, x2b, x3, w_ref, hid_hbm, out_hbm, hid, sems):
    me = me_ref[0]
    rhs = jnp.concatenate(
        [w_ref[pl.ds(pl.multiple_of(rel(me, -s) * B, B), B), :] for s in range(HID)], 0
    )
    for n in range(4096 // STEP):
        half, at = (x2a, n * STEP) if n < 2048 // STEP else (x2b, n * STEP - 2048)
        here = slice(n * STEP, (n + 1) * STEP)
        lhs = jnp.concatenate([x0[here, :], x1[here, :], half[at : at + STEP, :], x3[here, :]], 1)
        r = dot(lhs, rhs).astype(BF16)
        for j in range(STEP // B):
            hid[n * (STEP // B) + j] = r[j * B : (j + 1) * B]
    copies = [
        pltpu.make_async_copy(hid.at[send_ref[0, q]], out_hbm.at[q], sems.at[q]) for q in range(64)
    ]
    copies.append(pltpu.make_async_copy(hid, hid_hbm, sems.at[64]))
    for c in copies:
        c.start()
    for c in copies:
        c.wait()


def hidden_call(me, send, xs, w):
    return pl.pallas_call(
        hidden_kernel,
        out_shape=[
            jax.ShapeDtypeStruct((RB, B, B), BF16),
            jax.ShapeDtypeStruct((64, B, B), BF16),
        ],
        in_specs=[SMEM] * 2 + [VMEM] * 6,
        out_specs=[HBM] * 2,
        scratch_shapes=[pltpu.VMEM((RB, B, B), BF16), pltpu.SemaphoreType.DMA((65,))],
        compiler_params=params(),
        cost_estimate=cost(2 * 4096 * 512 * 128, 10 << 20),
        name="hidden",
    )(me, send, *xs, w)


def sum_kernel(me_ref, send_ref, own_hbm, got_hbm, x0, x1, x2a, x2b, x3, w_hbm, after,
               terms_hbm, p0, p1, p2a, p2b, p3, acc, got, xv, w, flat, pv, terms, sems, out_sems):
    me, y = me_ref[0], me_ref[1]
    ins = [
        pltpu.make_async_copy(own_hbm, acc, sems.at[0]),
        pltpu.make_async_copy(got_hbm, got, sems.at[1]),
        pltpu.make_async_copy(x0, xv.at[0], sems.at[2]),
        pltpu.make_async_copy(x1, xv.at[1], sems.at[3]),
        pltpu.make_async_copy(x2a, xv.at[2, pl.ds(0, 2048)], sems.at[4]),
        pltpu.make_async_copy(x2b, xv.at[2, pl.ds(2048, 2048)], sems.at[5]),
        pltpu.make_async_copy(x3, xv.at[3], sems.at[6]),
        pltpu.make_async_copy(w_hbm, w, sems.at[7]),
    ]
    for i in ins:
        i.start()
    ins[0].wait()
    ins[1].wait()

    def body(i, carry):
        for j in range(8):
            q = i * 8 + j
            acc[send_ref[0, q]] += got[q].astype(F32)
        return carry

    lax.fori_loop(0, 8, body, 0)
    outs = []

    ins[7].wait()
    rhs = jnp.concatenate(
        [w[pl.ds(pl.multiple_of(rel(me, s) * B, B), B), :] for s in range(HID)], 0
    )

    def part(i, carry):
        d = jnp.concatenate([acc[i * 4 + j].T.astype(BF16) for j in range(4)], 0)
        r = dot(d, rhs, ((1,), (1,))).astype(BF16)
        for s in range(HID):
            pv[s, pl.ds(pl.multiple_of(i * 512, 512), 512), :] = r[:, s * B : (s + 1) * B]
        return carry

    lax.fori_loop(0, RB // 4, part, 0)
    low, high = pl.ds(0, 2048), pl.ds(2048, 2048)
    for k, (p, v) in enumerate(
        ((p2a, pv.at[2, low]), (p2b, pv.at[2, high]), (p0, pv.at[0]), (p1, pv.at[1]), (p3, pv.at[3]))
    ):
        outs.append(pltpu.make_async_copy(v, p, out_sems.at[k]))
        outs[-1].start()
    for b in range(RB):
        flat[:, b * B : (b + 1) * B] = acc[b].astype(BF16)
    for i in ins[2:7]:
        i.wait()
    for s in range(HID):
        r = dot(flat[...], xv[s]).T
        terms[pl.ds(pl.multiple_of(rel(me, -s) * B, B), B), :] = r
    for k in range(4):
        at = pl.multiple_of(lax.rem(y + k, 4) * B, B)
        outs.append(
            pltpu.make_async_copy(
                terms.at[pl.ds(at, B)], terms_hbm.at[pl.ds(k * B, B)], out_sems.at[5 + k]
            )
        )
        outs[-1].start()
    for o in outs:
        o.wait()


def sum_call(me, send, own, got, xs, w, after):
    return pl.pallas_call(
        sum_kernel,
        out_shape=[jax.ShapeDtypeStruct((512, B), F32)]
        + [jax.ShapeDtypeStruct((n, B), BF16) for n in (4096, 4096, 2048, 2048, 4096)],
        in_specs=[SMEM] * 2 + [ANY] * 9,
        out_specs=[HBM] * 6,
        scratch_shapes=[
            pltpu.VMEM((RB, B, B), F32),
            pltpu.VMEM((64, B, B), BF16),
            pltpu.VMEM((HID, 4096, B), BF16),
            pltpu.VMEM((512, B), BF16),
            pltpu.VMEM((B, 4096), BF16),
            pltpu.VMEM((HID, 4096, B), BF16),
            pltpu.VMEM((512, B), F32),
            pltpu.SemaphoreType.DMA((8,)),
            pltpu.SemaphoreType.DMA((9,)),
        ],
        compiler_params=params(),
        cost_estimate=cost(2 * 4096 * 512 * 128, 12 << 20),
        name="sum_returned",
    )(me, send, own, got, *xs, w, after)


def add_kernel(a, b, c, d, out):
    out[...] = ((a[...] + b[...]) + (c[...] + d[...])).astype(BF16)


def add_call(parts):
    return pl.pallas_call(
        add_kernel,
        out_shape=jax.ShapeDtypeStruct((B, B), BF16),
        in_specs=[VMEM] * 4,
        out_specs=VMEM,
        compiler_params=params(8),
        cost_estimate=cost(4 * B * B, 1 << 18),
        name="add_y",
    )(*parts)


def add_z_kernel(me_ref, p0, p1, p2, p3, out, by_z):
    z = lax.div(me_ref[2], 2)
    for k, p in enumerate((p0, p1, p2, p3)):
        by_z[rel(z, -k)] = p[...].astype(F32)
    out[...] = (by_z[0] + by_z[1]) + (by_z[2] + by_z[3])


def add_z_call(me, parts):
    return pl.pallas_call(
        add_z_kernel,
        out_shape=jax.ShapeDtypeStruct((B, B), F32),
        in_specs=[SMEM] + [VMEM] * 4,
        out_specs=VMEM,
        scratch_shapes=[pltpu.VMEM((4, B, B), F32)],
        compiler_params=params(8),
        cost_estimate=cost(8 * B * B, 1 << 19),
        name="add_z",
    )(me, *parts)


def pair_kernel(a, b, after, out):
    out[...] = a[...] + b[...]


def pair_call(a, b, after):
    return pl.pallas_call(
        pair_kernel,
        out_shape=jax.ShapeDtypeStruct((B, B), F32),
        in_specs=[VMEM] * 2 + [ANY],
        out_specs=VMEM,
        compiler_params=params(8),
        cost_estimate=cost(B * B, 1 << 18),
        name="add_pair",
    )(a, b, after)


def relay_kernel(p1, p3, low, high, after, out1, out3):
    half = 2048
    out1[:half, :] = (p1[:half, :].astype(F32) + low[...].astype(F32)).astype(BF16)
    out1[half:, :] = p1[half:, :]
    out3[:half, :] = p3[:half, :]
    out3[half:, :] = (p3[half:, :].astype(F32) + high[...].astype(F32)).astype(BF16)


def relay_call(p1, p3, low, high, after):
    return pl.pallas_call(
        relay_kernel,
        out_shape=[jax.ShapeDtypeStruct((4096, B), BF16)] * 2,
        in_specs=[VMEM] * 4 + [ANY],
        out_specs=[VMEM] * 2,
        compiler_params=params(16),
        cost_estimate=cost(4096 * B, 6 << 20),
        name="relay",
    )(p1, p3, low, high, after)


def parts_kernel(p0, q1, q3, after, ig_hbm, p, ig, sems, out_sems):
    rows = [pl.ds(k * 1024, 1024) for k in range(4)]
    ins = [
        [pltpu.make_async_copy(v.at[r], p.at[s, r], sems.at[3 * k + s]) for s, v in enumerate((p0, q1, q3))]
        for k, r in enumerate(rows)
    ]
    for group in ins:
        for c in group:
            c.start()
    outs = []
    for k, r in enumerate(rows):
        for c in ins[k]:
            c.wait()
        v = p[0, r, :].astype(F32) + (p[1, r, :].astype(F32) + p[2, r, :].astype(F32))
        ig[r, :] = v.astype(BF16)
        outs.append(pltpu.make_async_copy(ig.at[r], ig_hbm.at[r], out_sems.at[k]))
        outs[-1].start()
    for c in outs:
        c.wait()


def parts_call(parts, after):
    return pl.pallas_call(
        parts_kernel,
        out_shape=jax.ShapeDtypeStruct((4096, B), BF16),
        in_specs=[ANY] * 4,
        out_specs=HBM,
        scratch_shapes=[
            pltpu.VMEM((3, 4096, B), BF16),
            pltpu.VMEM((4096, B), BF16),
            pltpu.SemaphoreType.DMA((12,)),
            pltpu.SemaphoreType.DMA((4,)),
        ],
        compiler_params=params(16),
        cost_estimate=cost(4096 * B * 4, 6 << 20),
        name="add_parts",
    )(*parts, after)


def finish_kernel(me_ref, t0, t1, t2, t3, out):
    for k, t in enumerate((t0, t1, t2, t3)):
        out[pl.ds(pl.multiple_of(rel(me_ref[1], -k) * B, B), B), :] = t[...]


def finish_call(me, totals):
    return pl.pallas_call(
        finish_kernel,
        out_shape=jax.ShapeDtypeStruct((512, B), F32),
        in_specs=[SMEM] + [VMEM] * 4,
        out_specs=VMEM,
        compiler_params=params(8),
        cost_estimate=cost(512 * B, 1 << 19),
        name="finish",
    )(me, *totals)


def shift_hid(v, s):
    return lax.ppermute(v, "hid", [(i, (i + s) % HID) for i in range(HID)])


def split_kernel(v1, v3, after, low, high):
    low[...] = v1[...]
    high[...] = v3[...]


def split_call(v1, v3, after):
    half = jax.ShapeDtypeStruct((2048, B), BF16)
    return pl.pallas_call(
        split_kernel,
        out_shape=[half] * 2,
        grid=(1,),
        in_specs=[
            pl.BlockSpec((2048, B), lambda i: (0, 0)),
            pl.BlockSpec((2048, B), lambda i: (1, 0)),
            ANY,
        ],
        out_specs=[pl.BlockSpec((2048, B), lambda i: (0, 0))] * 2,
        compiler_params=params(12),
        cost_estimate=cost(1000, 2 << 20),
        name="halves",
    )(v1, v3, after)


def gather_hid(v, after):
    v1, v3 = shift_hid(v, 1), shift_hid(v, 3)
    low, high = split_call(v1, v3, after)
    return v, v1, shift_hid(low, 1), shift_hid(high, 3), v3


def shift_dom(v, dz, dy, dc):
    pairs = [
        ((z * 4 + y) * 2 + c, (((z + dz) % 8) * 4 + (y + dy) % 4) * 2 + (c ^ dc))
        for z in range(8)
        for y in range(4)
        for c in range(2)
    ]
    return lax.ppermute(v, "dom", pairs)


def swap_z(v):
    return lax.ppermute(v, "dom", [(i, i ^ 8) for i in range(64)])


def all_to_all(v):
    return lax.all_to_all(v, "dom", split_axis=0, concat_axis=0, tiled=True)


def per_device(x, w, tiles, rows, cols, count, send, bits, cot):
    hid = lax.axis_index("hid").astype(jnp.int32)
    dom = lax.axis_index("dom").astype(jnp.int32)
    z, y = dom // 8, (dom // 2) % 4
    me = jnp.stack([hid, y, z])
    bits_t = bits.T

    own, slots = tiles_bwd_call(count, rows, cols, bits_t, cot, tiles)
    returned = all_to_all(slots)

    xs = gather_hid(x, slots)
    hidden, outgoing = hidden_call(me, send, xs, w)
    incoming = all_to_all(outgoing)

    terms, p0, p1, p2a, p2b, p3 = sum_call(me, send, own, returned, xs, w, outgoing)

    terms = (terms + shift_dom(terms, 0, 0, 1)).reshape(4, B, B)
    terms = [terms[0]] + [shift_dom(terms[k], 0, k, 0) for k in (1, 3, 2)]
    part = add_call(terms)

    p1, p3 = relay_call(p1, p3, shift_hid(p2a, 1), shift_hid(p2b, 3), part)
    parts = [p0, shift_hid(p1, 1), shift_hid(p3, 3)]

    total = add_z_call(me, [part] + [shift_dom(part, k, 0, 0) for k in (2, 4, 6)])
    out_act, token = tiles_fwd_call(count, rows, cols, bits_t, hidden, incoming, tiles)
    total = pair_call(total, swap_z(total), token)
    weight_grad = finish_call(me, [total] + [shift_dom(total, 0, k, 0) for k in range(1, 4)])
    input_grad = parts_call(parts, token)
    return out_act.reshape(4096, B), input_grad, weight_grad


def solution(mesh):
    placed = (
        P("dom", "hid"),
        P(None, "hid"),
        P("dom", None, None),
        P("dom", None),
        P("dom", None),
        P("dom"),
        P("dom", None),
        P("dom", "hid"),
        P("dom", "hid"),
    )
    return jax.shard_map(
        per_device,
        mesh=mesh,
        in_specs=placed,
        out_specs=(P("dom", "hid"), P("dom", "hid"), P(None, "hid")),
        check_vma=False,
    )
```

time: 185 us -> 158 us (0.85)
  Pallas kernels: 51.3 us -> 35.5 us
  starting transfers between devices: 61.7 us -> 52.3 us
  local copies, waits for them, and re-layouts: 10.7 us -> 4.65 us
  waiting for transfers between devices: 56.6 us -> 62.2 us
    pallas_call x3 -> x5, Pallas kernels: 18.2 us -> 11.6 us  [the longest x1 7.68 us: tiles_fwd_call(): pl.pallas_call(tiles_fwd_kernel, out_shape=[jax.ShapeDtypeStruct((RB, B,...]
    ppermute x14 -> x10, waiting for transfers between devices: 17.4 us -> 22.8 us  [shift_dom(): return lax.ppermute(v, 'dom', pairs)]
    ppermute x11 -> x8, starting transfers between devices: 15.4 us -> 10.1 us  [shift_hid(): return lax.ppermute(v, 'hid', [(i, (i + s) % HID) for i in range(HID)])]
    pallas_call x1, Pallas kernels: 13.2 us -> 8.31 us  [tiles_bwd_call(): pl.pallas_call(tiles_bwd_kernel, out_shape=[jax.ShapeDtypeStruct((RB, B,...]
    unnamed x54 -> x24, local copies, waits for them, and re-layouts: 9.45 us -> 4.63 us
    ppermute x14 -> x10, starting transfers between devices: 23.1 us -> 18.4 us  [shift_dom(): return lax.ppermute(v, 'dom', pairs)]
    pallas_call x2 -> x1, Pallas kernels: 4.5 us -> 0.07 us  [split_call(): pl.pallas_call(split_kernel, out_shape=[half] * 2, grid=(1,), in_specs=[p...]
    pallas_call x1, Pallas kernels: 6.53 us -> 9.15 us  [sum_call(): pl.pallas_call(sum_kernel, out_shape=[jax.ShapeDtypeStruct((512, B), F32)...]
  transfers between devices with their start and end apart: 27 -> 21, of which waited for: 11 -> 13; matrix products, arithmetic and copies ran while one was open for 2% -> 1% of each run, Pallas kernels for 18% -> 16%
where the time goes in v2:
time: 158 us
  waiting for transfers between devices  62.2 us (39%)
  starting transfers between devices  52.3 us (33%)
  Pallas kernels  35.5 us (22%)
  local copies, waits for them, and re-layouts  4.65 us (3%)
  other arithmetic  1.63 us (1%)
    ppermute x8, waiting for transfers between devices, shift_hid(): return lax.ppermute(v, 'hid', [(i, (i + s) % HID) for i in range(HID)])  38.7 us
    ppermute x10, waiting for transfers between devices, shift_dom(): return lax.ppermute(v, 'dom', pairs)  22.8 us
    all_to_all x2, starting transfers between devices, all_to_all(): return lax.all_to_all(v, 'dom', split_axis=0, concat_axis=0, tiled=True)  22.8 us
    ppermute x10, starting transfers between devices, shift_dom(): return lax.ppermute(v, 'dom', pairs)  18.4 us
    ppermute x8, starting transfers between devices, shift_hid(): return lax.ppermute(v, 'hid', [(i, (i + s) % HID) for i in range(HID)])  10.1 us
    pallas_call x1, Pallas kernels, sum_call(): pl.pallas_call(sum_kernel, out_shape=[jax.ShapeDtypeStruct((512, B), F32)...  9.15 us
    pallas_call x1, Pallas kernels, tiles_bwd_call(): pl.pallas_call(tiles_bwd_kernel, out_shape=[jax.ShapeDtypeStruct((RB, B,...  8.31 us
    pallas_call x1, Pallas kernels, tiles_fwd_call(): pl.pallas_call(tiles_fwd_kernel, out_shape=[jax.ShapeDtypeStruct((RB, B,...  7.68 us
  transfers between devices with their start and end apart: 21, of which 13 were waited for; matrix products, arithmetic and copies ran while one was open for 1% of the time, Pallas kernels for 16%

profile of v2, /device:TPU:6, one launch (start us, length us, event | category | flops | bytes accessed | tf_op | source)
XLA Modules:
  0.0 157.8 jit_solution(5427534810109971429)
XLA Ops:
  1.3 8.3 %tiles_bwd.1 = (f32[32,128,128]{2,1,0:T(8,128)}, bf16[64,128,128]{2,1,0:T(8,128)(2,1)}) custom-call(s32[1]{0:T(128)S(6)} %copy.12.count_ref, s32[1,176]{1,0:T(1,128)} %rows_ref.3, s32[1,176]{1,0:T(1,128)} %cols_ref.3, s32[8,4096]{1,0:T(8,128)} %bitcast.5, bf16[4096,128]{1,0:T(8,128)(2,1)} %cot_hbm.1, bf16[176,128,128]{2,1,0:T(8,128)(2,1)} %tiles_hbm.3), custom_call_target="tpu_custom_call" | custom-call | flops 738197504 | bytes 31457280 | tf_op jit(solution)/shard_map/tiles_bwd/pallas_call | solution.py:109
  9.6 12.6 %all-to-all-start.1 = ((bf16[64,128,128]{2,1,0:T(8,128)(2,1)}), bf16[64,128,128]{2,1,0:T(8,128)(2,1)}, u32[]{:S(2)}, u32[]{:S(2)}) async-start(bf16[64,128,128]{2,1,0:T(8,128)(2,1)} %get-tuple-element.19.after), calls=%async_computation.1 | async-start | bytes 4194304 | tf_op jit(solution)/shard_map/all_to_all | solution.py:491
  22.3 0.9 collective-permute-start.1
  23.2 2.4 %collective-permute-start = (bf16[4096,128]{1,0:T(8,128)(2,1)S(1)}, bf16[4096,128]{1,0:T(8,128)(2,1)S(1)}, u32[]{:S(2)}, u32[]{:S(2)}) collective-permute-start(bf16[4096,128]{1,0:T(8,128)(2,1)S(1)} %copy-done.9), channel_id=1, source_target_pairs={{0,1},{1,2},{2,3},{3,0},{4,5},{5,6},{6,7},{7,4},{8,9},{9,10},{10,1... | collective-permute-start | bytes 3145736 | tf_op jit(solution)/shard_map/ppermute | solution.py:444
  25.6 23.0 %collective-permute-done.1.v3.x3 = bf16[4096,128]{1,0:T(8,128)(2,1)S(1)} collective-permute-done((bf16[4096,128]{1,0:T(8,128)(2,1)S(1)}, bf16[4096,128]{1,0:T(8,128)(2,1)S(1)}, u32[]{:S(2)}, u32[]{:S(2)}) %collective-permute-start.1) | collective-permute-done | bytes 1048608 | tf_op jit(solution)/shard_map/ppermute | solution.py:444
  48.7 0.9 copy-done
  49.6 0.3 copy-done.1
  49.9 2.6 %collective-permute-start.2 = (bf16[2048,128]{1,0:T(8,128)(2,1)S(1)}, bf16[2048,128]{1,0:T(8,128)(2,1)S(1)}, u32[]{:S(2)}, u32[]{:S(2)}) collective-permute-start(bf16[2048,128]{1,0:T(8,128)(2,1)S(1)} %get-tuple-element.20), channel_id=1, source_target_pairs={{0,1},{1,2},{2,3},{3,0},{4,5},{5,6},{6,7},{7,4},{8,9},{9,10},{10,1... | collective-permute-start | bytes 1572872 | tf_op jit(solution)/shard_map/ppermute | solution.py:444
  52.5 0.6 pad_add_fusion.me_ref
  53.2 9.8 %collective-permute-done.2.x2a = bf16[2048,128]{1,0:T(8,128)(2,1)S(1)} collective-permute-done((bf16[2048,128]{1,0:T(8,128)(2,1)S(1)}, bf16[2048,128]{1,0:T(8,128)(2,1)S(1)}, u32[]{:S(2)}, u32[]{:S(2)}) %collective-permute-start.2) | collective-permute-done | bytes 524320 | tf_op jit(solution)/shard_map/ppermute | solution.py:444
  63.0 3.2 %collective-permute-done.3.x2b = bf16[2048,128]{1,0:T(8,128)(2,1)S(1)} collective-permute-done((bf16[2048,128]{1,0:T(8,128)(2,1)S(1)}, bf16[2048,128]{1,0:T(8,128)(2,1)S(1)}, u32[]{:S(2)}, u32[]{:S(2)}) %collective-permute-start.3) | collective-permute-done | bytes 524320 | tf_op jit(solution)/shard_map/ppermute | solution.py:444
  66.2 0.8 copy-done.11
  67.0 5.8 %hidden.1 = (bf16[32,128,128]{2,1,0:T(8,128)(2,1)}, bf16[64,128,128]{2,1,0:T(8,128)(2,1)}) custom-call(s32[3]{0:T(128)} %pad_add_fusion.me_ref, s32[1,64]{1,0:T(1,128)} %send_ref.3, bf16[4096,128]{1,0:T(8,128)(2,1)} %x0.3, bf16[4096,128]{1,0:T(8,128)(2,1)} %copy-done.1, bf16[2048,128]{1,0:T(8,128)(2,1)} %copy-done.10, bf16[2048,128]{1,0:T(8,128)(2,1)} %copy-done.11, ...), custom_call_target="tpu_custom_call" | custom-call | flops 536870912 | bytes 10485760 | tf_op jit(solution)/shard_map/hidden/pallas_call | solution.py:211
  72.8 0.7 all-to-all-done.1.got_hbm
  73.4 10.2 %all-to-all-start = ((bf16[64,128,128]{2,1,0:T(8,128)(2,1)}), bf16[64,128,128]{2,1,0:T(8,128)(2,1)}, u32[]{:S(2)}, u32[]{:S(2)}) async-start(bf16[64,128,128]{2,1,0:T(8,128)(2,1)} %get-tuple-element.23.after), calls=%async_computation | async-start | bytes 4194304 | tf_op jit(solution)/shard_map/all_to_all | solution.py:491
  83.6 9.2 %sum_returned.1 = (f32[512,128]{1,0:T(8,128)}, bf16[4096,128]{1,0:T(8,128)(2,1)}, bf16[4096,128]{1,0:T(8,128)(2,1)}, bf16[2048,128]{1,0:T(8,128)(2,1)}, bf16[204...) custom-call(s32[3]{0:T(128)} %pad_add_fusion.me_ref, s32[1,64]{1,0:T(1,128)} %send_ref.3, ...), custom_call_target="tpu_custom_call" | custom-call | flops 536870912 | bytes 12582912 | tf_op jit(solution)/shard_map/sum_returned/pallas_call | solution.py:292
  93.1 1.2 collective-permute-start.4
  94.3 0.9 collective-permute-start.5
  95.2 1.0 add.10
  96.2 3.2 %collective-permute-start.9 = (f32[128,128]{1,0:T(8,128)S(1)}, f32[128,128]{1,0:T(8,128)S(1)}, u32[]{:S(2)}, u32[]{:S(2)}) collective-permute-start(f32[128,128]{1,0:T(8,128)S(1)} %get-tuple-element.35), channel_id=1, source_target_pairs={{0,16},{4,20},{8,24},{12,28},{16,0},{20,4},{24,8},{28,12},{32,48},... | collective-permute-start | bytes 196616 | tf_op jit(solution)/shard_map/ppermute | solution.py:483
  99.4 1.2 collective-permute-start.8
  100.6 0.9 collective-permute-start.7
  101.4 2.1 %collective-permute-done.9.d = f32[128,128]{1,0:T(8,128)S(1)} collective-permute-done((f32[128,128]{1,0:T(8,128)S(1)}, f32[128,128]{1,0:T(8,128)S(1)}, u32[]{:S(2)}, u32[]{:S(2)}) %collective-permute-start.9) | collective-permute-done | bytes 65568 | tf_op jit(solution)/shard_map/ppermute | solution.py:483
  103.5 2.1 %collective-permute-done.8.c = f32[128,128]{1,0:T(8,128)S(1)} collective-permute-done((f32[128,128]{1,0:T(8,128)S(1)}, f32[128,128]{1,0:T(8,128)S(1)}, u32[]{:S(2)}, u32[]{:S(2)}) %collective-permute-start.8) | collective-permute-done | bytes 65568 | tf_op jit(solution)/shard_map/ppermute | solution.py:483
  105.6 1.4 collective-permute-done.7.b
  107.0 0.6 collective-permute-done.4.low
  107.6 2.0 %collective-permute-done.5.high = bf16[2048,128]{1,0:T(8,128)(2,1)S(1)} collective-permute-done((bf16[2048,128]{1,0:T(8,128)(2,1)}, bf16[2048,128]{1,0:T(8,128)(2,1)S(1)}, u32[]{:S(2)}, u32[]{:S(2)}) %collective-permute-start.5) | collective-permute-done | bytes 524320 | tf_op jit(solution)/shard_map/ppermute | solution.py:444
  109.7 1.2 copy-done.5
  110.9 1.2 relay.1
  112.1 0.3 collective-permute-start.10
  112.4 1.7 %collective-permute-start.11 = (bf16[4096,128]{1,0:T(8,128)(2,1)S(1)}, bf16[4096,128]{1,0:T(8,128)(2,1)S(1)}, u32[]{:S(2)}, u32[]{:S(2)}) collective-permute-start(bf16[4096,128]{1,0:T(8,128)(2,1)S(1)} %get-tuple-element.33), channel_id=1, source_target_pairs={{0,3},{1,0},{2,1},{3,2},{4,7},{5,4},{6,5},{7,6},{8,11},{9,8},{10,9... | collective-permute-start | bytes 3145736 | tf_op jit(solution)/shard_map/ppermute | solution.py:444
  114.1 3.8 %collective-permute-start.14 = (bf16[128,128]{1,0:T(8,128)(2,1)S(1)}, bf16[128,128]{1,0:T(8,128)(2,1)S(1)}, u32[]{:S(2)}, u32[]{:S(2)}) collective-permute-start(bf16[128,128]{1,0:T(8,128)(2,1)S(1)} %add_y.1.after.p0), channel_id=1, source_target_pairs={{0,192},{4,196},{8,200},{12,204},{16,208},{20,212},{24,216},{28,22... | collective-permute-start | bytes 98312 | tf_op jit(solution)/shard_map/ppermute | solution.py:483
  117.9 2.2 %collective-permute-start.13 = (bf16[128,128]{1,0:T(8,128)(2,1)S(1)}, bf16[128,128]{1,0:T(8,128)(2,1)S(1)}, u32[]{:S(2)}, u32[]{:S(2)}) collective-permute-start(bf16[128,128]{1,0:T(8,128)(2,1)S(1)} %add_y.1.after.p0), channel_id=1, source_target_pairs={{0,128},{4,132},{8,136},{12,140},{16,144},{20,148},{24,152},{28,15... | collective-permute-start | bytes 98312 | tf_op jit(solution)/shard_map/ppermute | solution.py:483
  120.1 2.5 %collective-permute-start.12 = (bf16[128,128]{1,0:T(8,128)(2,1)S(1)}, bf16[128,128]{1,0:T(8,128)(2,1)S(1)}, u32[]{:S(2)}, u32[]{:S(2)}) collective-permute-start(bf16[128,128]{1,0:T(8,128)(2,1)S(1)} %add_y.1.after.p0), channel_id=1, source_target_pairs={{0,64},{4,68},{8,72},{12,76},{16,80},{20,84},{24,88},{28,92},{32,9... | collective-permute-start | bytes 98312 | tf_op jit(solution)/shard_map/ppermute | solution.py:483
  122.5 9.7 %collective-permute-done.14.p3 = bf16[128,128]{1,0:T(8,128)(2,1)S(1)} collective-permute-done((bf16[128,128]{1,0:T(8,128)(2,1)S(1)}, bf16[128,128]{1,0:T(8,128)(2,1)S(1)}, u32[]{:S(2)}, u32[]{:S(2)}) %collective-permute-start.14) | collective-permute-done | bytes 32800 | tf_op jit(solution)/shard_map/ppermute | solution.py:483
  132.3 4.9 %collective-permute-done.13.p2 = bf16[128,128]{1,0:T(8,128)(2,1)S(1)} collective-permute-done((bf16[128,128]{1,0:T(8,128)(2,1)S(1)}, bf16[128,128]{1,0:T(8,128)(2,1)S(1)}, u32[]{:S(2)}, u32[]{:S(2)}) %collective-permute-start.13) | collective-permute-done | bytes 32800 | tf_op jit(solution)/shard_map/ppermute | solution.py:483
  137.2 0.6 add_z.1.a
  137.8 1.1 collective-permute-start.15
  138.9 7.7 %tiles_fwd.1 = (bf16[32,128,128]{2,1,0:T(8,128)(2,1)}, f32[8,128]{1,0:T(8,128)}) custom-call(s32[1]{0:T(128)S(6)} %copy.12.count_ref, s32[1,176]{1,0:T(1,128)} %rows_ref.3, s32[1,176]{1,0:T(1,128)} %cols_ref.3, s32[8,4096]{1,0:T(8,128)} %bitcast.6, bf16[32,128,128]{2,1,0:T(8,128)(2,1)} %get-tuple-element.22.own_hbm, ...), custom_call_target="tpu_custom_call" | custom-call | flops 738197504 | bytes 31457280 | tf_op jit(solution)/shard_map/tiles_fwd/pallas_call | solution.py:170
  146.6 0.7 copy-done.6
  147.3 2.8 %collective-permute-start.18 = (f32[128,128]{1,0:T(8,128)S(1)}, f32[128,128]{1,0:T(8,128)S(1)}, u32[]{:S(2)}, u32[]{:S(2)}) collective-permute-start(f32[128,128]{1,0:T(8,128)S(1)} %add_pair.1.t0), channel_id=1, source_target_pairs={{0,24},{4,28},{8,0},{12,4},{16,8},{20,12},{24,16},{28,20},{32,56},... | collective-permute-start | bytes 196616 | tf_op jit(solution)/shard_map/ppermute | solution.py:483
  150.0 0.8 collective-permute-start.17
  150.9 0.9 collective-permute-start.16
  151.8 0.7 copy-done.7
  152.5 1.5 add_parts.1
  153.9 1.9 %collective-permute-done.17.t2 = f32[128,128]{1,0:T(8,128)S(1)} collective-permute-done((f32[128,128]{1,0:T(8,128)S(1)}, f32[128,128]{1,0:T(8,128)S(1)}, u32[]{:S(2)}, u32[]{:S(2)}) %collective-permute-start.17) | collective-permute-done | bytes 65568 | tf_op jit(solution)/shard_map/ppermute | solution.py:483
  155.8 0.7 collective-permute-done.16.t1
  156.5 1.3 finish.1
  (32 shorter events, 0.5 us)
Async XLA Ops:
  9.6 12.7 %copy-start.9 = (bf16[4096,128]{1,0:T(8,128)(2,1)S(1)}, bf16[4096,128]{1,0:T(8,128)(2,1)}, u32[]{:S(2)}) copy-start(bf16[4096,128]{1,0:T(8,128)(2,1)} %x0.3) | copy-start | bytes 3145732
  9.6 39.0 %copy-start.2 = (bf16[64,128,128]{2,1,0:T(8,128)(2,1)S(1)}, bf16[64,128,128]{2,1,0:T(8,128)(2,1)}, u32[]{:S(2)}) copy-start(bf16[64,128,128]{2,1,0:T(8,128)(2,1)} %get-tuple-element.19.after) | copy-start | bytes 6291460
  9.6 63.8 %all-to-all-start.1 = ((bf16[64,128,128]{2,1,0:T(8,128)(2,1)}), bf16[64,128,128]{2,1,0:T(8,128)(2,1)}, u32[]{:S(2)}, u32[]{:S(2)}) async-start(bf16[64,128,128]{2,1,0:T(8,128)(2,1)} %get-tuple-element.19.after), calls=%async_computation.1 | async-start | bytes 4194304 | tf_op jit(solution)/shard_map/all_to_all | solution.py:491
  22.3 26.3 %collective-permute-start.1 = (bf16[4096,128]{1,0:T(8,128)(2,1)S(1)}, bf16[4096,128]{1,0:T(8,128)(2,1)S(1)}, u32[]{:S(2)}, u32[]{:S(2)}) collective-permute-start(bf16[4096,128]{1,0:T(8,128)(2,1)S(1)} %copy-done.9), channel_id=1, source_target_pairs={{0,3},{1,0},{2,1},{3,2},{4,7},{5,4},{6,5},{7,6},{8,11},{9,8},{10,9... | collective-permute-start | bytes 3145736 | tf_op jit(solution)/shard_map/ppermute | solution.py:444
  23.2 25.4 %collective-permute-start = (bf16[4096,128]{1,0:T(8,128)(2,1)S(1)}, bf16[4096,128]{1,0:T(8,128)(2,1)S(1)}, u32[]{:S(2)}, u32[]{:S(2)}) collective-permute-start(bf16[4096,128]{1,0:T(8,128)(2,1)S(1)} %copy-done.9), channel_id=1, source_target_pairs={{0,1},{1,2},{2,3},{3,0},{4,5},{5,6},{6,7},{7,4},{8,9},{9,10},{10,1... | collective-permute-start | bytes 3145736 | tf_op jit(solution)/shard_map/ppermute | solution.py:444
  48.6 1.0 copy-start
  48.6 1.3 copy-start.1
  49.9 13.1 %collective-permute-start.2 = (bf16[2048,128]{1,0:T(8,128)(2,1)S(1)}, bf16[2048,128]{1,0:T(8,128)(2,1)S(1)}, u32[]{:S(2)}, u32[]{:S(2)}) collective-permute-start(bf16[2048,128]{1,0:T(8,128)(2,1)S(1)} %get-tuple-element.20), channel_id=1, source_target_pairs={{0,1},{1,2},{2,3},{3,0},{4,5},{5,6},{6,7},{7,4},{8,9},{9,10},{10,1... | collective-permute-start | bytes 1572872 | tf_op jit(solution)/shard_map/ppermute | solution.py:444
  52.5 13.7 %collective-permute-start.3 = (bf16[2048,128]{1,0:T(8,128)(2,1)S(1)}, bf16[2048,128]{1,0:T(8,128)(2,1)S(1)}, u32[]{:S(2)}, u32[]{:S(2)}) collective-permute-start(bf16[2048,128]{1,0:T(8,128)(2,1)S(1)} %get-tuple-element.21), channel_id=1, source_target_pairs={{0,3},{1,0},{2,1},{3,2},{4,7},{5,4},{6,5},{7,6},{8,11},{9,8},{10,9... | collective-permute-start | bytes 1572872 | tf_op jit(solution)/shard_map/ppermute | solution.py:444
  63.0 3.2 %copy-start.10 = (bf16[2048,128]{1,0:T(8,128)(2,1)}, bf16[2048,128]{1,0:T(8,128)(2,1)S(1)}, u32[]{:S(2)}) copy-start(bf16[2048,128]{1,0:T(8,128)(2,1)S(1)} %collective-permute-done.2.x2a) | copy-start | bytes 1572868
  66.2 0.8 copy-start.11
  73.4 65.4 %all-to-all-start = ((bf16[64,128,128]{2,1,0:T(8,128)(2,1)}), bf16[64,128,128]{2,1,0:T(8,128)(2,1)}, u32[]{:S(2)}, u32[]{:S(2)}) async-start(bf16[64,128,128]{2,1,0:T(8,128)(2,1)} %get-tuple-element.23.after), calls=%async_computation | async-start | bytes 4194304 | tf_op jit(solution)/shard_map/all_to_all | solution.py:491
  92.8 16.9 %copy-start.4 = (bf16[4096,128]{1,0:T(8,128)(2,1)S(1)}, bf16[4096,128]{1,0:T(8,128)(2,1)}, u32[]{:S(2)}) copy-start(bf16[4096,128]{1,0:T(8,128)(2,1)} %get-tuple-element.27.p1) | copy-start | bytes 3145732
  92.8 2.4 %collective-permute-start.6 = (f32[512,128]{1,0:T(8,128)}, f32[512,128]{1,0:T(8,128)S(1)}, u32[]{:S(2)}, u32[]{:S(2)}) collective-permute-start(f32[512,128]{1,0:T(8,128)} %get-tuple-element.31), channel_id=1, source_target_pairs={{0,4},{4,0},{8,12},{12,8},{16,20},{20,16},{24,28},{28,24},{32,36},... | collective-permute-start | bytes 786440 | tf_op jit(solution)/shard_map/ppermute | solution.py:483
  93.1 14.6 %collective-permute-start.4 = (bf16[2048,128]{1,0:T(8,128)(2,1)}, bf16[2048,128]{1,0:T(8,128)(2,1)S(1)}, u32[]{:S(2)}, u32[]{:S(2)}) collective-permute-start(bf16[2048,128]{1,0:T(8,128)(2,1)} %get-tuple-element.29), channel_id=1, source_target_pairs={{0,1},{1,2},{2,3},{3,0},{4,5},{5,6},{6,7},{7,4},{8,9},{9,10},{10,1... | collective-permute-start | bytes 1572872 | tf_op jit(solution)/shard_map/ppermute | solution.py:444
  94.3 15.4 %collective-permute-start.5 = (bf16[2048,128]{1,0:T(8,128)(2,1)}, bf16[2048,128]{1,0:T(8,128)(2,1)S(1)}, u32[]{:S(2)}, u32[]{:S(2)}) collective-permute-start(bf16[2048,128]{1,0:T(8,128)(2,1)} %get-tuple-element.30), channel_id=1, source_target_pairs={{0,3},{1,0},{2,1},{3,2},{4,7},{5,4},{6,5},{7,6},{8,11},{9,8},{10,9... | collective-permute-start | bytes 1572872 | tf_op jit(solution)/shard_map/ppermute | solution.py:444
  96.2 41.0 %copy-start.8 = (s32[3]{0:T(128)S(1)}, s32[3]{0:T(128)}, u32[]{:S(2)}) copy-start(s32[3]{0:T(128)} %pad_add_fusion.me_ref) | copy-start | bytes 40
  96.2 7.3 %collective-permute-start.9 = (f32[128,128]{1,0:T(8,128)S(1)}, f32[128,128]{1,0:T(8,128)S(1)}, u32[]{:S(2)}, u32[]{:S(2)}) collective-permute-start(f32[128,128]{1,0:T(8,128)S(1)} %get-tuple-element.35), channel_id=1, source_target_pairs={{0,16},{4,20},{8,24},{12,28},{16,0},{20,4},{24,8},{28,12},{32,48},... | collective-permute-start | bytes 196616 | tf_op jit(solution)/shard_map/ppermute | solution.py:483
  99.4 6.2 %collective-permute-start.8 = (f32[128,128]{1,0:T(8,128)S(1)}, f32[128,128]{1,0:T(8,128)S(1)}, u32[]{:S(2)}, u32[]{:S(2)}) collective-permute-start(f32[128,128]{1,0:T(8,128)S(1)} %get-tuple-element.36), channel_id=1, source_target_pairs={{0,24},{4,28},{8,0},{12,4},{16,8},{20,12},{24,16},{28,20},{32,56},... | collective-permute-start | bytes 196616 | tf_op jit(solution)/shard_map/ppermute | solution.py:483
  100.6 6.5 %collective-permute-start.7 = (f32[128,128]{1,0:T(8,128)S(1)}, f32[128,128]{1,0:T(8,128)S(1)}, u32[]{:S(2)}, u32[]{:S(2)}) collective-permute-start(f32[128,128]{1,0:T(8,128)S(1)} %get-tuple-element.37), channel_id=1, source_target_pairs={{0,8},{4,12},{8,16},{12,20},{16,24},{20,28},{24,0},{28,4},{32,40},... | collective-permute-start | bytes 196616 | tf_op jit(solution)/shard_map/ppermute | solution.py:483
  109.7 1.2 copy-start.5
  112.1 39.7 %collective-permute-start.10 = (bf16[4096,128]{1,0:T(8,128)(2,1)}, bf16[4096,128]{1,0:T(8,128)(2,1)S(1)}, u32[]{:S(2)}, u32[]{:S(2)}) collective-permute-start(bf16[4096,128]{1,0:T(8,128)(2,1)} %get-tuple-element.32), channel_id=1, source_target_pairs={{0,1},{1,2},{2,3},{3,0},{4,5},{5,6},{6,7},{7,4},{8,9},{9,10},{10,1... | collective-permute-start | bytes 3145736 | tf_op jit(solution)/shard_map/ppermute | solution.py:444
  112.4 39.4 %collective-permute-start.11 = (bf16[4096,128]{1,0:T(8,128)(2,1)S(1)}, bf16[4096,128]{1,0:T(8,128)(2,1)S(1)}, u32[]{:S(2)}, u32[]{:S(2)}) collective-permute-start(bf16[4096,128]{1,0:T(8,128)(2,1)S(1)} %get-tuple-element.33), channel_id=1, source_target_pairs={{0,3},{1,0},{2,1},{3,2},{4,7},{5,4},{6,5},{7,6},{8,11},{9,8},{10,9... | collective-permute-start | bytes 3145736 | tf_op jit(solution)/shard_map/ppermute | solution.py:444
  114.1 18.1 %collective-permute-start.14 = (bf16[128,128]{1,0:T(8,128)(2,1)S(1)}, bf16[128,128]{1,0:T(8,128)(2,1)S(1)}, u32[]{:S(2)}, u32[]{:S(2)}) collective-permute-start(bf16[128,128]{1,0:T(8,128)(2,1)S(1)} %add_y.1.after.p0), channel_id=1, source_target_pairs={{0,192},{4,196},{8,200},{12,204},{16,208},{20,212},{24,216},{28,22... | collective-permute-start | bytes 98312 | tf_op jit(solution)/shard_map/ppermute | solution.py:483
  117.9 19.3 %collective-permute-start.13 = (bf16[128,128]{1,0:T(8,128)(2,1)S(1)}, bf16[128,128]{1,0:T(8,128)(2,1)S(1)}, u32[]{:S(2)}, u32[]{:S(2)}) collective-permute-start(bf16[128,128]{1,0:T(8,128)(2,1)S(1)} %add_y.1.after.p0), channel_id=1, source_target_pairs={{0,128},{4,132},{8,136},{12,140},{16,144},{20,148},{24,152},{28,15... | collective-permute-start | bytes 98312 | tf_op jit(solution)/shard_map/ppermute | solution.py:483
  120.1 17.1 %collective-permute-start.12 = (bf16[128,128]{1,0:T(8,128)(2,1)S(1)}, bf16[128,128]{1,0:T(8,128)(2,1)S(1)}, u32[]{:S(2)}, u32[]{:S(2)}) collective-permute-start(bf16[128,128]{1,0:T(8,128)(2,1)S(1)} %add_y.1.after.p0), channel_id=1, source_target_pairs={{0,64},{4,68},{8,72},{12,76},{16,80},{20,84},{24,88},{28,92},{32,9... | collective-permute-start | bytes 98312 | tf_op jit(solution)/shard_map/ppermute | solution.py:483
  137.8 8.8 %collective-permute-start.15 = (f32[128,128]{1,0:T(8,128)S(1)}, f32[128,128]{1,0:T(8,128)S(1)}, u32[]{:S(2)}, u32[]{:S(2)}) collective-permute-start(f32[128,128]{1,0:T(8,128)S(1)} %add_z.1.a), channel_id=1, source_target_pairs={{0,32},{4,36},{8,40},{12,44},{16,48},{20,52},{24,56},{28,60},{32,0... | collective-permute-start | bytes 196616 | tf_op jit(solution)/shard_map/ppermute | solution.py:487
  138.9 12.9 %copy-start.3 = (bf16[4096,128]{1,0:T(8,128)(2,1)S(1)}, bf16[4096,128]{1,0:T(8,128)(2,1)}, u32[]{:S(2)}) copy-start(bf16[4096,128]{1,0:T(8,128)(2,1)} %get-tuple-element.26.p0) | copy-start | bytes 3145732
  146.6 0.7 copy-start.6
  147.3 6.7 %collective-permute-start.18 = (f32[128,128]{1,0:T(8,128)S(1)}, f32[128,128]{1,0:T(8,128)S(1)}, u32[]{:S(2)}, u32[]{:S(2)}) collective-permute-start(f32[128,128]{1,0:T(8,128)S(1)} %add_pair.1.t0), channel_id=1, source_target_pairs={{0,24},{4,28},{8,0},{12,4},{16,8},{20,12},{24,16},{28,20},{32,56},... | collective-permute-start | bytes 196616 | tf_op jit(solution)/shard_map/ppermute | solution.py:483
  150.0 5.8 %collective-permute-start.17 = (f32[128,128]{1,0:T(8,128)S(1)}, f32[128,128]{1,0:T(8,128)S(1)}, u32[]{:S(2)}, u32[]{:S(2)}) collective-permute-start(f32[128,128]{1,0:T(8,128)S(1)} %add_pair.1.t0), channel_id=1, source_target_pairs={{0,16},{4,20},{8,24},{12,28},{16,0},{20,4},{24,8},{28,12},{32,48},... | collective-permute-start | bytes 196616 | tf_op jit(solution)/shard_map/ppermute | solution.py:483
  150.9 5.6 %collective-permute-start.16 = (f32[128,128]{1,0:T(8,128)S(1)}, f32[128,128]{1,0:T(8,128)S(1)}, u32[]{:S(2)}, u32[]{:S(2)}) collective-permute-start(f32[128,128]{1,0:T(8,128)S(1)} %add_pair.1.t0), channel_id=1, source_target_pairs={{0,8},{4,12},{8,16},{12,20},{16,24},{20,28},{24,0},{28,4},{32,40},... | collective-permute-start | bytes 196616 | tf_op jit(solution)/shard_map/ppermute | solution.py:483
  151.8 0.7 copy-start.7

commit v3 on v2

--- a/solution.py
+++ b/solution.py
@@ -49,7 +49,7 @@
 
 
 STEP = 256
-MASK_STEP = 1024
+MASK_STEP = 2048
 TILES = 176
 PIECES = 4
 PIECE = TILES // PIECES
@@ -68,39 +68,39 @@
                      slot_hbm, tiles, bits, cot, d_t, acc, slots, sems, out_sems):
     count = count_ref[0]
     bits_in = pltpu.make_async_copy(bits_hbm, bits, sems.at[PIECES])
-    cot_in = pltpu.make_async_copy(cot_hbm, cot, sems.at[PIECES + 1])
+    steps = [pl.ds(i * MASK_STEP, MASK_STEP) for i in range(4096 // MASK_STEP)]
+    cot_in = [
+        pltpu.make_async_copy(cot_hbm.at[r], cot.at[r], sems.at[PIECES + 1 + i])
+        for i, r in enumerate(steps)
+    ]
     bits_in.start()
-    cot_in.start()
+    for c in cot_in:
+        c.start()
     copies = tile_copies(tiles_hbm, tiles, sems)
     for c in copies:
         c.start()
     acc[...] = jnp.zeros_like(acc)
     bits_in.wait()
-    cot_in.wait()
-
-    def mask(i, carry):
-        at = pl.multiple_of(i * MASK_STEP, MASK_STEP)
-        active = bit_mask(bits[:, pl.ds(at, MASK_STEP)])
-        v = jnp.where(active, cot[pl.ds(at, MASK_STEP), :].astype(F32), 0.0)
+
+    for i, r in enumerate(steps):
+        cot_in[i].wait()
+        active = bit_mask(bits[:, r])
+        v = jnp.where(active, cot[r, :].astype(F32), 0.0)
         for j in range(MASK_STEP // B):
             d_t[i * (MASK_STEP // B) + j] = v[j * B : (j + 1) * B].T.astype(BF16)
-        return carry
-
-    lax.fori_loop(0, 4096 // MASK_STEP, mask, 0)
     for k in range(PIECES):
         copies[k].wait()
 
         for t in range(k * PIECE, (k + 1) * PIECE):
             s = jnp.where(t < count, cols_ref[0, t], RB + 64)
             acc[s] += dot(d_t[rows_ref[0, t]], tiles[t])
-    outs = []
+    outs = [pltpu.make_async_copy(acc.at[pl.ds(0, RB)], own_hbm, out_sems.at[4])]
+    outs[0].start()
     for k in range(4):
         at = pl.ds(k * 16, 16)
         slots[at] = acc[RB + k * 16 : RB + (k + 1) * 16].astype(BF16)
         outs.append(pltpu.make_async_copy(slots.at[at], slot_hbm.at[at], out_sems.at[k]))
         outs[-1].start()
-    outs.append(pltpu.make_async_copy(acc.at[pl.ds(0, RB)], own_hbm, out_sems.at[4]))
-    outs[-1].start()
     for c in outs:
         c.wait()
 
@@ -121,7 +121,7 @@
             pltpu.VMEM((RB, B, B), BF16),
             pltpu.VMEM((RB + 65, B, B), F32),
             pltpu.VMEM((64, B, B), BF16),
-            pltpu.SemaphoreType.DMA((PIECES + 2,)),
+            pltpu.SemaphoreType.DMA((PIECES + 3,)),
             pltpu.SemaphoreType.DMA((5,)),
         ],
         compiler_params=params(),
@@ -130,18 +130,37 @@
     )(count, rows, cols, bits_t, cot, tiles)
 
 
-def tiles_fwd_kernel(count_ref, rows_ref, cols_ref, bits_hbm, own_hbm, recv_hbm, tiles_hbm,
-                     out_ref, token, tiles, src, acc, bits, sems):
+def active_kernel(bits_ref, mask_ref, token):
+    for i in range(4096 // MASK_STEP):
+        r = pl.ds(i * MASK_STEP, MASK_STEP)
+        mask_ref[r, :] = jnp.where(bit_mask(bits_ref[:, r]), 1.0, 0.0).astype(BF16)
+    token[...] = jnp.zeros_like(token)
+
+
+def active_call(bits_t):
+    return pl.pallas_call(
+        active_kernel,
+        out_shape=[jax.ShapeDtypeStruct((4096, B), BF16), jax.ShapeDtypeStruct((8, B), F32)],
+        in_specs=[VMEM],
+        out_specs=[VMEM] * 2,
+        compiler_params=params(40),
+        cost_estimate=cost(4096 * B * 40, 2 << 20),
+        name="active",
+    )(bits_t)
+
+
+def tiles_fwd_kernel(count_ref, rows_ref, cols_ref, mask_hbm, own_hbm, recv_hbm, tiles_hbm,
+                     out_ref, token, tiles, src, acc, active, sems):
     count = count_ref[0]
     own = pltpu.make_async_copy(own_hbm, src.at[pl.ds(0, RB)], sems.at[PIECES])
     got = pltpu.make_async_copy(recv_hbm, src.at[pl.ds(RB, 64)], sems.at[PIECES + 1])
-    bits_in = pltpu.make_async_copy(bits_hbm, bits, sems.at[PIECES + 2])
+    mask_in = pltpu.make_async_copy(mask_hbm, active, sems.at[PIECES + 2])
     own.start()
     got.start()
     copies = tile_copies(tiles_hbm, tiles, sems)
     for c in copies:
         c.start()
-    bits_in.start()
+    mask_in.start()
     acc[...] = jnp.zeros_like(acc)
     own.wait()
     got.wait()
@@ -153,20 +172,14 @@
             acc[r] += dot(tiles[t], src[cols_ref[0, t]])
 
     token[...] = jnp.zeros_like(token)
-    bits_in.wait()
-
-    def mask(i, carry):
-        at = pl.multiple_of(i * MASK_STEP, MASK_STEP)
-        active = bit_mask(bits[:, pl.ds(at, MASK_STEP)])
-        for j in range(MASK_STEP // B):
-            b = i * (MASK_STEP // B) + j
-            out_ref[b] = jnp.where(active[j * B : (j + 1) * B], acc[b], 0.0).astype(BF16)
-        return carry
-
-    lax.fori_loop(0, 4096 // MASK_STEP, mask, 0)
-
-
-def tiles_fwd_call(count, rows, cols, bits_t, own, recv, tiles):
+    mask_in.wait()
+
+    for b in range(RB):
+        keep = active[b * B : (b + 1) * B, :].astype(F32) > 0.5
+        out_ref[b] = jnp.where(keep, acc[b], 0.0).astype(BF16)
+
+
+def tiles_fwd_call(count, rows, cols, mask, own, recv, tiles):
     return pl.pallas_call(
         tiles_fwd_kernel,
         out_shape=[jax.ShapeDtypeStruct((RB, B, B), BF16), jax.ShapeDtypeStruct((8, B), F32)],
@@ -176,16 +189,16 @@
             pltpu.VMEM((TILES, B, B), BF16),
             pltpu.VMEM((RB + 64, B, B), BF16),
             pltpu.VMEM((RB + 1, B, B), F32),
-            pltpu.VMEM((8, 4096), jnp.int32),
+            pltpu.VMEM((4096, B), BF16),
             pltpu.SemaphoreType.DMA((PIECES + 3,)),
         ],
         compiler_params=params(58),
         cost_estimate=cost(2 * TILES * B * B * B, 30 << 20),
         name="tiles_fwd",
-    )(count, rows, cols, bits_t, own, recv, tiles)
-
-
-def hidden_kernel(me_ref, send_ref, x0, x1, x2a, x2b, x3, w_ref, hid_hbm, out_hbm, hid, sems):
+    )(count, rows, cols, mask, own, recv, tiles)
+
+
+def hidden_kernel(me_ref, send_ref, x0, x1, x2a, x2b, x3, w_ref, after, hid_hbm, out_hbm, hid, sems):
     me = me_ref[0]
     rhs = jnp.concatenate(
         [w_ref[pl.ds(pl.multiple_of(rel(me, -s) * B, B), B), :] for s in range(HID)], 0
@@ -207,20 +220,20 @@
         c.wait()
 
 
-def hidden_call(me, send, xs, w):
+def hidden_call(me, send, xs, w, after):
     return pl.pallas_call(
         hidden_kernel,
         out_shape=[
             jax.ShapeDtypeStruct((RB, B, B), BF16),
             jax.ShapeDtypeStruct((64, B, B), BF16),
         ],
-        in_specs=[SMEM] * 2 + [VMEM] * 6,
+        in_specs=[SMEM] * 2 + [VMEM] * 6 + [ANY],
         out_specs=[HBM] * 2,
         scratch_shapes=[pltpu.VMEM((RB, B, B), BF16), pltpu.SemaphoreType.DMA((65,))],
         compiler_params=params(),
         cost_estimate=cost(2 * 4096 * 512 * 128, 10 << 20),
         name="hidden",
-    )(me, send, *xs, w)
+    )(me, send, *xs, w, after)
 
 
 def sum_kernel(me_ref, send_ref, own_hbm, got_hbm, x0, x1, x2a, x2b, x3, w_hbm, after,
@@ -329,16 +342,16 @@
 
 
 def add_z_kernel(me_ref, p0, p1, p2, p3, out, by_z):
-    z = lax.div(me_ref[2], 2)
+    z = me_ref[2] & 3
     for k, p in enumerate((p0, p1, p2, p3)):
-        by_z[rel(z, -k)] = p[...].astype(F32)
-    out[...] = (by_z[0] + by_z[1]) + (by_z[2] + by_z[3])
+        by_z[z ^ k] = p[...].astype(F32)
+    out[...] = ((by_z[0] + by_z[1]) + (by_z[2] + by_z[3])).astype(BF16)
 
 
 def add_z_call(me, parts):
     return pl.pallas_call(
         add_z_kernel,
-        out_shape=jax.ShapeDtypeStruct((B, B), F32),
+        out_shape=jax.ShapeDtypeStruct((B, B), BF16),
         in_specs=[SMEM] + [VMEM] * 4,
         out_specs=VMEM,
         scratch_shapes=[pltpu.VMEM((4, B, B), F32)],
@@ -349,7 +362,7 @@
 
 
 def pair_kernel(a, b, after, out):
-    out[...] = a[...] + b[...]
+    out[...] = a[...].astype(F32) + b[...].astype(F32)
 
 
 def pair_call(a, b, after):
@@ -483,8 +496,8 @@
     return lax.ppermute(v, "dom", pairs)
 
 
-def swap_z(v):
-    return lax.ppermute(v, "dom", [(i, i ^ 8) for i in range(64)])
+def swap_z(v, k):
+    return lax.ppermute(v, "dom", [(i, i ^ (8 * k)) for i in range(64)])
 
 
 def all_to_all(v):
@@ -502,7 +515,8 @@
     returned = all_to_all(slots)
 
     xs = gather_hid(x, slots)
-    hidden, outgoing = hidden_call(me, send, xs, w)
+    mask, ready = active_call(bits_t)
+    hidden, outgoing = hidden_call(me, send, xs, w, ready)
     incoming = all_to_all(outgoing)
 
     terms, p0, p1, p2a, p2b, p3 = sum_call(me, send, own, returned, xs, w, outgoing)
@@ -514,9 +528,9 @@
     p1, p3 = relay_call(p1, p3, shift_hid(p2a, 1), shift_hid(p2b, 3), part)
     parts = [p0, shift_hid(p1, 1), shift_hid(p3, 3)]
 
-    total = add_z_call(me, [part] + [shift_dom(part, k, 0, 0) for k in (2, 4, 6)])
-    out_act, token = tiles_fwd_call(count, rows, cols, bits_t, hidden, incoming, tiles)
-    total = pair_call(total, swap_z(total), token)
+    total = add_z_call(me, [part] + [swap_z(part, k) for k in (1, 2, 3)])
+    out_act, token = tiles_fwd_call(count, rows, cols, mask, hidden, incoming, tiles)
+    total = pair_call(total, swap_z(total, 4), token)
     weight_grad = finish_call(me, [total] + [shift_dom(total, 0, k, 0) for k in range(1, 4)])
     input_grad = parts_call(parts, token)
     return out_act.reshape(4096, B), input_grad, weight_grad

time: 158 us -> 154 us (0.975)
  starting transfers between devices: 52.3 us -> 48.8 us
    ppermute x10 -> x7, waiting for transfers between devices: 22.8 us -> 5.92 us  [shift_dom(): return lax.ppermute(v, 'dom', pairs)]
    ppermute x1 -> x4, waiting for transfers between devices: 0.01 us -> 16.1 us  [swap_z(): return lax.ppermute(v, 'dom', [(i, i ^ 8 * k) for i in range(64)])]
    ppermute x10 -> x7, starting transfers between devices: 18.4 us -> 11.1 us  [shift_dom(): return lax.ppermute(v, 'dom', pairs)]
    ppermute x1 -> x4, starting transfers between devices: 1.06 us -> 8.19 us  [swap_z(): return lax.ppermute(v, 'dom', [(i, i ^ 8 * k) for i in range(64)])]
    ppermute x8, waiting for transfers between devices: 38.7 us -> 36.6 us  [shift_hid(): return lax.ppermute(v, 'hid', [(i, (i + s) % HID) for i in range(HID)])]
    ppermute x8, starting transfers between devices: 10.1 us -> 8.26 us  [shift_hid(): return lax.ppermute(v, 'hid', [(i, (i + s) % HID) for i in range(HID)])]
    all_to_all x2, waiting for transfers between devices: 0.69 us -> 2.45 us  [all_to_all(): return lax.all_to_all(v, 'dom', split_axis=0, concat_axis=0, tiled=True)]
    unnamed x24 -> x30, local copies, waits for them, and re-layouts: 4.63 us -> 5.87 us
  transfers between devices with their start and end apart: 21 -> 21, of which waited for: 13 -> 13; matrix products, arithmetic and copies ran while one was open for 1% -> 1% of each run, Pallas kernels for 16% -> 17%
where the time goes in v3:
time: 154 us; the launch traced here: 153 us
  waiting for transfers between devices  61.1 us (40%)
  starting transfers between devices  48.8 us (32%)
  Pallas kernels  34.4 us (22%)
  local copies, waits for them, and re-layouts  5.89 us (4%)
  other arithmetic  1.64 us (1%)
    ppermute x8, waiting for transfers between devices, shift_hid(): return lax.ppermute(v, 'hid', [(i, (i + s) % HID) for i in range(HID)])  36.6 us
    all_to_all x2, starting transfers between devices, all_to_all(): return lax.all_to_all(v, 'dom', split_axis=0, concat_axis=0, tiled=True)  21.2 us
    ppermute x4, waiting for transfers between devices, swap_z(): return lax.ppermute(v, 'dom', [(i, i ^ 8 * k) for i in range(64)])  16.1 us
    ppermute x7, starting transfers between devices, shift_dom(): return lax.ppermute(v, 'dom', pairs)  11.1 us
    pallas_call x1, Pallas kernels, sum_call(): pl.pallas_call(sum_kernel, out_shape=[jax.ShapeDtypeStruct((512, B), F32)...  9.15 us
    ppermute x8, starting transfers between devices, shift_hid(): return lax.ppermute(v, 'hid', [(i, (i + s) % HID) for i in range(HID)])  8.26 us
    ppermute x4, starting transfers between devices, swap_z(): return lax.ppermute(v, 'dom', [(i, i ^ 8 * k) for i in range(64)])  8.19 us
    pallas_call x1, Pallas kernels, tiles_bwd_call(): pl.pallas_call(tiles_bwd_kernel, out_shape=[jax.ShapeDtypeStruct((RB, B,...  7.43 us
  transfers between devices with their start and end apart: 21, of which 13 were waited for; matrix products, arithmetic and copies ran while one was open for 1% of the time, Pallas kernels for 17%

profile of v3, /device:TPU:6, one launch (start us, length us, event | category | flops | bytes accessed | tf_op | source)
XLA Modules:
  0.0 153.3 jit_solution(736729916236598129)
XLA Ops:
  1.3 7.4 %tiles_bwd.1 = (f32[32,128,128]{2,1,0:T(8,128)}, bf16[64,128,128]{2,1,0:T(8,128)(2,1)}) custom-call(s32[1]{0:T(128)S(6)} %copy.12.count_ref, s32[1,176]{1,0:T(1,128)} %rows_ref.3, s32[1,176]{1,0:T(1,128)} %cols_ref.3, s32[8,4096]{1,0:T(8,128)} %bitcast.5, bf16[4096,128]{1,0:T(8,128)(2,1)} %cot_hbm.1, bf16[176,128,128]{2,1,0:T(8,128)(2,1)} %tiles_hbm.3), custom_call_target="tpu_custom_call" | custom-call | flops 738197504 | bytes 31457280 | tf_op jit(solution)/shard_map/tiles_bwd/pallas_call | solution.py:109
  8.7 12.6 %all-to-all-start.1 = ((bf16[64,128,128]{2,1,0:T(8,128)(2,1)}), bf16[64,128,128]{2,1,0:T(8,128)(2,1)}, u32[]{:S(2)}, u32[]{:S(2)}) async-start(bf16[64,128,128]{2,1,0:T(8,128)(2,1)} %get-tuple-element.22.after), calls=%async_computation.1 | async-start | bytes 4194304 | tf_op jit(solution)/shard_map/all_to_all | solution.py:504
  22.0 1.5 %collective-permute-start.1 = (bf16[4096,128]{1,0:T(8,128)(2,1)S(1)}, bf16[4096,128]{1,0:T(8,128)(2,1)S(1)}, u32[]{:S(2)}, u32[]{:S(2)}) collective-permute-start(bf16[4096,128]{1,0:T(8,128)(2,1)S(1)} %copy-done.12), channel_id=1, source_target_pairs={{0,3},{1,0},{2,1},{3,2},{4,7},{5,4},{6,5},{7,6},{8,11},{9,8},{10,9... | collective-permute-start | bytes 3145736 | tf_op jit(solution)/shard_map/ppermute | solution.py:457
  23.5 23.0 %collective-permute-done.v1.x1 = bf16[4096,128]{1,0:T(8,128)(2,1)S(1)} collective-permute-done((bf16[4096,128]{1,0:T(8,128)(2,1)S(1)}, bf16[4096,128]{1,0:T(8,128)(2,1)S(1)}, u32[]{:S(2)}, u32[]{:S(2)}) %collective-permute-start) | collective-permute-done | bytes 1048608 | tf_op jit(solution)/shard_map/ppermute | solution.py:457
  46.5 1.4 collective-permute-done.1.v3.x3
  48.0 0.9 copy-done.1
  48.9 0.6 collective-permute-start.2
  49.5 1.4 collective-permute-start.3
  51.0 0.6 active.1
  51.6 1.0 copy-done.6
  52.5 0.6 copy-done.11
  53.1 0.7 pad_add_fusion.me_ref
  53.8 7.9 %collective-permute-done.2.x2a = bf16[2048,128]{1,0:T(8,128)(2,1)S(1)} collective-permute-done((bf16[2048,128]{1,0:T(8,128)(2,1)S(1)}, bf16[2048,128]{1,0:T(8,128)(2,1)S(1)}, u32[]{:S(2)}, u32[]{:S(2)}) %collective-permute-start.2) | collective-permute-done | bytes 524320 | tf_op jit(solution)/shard_map/ppermute | solution.py:457
  61.7 1.9 %collective-permute-done.3.x2b = bf16[2048,128]{1,0:T(8,128)(2,1)S(1)} collective-permute-done((bf16[2048,128]{1,0:T(8,128)(2,1)S(1)}, bf16[2048,128]{1,0:T(8,128)(2,1)S(1)}, u32[]{:S(2)}, u32[]{:S(2)}) %collective-permute-start.3) | collective-permute-done | bytes 524320 | tf_op jit(solution)/shard_map/ppermute | solution.py:457
  63.5 0.8 copy-done.14
  64.3 5.8 %hidden.1 = (bf16[32,128,128]{2,1,0:T(8,128)(2,1)}, bf16[64,128,128]{2,1,0:T(8,128)(2,1)}) custom-call(s32[3]{0:T(128)} %pad_add_fusion.me_ref, s32[1,64]{1,0:T(1,128)} %send_ref.3, bf16[4096,128]{1,0:T(8,128)(2,1)} %x0.3, bf16[4096,128]{1,0:T(8,128)(2,1)} %copy-done, bf16[2048,128]{1,0:T(8,128)(2,1)} %copy-done.13, bf16[2048,128]{1,0:T(8,128)(2,1)} %copy-done.14, ...), custom_call_target="tpu_custom_call" | custom-call | flops 536870912 | bytes 10485760 | tf_op jit(solution)/shard_map/hidden/pallas_call | solution.py:224
  70.1 2.4 %all-to-all-done.1.got_hbm = bf16[64,128,128]{2,1,0:T(8,128)(2,1)} async-done(((bf16[64,128,128]{2,1,0:T(8,128)(2,1)}), bf16[64,128,128]{2,1,0:T(8,128)(2,1)}, u32[]{:S(2)}, u32[]{:S(2)}) %all-to-all-start.1) | async-done | bytes 2097184 | tf_op jit(solution)/shard_map/all_to_all | solution.py:504
  72.6 8.6 %all-to-all-start = ((bf16[64,128,128]{2,1,0:T(8,128)(2,1)}), bf16[64,128,128]{2,1,0:T(8,128)(2,1)}, u32[]{:S(2)}, u32[]{:S(2)}) async-start(bf16[64,128,128]{2,1,0:T(8,128)(2,1)} %get-tuple-element.27.after), calls=%async_computation | async-start | bytes 4194304 | tf_op jit(solution)/shard_map/all_to_all | solution.py:504
  81.2 9.2 %sum_returned.1 = (f32[512,128]{1,0:T(8,128)}, bf16[4096,128]{1,0:T(8,128)(2,1)}, bf16[4096,128]{1,0:T(8,128)(2,1)}, bf16[2048,128]{1,0:T(8,128)(2,1)}, bf16[204...) custom-call(s32[3]{0:T(128)} %pad_add_fusion.me_ref, s32[1,64]{1,0:T(1,128)} %send_ref.3, ...), custom_call_target="tpu_custom_call" | custom-call | flops 536870912 | bytes 12582912 | tf_op jit(solution)/shard_map/sum_returned/pallas_call | solution.py:305
  91.0 1.6 %collective-permute-start.5 = (bf16[2048,128]{1,0:T(8,128)(2,1)}, bf16[2048,128]{1,0:T(8,128)(2,1)S(1)}, u32[]{:S(2)}, u32[]{:S(2)}) collective-permute-start(bf16[2048,128]{1,0:T(8,128)(2,1)} %get-tuple-element.34), channel_id=1, source_target_pairs={{0,3},{1,0},{2,1},{3,2},{4,7},{5,4},{6,5},{7,6},{8,11},{9,8},{10,9... | collective-permute-start | bytes 1572872 | tf_op jit(solution)/shard_map/ppermute | solution.py:457
  92.6 1.0 add.10
  93.6 1.5 collective-permute-start.7
  95.1 1.8 %collective-permute-start.8 = (f32[128,128]{1,0:T(8,128)S(1)}, f32[128,128]{1,0:T(8,128)S(1)}, u32[]{:S(2)}, u32[]{:S(2)}) collective-permute-start(f32[128,128]{1,0:T(8,128)S(1)} %get-tuple-element.40), channel_id=1, source_target_pairs={{0,24},{4,28},{8,0},{12,4},{16,8},{20,12},{24,16},{28,20},{32,56},... | collective-permute-start | bytes 196616 | tf_op jit(solution)/shard_map/ppermute | solution.py:496
  96.9 1.7 %collective-permute-start.9 = (f32[128,128]{1,0:T(8,128)S(1)}, f32[128,128]{1,0:T(8,128)S(1)}, u32[]{:S(2)}, u32[]{:S(2)}) collective-permute-start(f32[128,128]{1,0:T(8,128)S(1)} %get-tuple-element.39), channel_id=1, source_target_pairs={{0,16},{4,20},{8,24},{12,28},{16,0},{20,4},{24,8},{28,12},{32,48},... | collective-permute-start | bytes 196616 | tf_op jit(solution)/shard_map/ppermute | solution.py:496
  98.6 1.5 collective-permute-done.7.b
  100.1 0.6 collective-permute-done.8.c
  100.7 3.2 %collective-permute-done.9.d = f32[128,128]{1,0:T(8,128)S(1)} collective-permute-done((f32[128,128]{1,0:T(8,128)S(1)}, f32[128,128]{1,0:T(8,128)S(1)}, u32[]{:S(2)}, u32[]{:S(2)}) %collective-permute-start.9) | collective-permute-done | bytes 65568 | tf_op jit(solution)/shard_map/ppermute | solution.py:496
  103.9 1.1 collective-permute-done.4.low
  105.0 1.4 collective-permute-done.5.high
  106.4 1.2 copy-done.5
  107.6 1.2 relay.1
  109.1 1.7 %collective-permute-start.11 = (bf16[4096,128]{1,0:T(8,128)(2,1)S(1)}, bf16[4096,128]{1,0:T(8,128)(2,1)S(1)}, u32[]{:S(2)}, u32[]{:S(2)}) collective-permute-start(bf16[4096,128]{1,0:T(8,128)(2,1)S(1)} %get-tuple-element.37), channel_id=1, source_target_pairs={{0,3},{1,0},{2,1},{3,2},{4,7},{5,4},{6,5},{7,6},{8,11},{9,8},{10,9... | collective-permute-start | bytes 3145736 | tf_op jit(solution)/shard_map/ppermute | solution.py:457
  110.9 1.3 collective-permute-start.12
  112.2 2.4 %collective-permute-start.13 = (bf16[128,128]{1,0:T(8,128)(2,1)S(1)}, bf16[128,128]{1,0:T(8,128)(2,1)S(1)}, u32[]{:S(2)}, u32[]{:S(2)}) collective-permute-start(bf16[128,128]{1,0:T(8,128)(2,1)S(1)} %add_y.1.after.p0), channel_id=1, source_target_pairs={{0,64},{4,68},{8,72},{12,76},{16,80},{20,84},{24,88},{28,92},{32,9... | collective-permute-start | bytes 98312 | tf_op jit(solution)/shard_map/ppermute | solution.py:500
  114.6 0.7 collective-permute-start.14
  115.2 14.3 %collective-permute-done.12.p1 = bf16[128,128]{1,0:T(8,128)(2,1)S(1)} collective-permute-done((bf16[128,128]{1,0:T(8,128)(2,1)S(1)}, bf16[128,128]{1,0:T(8,128)(2,1)S(1)}, u32[]{:S(2)}, u32[]{:S(2)}) %collective-permute-start.12) | collective-permute-done | bytes 32800 | tf_op jit(solution)/shard_map/ppermute | solution.py:500
  129.5 1.8 %collective-permute-done.14.p3 = bf16[128,128]{1,0:T(8,128)(2,1)S(1)} collective-permute-done((bf16[128,128]{1,0:T(8,128)(2,1)S(1)}, bf16[128,128]{1,0:T(8,128)(2,1)S(1)}, u32[]{:S(2)}, u32[]{:S(2)}) %collective-permute-start.14) | collective-permute-done | bytes 32800 | tf_op jit(solution)/shard_map/ppermute | solution.py:500
  131.4 0.6 add_z.1.a
  131.9 3.8 %collective-permute-start.15 = (bf16[128,128]{1,0:T(8,128)(2,1)S(1)}, bf16[128,128]{1,0:T(8,128)(2,1)S(1)}, u32[]{:S(2)}, u32[]{:S(2)}) collective-permute-start(bf16[128,128]{1,0:T(8,128)(2,1)S(1)} %add_z.1.a), channel_id=1, source_target_pairs={{0,128},{4,132},{8,136},{12,140},{16,144},{20,148},{24,152},{28,15... | collective-permute-start | bytes 98312 | tf_op jit(solution)/shard_map/ppermute | solution.py:500
  135.8 6.8 %tiles_fwd.1 = (bf16[32,128,128]{2,1,0:T(8,128)(2,1)}, f32[8,128]{1,0:T(8,128)}) custom-call(s32[1]{0:T(128)S(6)} %copy.12.count_ref, s32[1,176]{1,0:T(1,128)} %rows_ref.3, s32[1,176]{1,0:T(1,128)} %cols_ref.3, bf16[4096,128]{1,0:T(8,128)(2,1)} %copy-done.6, bf16[32,128,128]{2,1,0:T(8,128)(2,1)} %get-tuple-element.26.own_hbm, ...), custom_call_target="tpu_custom_call" | custom-call | flops 738197504 | bytes 31457280 | tf_op jit(solution)/shard_map/tiles_fwd/pallas_call | solution.py:183
  142.6 0.7 copy-done.8
  143.3 1.8 %collective-permute-start.16 = (f32[128,128]{1,0:T(8,128)S(1)}, f32[128,128]{1,0:T(8,128)S(1)}, u32[]{:S(2)}, u32[]{:S(2)}) collective-permute-start(f32[128,128]{1,0:T(8,128)S(1)} %add_pair.1.t0), channel_id=1, source_target_pairs={{0,8},{4,12},{8,16},{12,20},{16,24},{20,28},{24,0},{28,4},{32,40},... | collective-permute-start | bytes 196616 | tf_op jit(solution)/shard_map/ppermute | solution.py:496
  145.0 2.7 %collective-permute-start.17 = (f32[128,128]{1,0:T(8,128)S(1)}, f32[128,128]{1,0:T(8,128)S(1)}, u32[]{:S(2)}, u32[]{:S(2)}) collective-permute-start(f32[128,128]{1,0:T(8,128)S(1)} %add_pair.1.t0), channel_id=1, source_target_pairs={{0,16},{4,20},{8,24},{12,28},{16,0},{20,4},{24,8},{28,12},{32,48},... | collective-permute-start | bytes 196616 | tf_op jit(solution)/shard_map/ppermute | solution.py:496
  147.8 1.5 collective-permute-start.18
  149.3 0.7 copy-done.9
  149.9 1.5 add_parts.1
  151.4 0.6 collective-permute-done.18.t3
  152.0 1.3 finish.1
  (39 shorter events, 1.6 us)
Async XLA Ops:
  8.7 12.7 %copy-start.12 = (bf16[4096,128]{1,0:T(8,128)(2,1)S(1)}, bf16[4096,128]{1,0:T(8,128)(2,1)}, u32[]{:S(2)}) copy-start(bf16[4096,128]{1,0:T(8,128)(2,1)} %x0.3) | copy-start | bytes 3145732
  8.7 39.2 %copy-start.2 = (bf16[64,128,128]{2,1,0:T(8,128)(2,1)S(1)}, bf16[64,128,128]{2,1,0:T(8,128)(2,1)}, u32[]{:S(2)}) copy-start(bf16[64,128,128]{2,1,0:T(8,128)(2,1)} %get-tuple-element.22.after) | copy-start | bytes 6291460
  8.7 63.9 %all-to-all-start.1 = ((bf16[64,128,128]{2,1,0:T(8,128)(2,1)}), bf16[64,128,128]{2,1,0:T(8,128)(2,1)}, u32[]{:S(2)}, u32[]{:S(2)}) async-start(bf16[64,128,128]{2,1,0:T(8,128)(2,1)} %get-tuple-element.22.after), calls=%async_computation.1 | async-start | bytes 4194304 | tf_op jit(solution)/shard_map/all_to_all | solution.py:504
  21.4 29.6 %copy-start.7 = (s32[4096,8]{0,1:T(8,128)S(1)}, s32[4096,8]{0,1:T(8,128)}, u32[]{:S(2)}) copy-start(s32[4096,8]{0,1:T(8,128)} %param.16) | copy-start | bytes 393220
  21.4 25.1 %collective-permute-start = (bf16[4096,128]{1,0:T(8,128)(2,1)S(1)}, bf16[4096,128]{1,0:T(8,128)(2,1)S(1)}, u32[]{:S(2)}, u32[]{:S(2)}) collective-permute-start(bf16[4096,128]{1,0:T(8,128)(2,1)S(1)} %copy-done.12), channel_id=1, source_target_pairs={{0,1},{1,2},{2,3},{3,0},{4,5},{5,6},{6,7},{7,4},{8,9},{9,10},{10,1... | collective-permute-start | bytes 3145736 | tf_op jit(solution)/shard_map/ppermute | solution.py:457
  22.0 26.0 %collective-permute-start.1 = (bf16[4096,128]{1,0:T(8,128)(2,1)S(1)}, bf16[4096,128]{1,0:T(8,128)(2,1)S(1)}, u32[]{:S(2)}, u32[]{:S(2)}) collective-permute-start(bf16[4096,128]{1,0:T(8,128)(2,1)S(1)} %copy-done.12), channel_id=1, source_target_pairs={{0,3},{1,0},{2,1},{3,2},{4,7},{5,4},{6,5},{7,6},{8,11},{9,8},{10,9... | collective-permute-start | bytes 3145736 | tf_op jit(solution)/shard_map/ppermute | solution.py:457
  46.5 1.5 copy-start
  47.9 1.0 copy-start.1
  48.9 12.7 %collective-permute-start.2 = (bf16[2048,128]{1,0:T(8,128)(2,1)S(1)}, bf16[2048,128]{1,0:T(8,128)(2,1)S(1)}, u32[]{:S(2)}, u32[]{:S(2)}) collective-permute-start(bf16[2048,128]{1,0:T(8,128)(2,1)S(1)} %get-tuple-element.23), channel_id=1, source_target_pairs={{0,1},{1,2},{2,3},{3,0},{4,5},{5,6},{6,7},{7,4},{8,9},{9,10},{10,1... | collective-permute-start | bytes 1572872 | tf_op jit(solution)/shard_map/ppermute | solution.py:457
  49.5 14.0 %collective-permute-start.3 = (bf16[2048,128]{1,0:T(8,128)(2,1)S(1)}, bf16[2048,128]{1,0:T(8,128)(2,1)S(1)}, u32[]{:S(2)}, u32[]{:S(2)}) collective-permute-start(bf16[2048,128]{1,0:T(8,128)(2,1)S(1)} %get-tuple-element.24), channel_id=1, source_target_pairs={{0,3},{1,0},{2,1},{3,2},{4,7},{5,4},{6,5},{7,6},{8,11},{9,8},{10,9... | collective-permute-start | bytes 1572872 | tf_op jit(solution)/shard_map/ppermute | solution.py:457
  51.6 1.0 copy-start.6
  52.5 0.6 copy-start.11
  61.7 1.9 %copy-start.13 = (bf16[2048,128]{1,0:T(8,128)(2,1)}, bf16[2048,128]{1,0:T(8,128)(2,1)S(1)}, u32[]{:S(2)}) copy-start(bf16[2048,128]{1,0:T(8,128)(2,1)S(1)} %collective-permute-done.2.x2a) | copy-start | bytes 1572868
  63.5 0.8 copy-start.14
  72.6 63.2 %all-to-all-start = ((bf16[64,128,128]{2,1,0:T(8,128)(2,1)}), bf16[64,128,128]{2,1,0:T(8,128)(2,1)}, u32[]{:S(2)}, u32[]{:S(2)}) async-start(bf16[64,128,128]{2,1,0:T(8,128)(2,1)} %get-tuple-element.27.after), calls=%async_computation | async-start | bytes 4194304 | tf_op jit(solution)/shard_map/all_to_all | solution.py:504
  90.4 16.0 %copy-start.4 = (bf16[4096,128]{1,0:T(8,128)(2,1)S(1)}, bf16[4096,128]{1,0:T(8,128)(2,1)}, u32[]{:S(2)}) copy-start(bf16[4096,128]{1,0:T(8,128)(2,1)} %get-tuple-element.31.p1) | copy-start | bytes 3145732
  90.4 2.2 %collective-permute-start.6 = (f32[512,128]{1,0:T(8,128)}, f32[512,128]{1,0:T(8,128)S(1)}, u32[]{:S(2)}, u32[]{:S(2)}) collective-permute-start(f32[512,128]{1,0:T(8,128)} %get-tuple-element.35), channel_id=1, source_target_pairs={{0,4},{4,0},{8,12},{12,8},{16,20},{20,16},{24,28},{28,24},{32,36},... | collective-permute-start | bytes 786440 | tf_op jit(solution)/shard_map/ppermute | solution.py:496
  90.5 14.6 %collective-permute-start.4 = (bf16[2048,128]{1,0:T(8,128)(2,1)}, bf16[2048,128]{1,0:T(8,128)(2,1)S(1)}, u32[]{:S(2)}, u32[]{:S(2)}) collective-permute-start(bf16[2048,128]{1,0:T(8,128)(2,1)} %get-tuple-element.33), channel_id=1, source_target_pairs={{0,1},{1,2},{2,3},{3,0},{4,5},{5,6},{6,7},{7,4},{8,9},{9,10},{10,1... | collective-permute-start | bytes 1572872 | tf_op jit(solution)/shard_map/ppermute | solution.py:457
  91.0 15.4 %collective-permute-start.5 = (bf16[2048,128]{1,0:T(8,128)(2,1)}, bf16[2048,128]{1,0:T(8,128)(2,1)S(1)}, u32[]{:S(2)}, u32[]{:S(2)}) collective-permute-start(bf16[2048,128]{1,0:T(8,128)(2,1)} %get-tuple-element.34), channel_id=1, source_target_pairs={{0,3},{1,0},{2,1},{3,2},{4,7},{5,4},{6,5},{7,6},{8,11},{9,8},{10,9... | collective-permute-start | bytes 1572872 | tf_op jit(solution)/shard_map/ppermute | solution.py:457
  93.6 37.8 %copy-start.10 = (s32[3]{0:T(128)S(1)}, s32[3]{0:T(128)}, u32[]{:S(2)}) copy-start(s32[3]{0:T(128)} %pad_add_fusion.me_ref) | copy-start | bytes 40
  93.6 6.5 %collective-permute-start.7 = (f32[128,128]{1,0:T(8,128)S(1)}, f32[128,128]{1,0:T(8,128)S(1)}, u32[]{:S(2)}, u32[]{:S(2)}) collective-permute-start(f32[128,128]{1,0:T(8,128)S(1)} %get-tuple-element.41), channel_id=1, source_target_pairs={{0,8},{4,12},{8,16},{12,20},{16,24},{20,28},{24,0},{28,4},{32,40},... | collective-permute-start | bytes 196616 | tf_op jit(solution)/shard_map/ppermute | solution.py:496
  95.1 5.6 %collective-permute-start.8 = (f32[128,128]{1,0:T(8,128)S(1)}, f32[128,128]{1,0:T(8,128)S(1)}, u32[]{:S(2)}, u32[]{:S(2)}) collective-permute-start(f32[128,128]{1,0:T(8,128)S(1)} %get-tuple-element.40), channel_id=1, source_target_pairs={{0,24},{4,28},{8,0},{12,4},{16,8},{20,12},{24,16},{28,20},{32,56},... | collective-permute-start | bytes 196616 | tf_op jit(solution)/shard_map/ppermute | solution.py:496
  96.9 7.0 %collective-permute-start.9 = (f32[128,128]{1,0:T(8,128)S(1)}, f32[128,128]{1,0:T(8,128)S(1)}, u32[]{:S(2)}, u32[]{:S(2)}) collective-permute-start(f32[128,128]{1,0:T(8,128)S(1)} %get-tuple-element.39), channel_id=1, source_target_pairs={{0,16},{4,20},{8,24},{12,28},{16,0},{20,4},{24,8},{28,12},{32,48},... | collective-permute-start | bytes 196616 | tf_op jit(solution)/shard_map/ppermute | solution.py:496
  106.4 1.2 copy-start.5
  108.8 40.4 %collective-permute-start.10 = (bf16[4096,128]{1,0:T(8,128)(2,1)}, bf16[4096,128]{1,0:T(8,128)(2,1)S(1)}, u32[]{:S(2)}, u32[]{:S(2)}) collective-permute-start(bf16[4096,128]{1,0:T(8,128)(2,1)} %get-tuple-element.36), channel_id=1, source_target_pairs={{0,1},{1,2},{2,3},{3,0},{4,5},{5,6},{6,7},{7,4},{8,9},{9,10},{10,1... | collective-permute-start | bytes 3145736 | tf_op jit(solution)/shard_map/ppermute | solution.py:457
  109.1 40.1 %collective-permute-start.11 = (bf16[4096,128]{1,0:T(8,128)(2,1)S(1)}, bf16[4096,128]{1,0:T(8,128)(2,1)S(1)}, u32[]{:S(2)}, u32[]{:S(2)}) collective-permute-start(bf16[4096,128]{1,0:T(8,128)(2,1)S(1)} %get-tuple-element.37), channel_id=1, source_target_pairs={{0,3},{1,0},{2,1},{3,2},{4,7},{5,4},{6,5},{7,6},{8,11},{9,8},{10,9... | collective-permute-start | bytes 3145736 | tf_op jit(solution)/shard_map/ppermute | solution.py:457
  110.9 18.7 %collective-permute-start.12 = (bf16[128,128]{1,0:T(8,128)(2,1)S(1)}, bf16[128,128]{1,0:T(8,128)(2,1)S(1)}, u32[]{:S(2)}, u32[]{:S(2)}) collective-permute-start(bf16[128,128]{1,0:T(8,128)(2,1)S(1)} %add_y.1.after.p0), channel_id=1, source_target_pairs={{0,32},{4,36},{8,40},{12,44},{16,48},{20,52},{24,56},{28,60},{32,0... | collective-permute-start | bytes 98312 | tf_op jit(solution)/shard_map/ppermute | solution.py:500
  112.2 17.3 %collective-permute-start.13 = (bf16[128,128]{1,0:T(8,128)(2,1)S(1)}, bf16[128,128]{1,0:T(8,128)(2,1)S(1)}, u32[]{:S(2)}, u32[]{:S(2)}) collective-permute-start(bf16[128,128]{1,0:T(8,128)(2,1)S(1)} %add_y.1.after.p0), channel_id=1, source_target_pairs={{0,64},{4,68},{8,72},{12,76},{16,80},{20,84},{24,88},{28,92},{32,9... | collective-permute-start | bytes 98312 | tf_op jit(solution)/shard_map/ppermute | solution.py:500
  114.6 16.8 %collective-permute-start.14 = (bf16[128,128]{1,0:T(8,128)(2,1)S(1)}, bf16[128,128]{1,0:T(8,128)(2,1)S(1)}, u32[]{:S(2)}, u32[]{:S(2)}) collective-permute-start(bf16[128,128]{1,0:T(8,128)(2,1)S(1)} %add_y.1.after.p0), channel_id=1, source_target_pairs={{0,96},{4,100},{8,104},{12,108},{16,112},{20,116},{24,120},{28,124... | collective-permute-start | bytes 98312 | tf_op jit(solution)/shard_map/ppermute | solution.py:500
  131.9 10.6 %collective-permute-start.15 = (bf16[128,128]{1,0:T(8,128)(2,1)S(1)}, bf16[128,128]{1,0:T(8,128)(2,1)S(1)}, u32[]{:S(2)}, u32[]{:S(2)}) collective-permute-start(bf16[128,128]{1,0:T(8,128)(2,1)S(1)} %add_z.1.a), channel_id=1, source_target_pairs={{0,128},{4,132},{8,136},{12,140},{16,144},{20,148},{24,152},{28,15... | collective-permute-start | bytes 98312 | tf_op jit(solution)/shard_map/ppermute | solution.py:500
  135.7 13.5 %copy-start.3 = (bf16[4096,128]{1,0:T(8,128)(2,1)S(1)}, bf16[4096,128]{1,0:T(8,128)(2,1)}, u32[]{:S(2)}) copy-start(bf16[4096,128]{1,0:T(8,128)(2,1)} %get-tuple-element.30.p0) | copy-start | bytes 3145732
  142.6 0.7 copy-start.8
  143.3 8.2 %collective-permute-start.16 = (f32[128,128]{1,0:T(8,128)S(1)}, f32[128,128]{1,0:T(8,128)S(1)}, u32[]{:S(2)}, u32[]{:S(2)}) collective-permute-start(f32[128,128]{1,0:T(8,128)S(1)} %add_pair.1.t0), channel_id=1, source_target_pairs={{0,8},{4,12},{8,16},{12,20},{16,24},{20,28},{24,0},{28,4},{32,40},... | collective-permute-start | bytes 196616 | tf_op jit(solution)/shard_map/ppermute | solution.py:496
  145.0 6.4 %collective-permute-start.17 = (f32[128,128]{1,0:T(8,128)S(1)}, f32[128,128]{1,0:T(8,128)S(1)}, u32[]{:S(2)}, u32[]{:S(2)}) collective-permute-start(f32[128,128]{1,0:T(8,128)S(1)} %add_pair.1.t0), channel_id=1, source_target_pairs={{0,16},{4,20},{8,24},{12,28},{16,0},{20,4},{24,8},{28,12},{32,48},... | collective-permute-start | bytes 196616 | tf_op jit(solution)/shard_map/ppermute | solution.py:496
  147.8 4.3 %collective-permute-start.18 = (f32[128,128]{1,0:T(8,128)S(1)}, f32[128,128]{1,0:T(8,128)S(1)}, u32[]{:S(2)}, u32[]{:S(2)}) collective-permute-start(f32[128,128]{1,0:T(8,128)S(1)} %add_pair.1.t0), channel_id=1, source_target_pairs={{0,24},{4,28},{8,0},{12,4},{16,8},{20,12},{24,16},{28,20},{32,56},... | collective-permute-start | bytes 196616 | tf_op jit(solution)/shard_map/ppermute | solution.py:496
  149.3 0.7 copy-start.9

commit v4 on v3

--- a/solution.py
+++ b/solution.py
@@ -52,31 +52,32 @@
 MASK_STEP = 2048
 TILES = 176
 PIECES = 4
-PIECE = TILES // PIECES
-
-
-def tile_copies(tiles_hbm, tiles, sems):
+BACK_PIECES = 2
+
+
+def tile_copies(tiles_hbm, tiles, sems, pieces):
+    size = TILES // pieces
     return [
         pltpu.make_async_copy(
-            tiles_hbm.at[pl.ds(k * PIECE, PIECE)], tiles.at[pl.ds(k * PIECE, PIECE)], sems.at[k]
+            tiles_hbm.at[pl.ds(k * size, size)], tiles.at[pl.ds(k * size, size)], sems.at[k]
         )
-        for k in range(PIECES)
+        for k in range(pieces)
     ]
 
 
 def tiles_bwd_kernel(count_ref, rows_ref, cols_ref, bits_hbm, cot_hbm, tiles_hbm, own_hbm,
                      slot_hbm, tiles, bits, cot, d_t, acc, slots, sems, out_sems):
     count = count_ref[0]
-    bits_in = pltpu.make_async_copy(bits_hbm, bits, sems.at[PIECES])
+    bits_in = pltpu.make_async_copy(bits_hbm, bits, sems.at[BACK_PIECES])
     steps = [pl.ds(i * MASK_STEP, MASK_STEP) for i in range(4096 // MASK_STEP)]
     cot_in = [
-        pltpu.make_async_copy(cot_hbm.at[r], cot.at[r], sems.at[PIECES + 1 + i])
+        pltpu.make_async_copy(cot_hbm.at[r], cot.at[r], sems.at[BACK_PIECES + 1 + i])
         for i, r in enumerate(steps)
     ]
     bits_in.start()
     for c in cot_in:
         c.start()
-    copies = tile_copies(tiles_hbm, tiles, sems)
+    copies = tile_copies(tiles_hbm, tiles, sems, BACK_PIECES)
     for c in copies:
         c.start()
     acc[...] = jnp.zeros_like(acc)
@@ -88,10 +89,10 @@
         v = jnp.where(active, cot[r, :].astype(F32), 0.0)
         for j in range(MASK_STEP // B):
             d_t[i * (MASK_STEP // B) + j] = v[j * B : (j + 1) * B].T.astype(BF16)
-    for k in range(PIECES):
+    for k in range(BACK_PIECES):
         copies[k].wait()
 
-        for t in range(k * PIECE, (k + 1) * PIECE):
+        for t in range(k * TILES // BACK_PIECES, (k + 1) * TILES // BACK_PIECES):
             s = jnp.where(t < count, cols_ref[0, t], RB + 64)
             acc[s] += dot(d_t[rows_ref[0, t]], tiles[t])
     outs = [pltpu.make_async_copy(acc.at[pl.ds(0, RB)], own_hbm, out_sems.at[4])]
@@ -121,7 +122,7 @@
             pltpu.VMEM((RB, B, B), BF16),
             pltpu.VMEM((RB + 65, B, B), F32),
             pltpu.VMEM((64, B, B), BF16),
-            pltpu.SemaphoreType.DMA((PIECES + 3,)),
+            pltpu.SemaphoreType.DMA((BACK_PIECES + 3,)),
             pltpu.SemaphoreType.DMA((5,)),
         ],
         compiler_params=params(),
@@ -150,14 +151,14 @@
 
 
 def tiles_fwd_kernel(count_ref, rows_ref, cols_ref, mask_hbm, own_hbm, recv_hbm, tiles_hbm,
-                     out_ref, token, tiles, src, acc, active, sems):
+                     out_hbm, token, tiles, src, acc, active, out, sems, out_sems):
     count = count_ref[0]
     own = pltpu.make_async_copy(own_hbm, src.at[pl.ds(0, RB)], sems.at[PIECES])
     got = pltpu.make_async_copy(recv_hbm, src.at[pl.ds(RB, 64)], sems.at[PIECES + 1])
     mask_in = pltpu.make_async_copy(mask_hbm, active, sems.at[PIECES + 2])
     own.start()
     got.start()
-    copies = tile_copies(tiles_hbm, tiles, sems)
+    copies = tile_copies(tiles_hbm, tiles, sems, PIECES)
     for c in copies:
         c.start()
     mask_in.start()
@@ -167,16 +168,23 @@
     for k in range(PIECES):
         copies[k].wait()
 
-        for t in range(k * PIECE, (k + 1) * PIECE):
+        for t in range(k * TILES // PIECES, (k + 1) * TILES // PIECES):
             r = jnp.where(t < count, rows_ref[0, t], RB)
             acc[r] += dot(tiles[t], src[cols_ref[0, t]])
 
     token[...] = jnp.zeros_like(token)
     mask_in.wait()
 
-    for b in range(RB):
-        keep = active[b * B : (b + 1) * B, :].astype(F32) > 0.5
-        out_ref[b] = jnp.where(keep, acc[b], 0.0).astype(BF16)
+    outs = []
+    for k in range(4):
+        at = pl.ds(k * CHUNK, CHUNK)
+        for b in range(k * CHUNK, (k + 1) * CHUNK):
+            keep = active[b * B : (b + 1) * B, :].astype(F32) > 0.5
+            out[b] = jnp.where(keep, acc[b], 0.0).astype(BF16)
+        outs.append(pltpu.make_async_copy(out.at[at], out_hbm.at[at], out_sems.at[k]))
+        outs[-1].start()
+    for c in outs:
+        c.wait()
 
 
 def tiles_fwd_call(count, rows, cols, mask, own, recv, tiles):
@@ -184,13 +192,15 @@
         tiles_fwd_kernel,
         out_shape=[jax.ShapeDtypeStruct((RB, B, B), BF16), jax.ShapeDtypeStruct((8, B), F32)],
         in_specs=[SMEM] * 3 + [ANY] * 4,
-        out_specs=[VMEM] * 2,
+        out_specs=[HBM, VMEM],
         scratch_shapes=[
             pltpu.VMEM((TILES, B, B), BF16),
             pltpu.VMEM((RB + 64, B, B), BF16),
             pltpu.VMEM((RB + 1, B, B), F32),
             pltpu.VMEM((4096, B), BF16),
+            pltpu.VMEM((RB, B, B), BF16),
             pltpu.SemaphoreType.DMA((PIECES + 3,)),
+            pltpu.SemaphoreType.DMA((4,)),
         ],
         compiler_params=params(58),
         cost_estimate=cost(2 * TILES * B * B * B, 30 << 20),
@@ -532,7 +542,7 @@
     out_act, token = tiles_fwd_call(count, rows, cols, mask, hidden, incoming, tiles)
     total = pair_call(total, swap_z(total, 4), token)
     weight_grad = finish_call(me, [total] + [shift_dom(total, 0, k, 0) for k in range(1, 4)])
-    input_grad = parts_call(parts, token)
+    input_grad = parts_call(parts, total)
     return out_act.reshape(4096, B), input_grad, weight_grad
 
 

time: 154 us -> 154 us (level)
    unnamed x30 -> x28, local copies, waits for them, and re-layouts: 5.87 us -> 5.18 us
  transfers between devices with their start and end apart: 21 -> 21, of which waited for: 13 -> 14; matrix products, arithmetic and copies ran while one was open for 1% -> 1% of each run, Pallas kernels for 17% -> 17%
where the time goes in v4:
time: 154 us
  waiting for transfers between devices  61.9 us (40%)
  starting transfers between devices  48.8 us (32%)
  Pallas kernels  34.6 us (22%)
  local copies, waits for them, and re-layouts  5.2 us (3%)
  other arithmetic  1.55 us (1%)
    ppermute x8, waiting for transfers between devices, shift_hid(): return lax.ppermute(v, 'hid', [(i, (i + s) % HID) for i in range(HID)])  36.7 us
    all_to_all x2, starting transfers between devices, all_to_all(): return lax.all_to_all(v, 'dom', split_axis=0, concat_axis=0, tiled=True)  21.2 us
    ppermute x4, waiting for transfers between devices, swap_z(): return lax.ppermute(v, 'dom', [(i, i ^ 8 * k) for i in range(64)])  16.1 us
    ppermute x7, starting transfers between devices, shift_dom(): return lax.ppermute(v, 'dom', pairs)  11.1 us
    pallas_call x1, Pallas kernels, sum_call(): pl.pallas_call(sum_kernel, out_shape=[jax.ShapeDtypeStruct((512, B), F32)...  9.15 us
    ppermute x8, starting transfers between devices, shift_hid(): return lax.ppermute(v, 'hid', [(i, (i + s) % HID) for i in range(HID)])  8.26 us
    ppermute x4, starting transfers between devices, swap_z(): return lax.ppermute(v, 'dom', [(i, i ^ 8 * k) for i in range(64)])  8.19 us
    pallas_call x1, Pallas kernels, tiles_fwd_call(): pl.pallas_call(tiles_fwd_kernel, out_shape=[jax.ShapeDtypeStruct((RB, B,...  7.21 us
  transfers between devices with their start and end apart: 21, of which 14 were waited for; matrix products, arithmetic and copies ran while one was open for 1% of the time, Pallas kernels for 17%

profile of v4, /device:TPU:6, one launch (start us, length us, event | category | flops | bytes accessed | tf_op | source)
XLA Modules:
  0.0 153.5 jit_solution(15792108162704241600)
XLA Ops:
  1.3 7.2 %tiles_bwd.1 = (f32[32,128,128]{2,1,0:T(8,128)}, bf16[64,128,128]{2,1,0:T(8,128)(2,1)}) custom-call(s32[1]{0:T(128)S(6)} %copy.12.count_ref, s32[1,176]{1,0:T(1,128)} %rows_ref.3, s32[1,176]{1,0:T(1,128)} %cols_ref.3, s32[8,4096]{1,0:T(8,128)} %bitcast.5, bf16[4096,128]{1,0:T(8,128)(2,1)} %cot_hbm.1, bf16[176,128,128]{2,1,0:T(8,128)(2,1)} %tiles_hbm.3), custom_call_target="tpu_custom_call" | custom-call | flops 738197504 | bytes 31457280 | tf_op jit(solution)/shard_map/tiles_bwd/pallas_call | solution.py:110
  8.5 12.6 %all-to-all-start.1 = ((bf16[64,128,128]{2,1,0:T(8,128)(2,1)}), bf16[64,128,128]{2,1,0:T(8,128)(2,1)}, u32[]{:S(2)}, u32[]{:S(2)}) async-start(bf16[64,128,128]{2,1,0:T(8,128)(2,1)} %get-tuple-element.22.after), calls=%async_computation.1 | async-start | bytes 4194304 | tf_op jit(solution)/shard_map/all_to_all | solution.py:514
  21.2 0.6 collective-permute-start
  21.7 1.6 %collective-permute-start.1 = (bf16[4096,128]{1,0:T(8,128)(2,1)S(1)}, bf16[4096,128]{1,0:T(8,128)(2,1)S(1)}, u32[]{:S(2)}, u32[]{:S(2)}) collective-permute-start(bf16[4096,128]{1,0:T(8,128)(2,1)S(1)} %copy-done.11), channel_id=1, source_target_pairs={{0,3},{1,0},{2,1},{3,2},{4,7},{5,4},{6,5},{7,6},{8,11},{9,8},{10,9... | collective-permute-start | bytes 3145736 | tf_op jit(solution)/shard_map/ppermute | solution.py:467
  23.3 23.0 %collective-permute-done.v1.x1 = bf16[4096,128]{1,0:T(8,128)(2,1)S(1)} collective-permute-done((bf16[4096,128]{1,0:T(8,128)(2,1)S(1)}, bf16[4096,128]{1,0:T(8,128)(2,1)S(1)}, u32[]{:S(2)}, u32[]{:S(2)}) %collective-permute-start) | collective-permute-done | bytes 1048608 | tf_op jit(solution)/shard_map/ppermute | solution.py:467
  46.3 1.4 collective-permute-done.1.v3.x3
  47.8 0.9 copy-done.1
  48.7 0.6 collective-permute-start.2
  49.3 1.4 collective-permute-start.3
  50.7 0.6 active.1
  51.3 1.0 copy-done.6
  52.3 0.6 copy-done.10
  52.9 0.6 pad_add_fusion.me_ref
  53.4 8.0 %collective-permute-done.2.x2a = bf16[2048,128]{1,0:T(8,128)(2,1)S(1)} collective-permute-done((bf16[2048,128]{1,0:T(8,128)(2,1)S(1)}, bf16[2048,128]{1,0:T(8,128)(2,1)S(1)}, u32[]{:S(2)}, u32[]{:S(2)}) %collective-permute-start.2) | collective-permute-done | bytes 524320 | tf_op jit(solution)/shard_map/ppermute | solution.py:467
  61.4 1.9 %collective-permute-done.3.x2b = bf16[2048,128]{1,0:T(8,128)(2,1)S(1)} collective-permute-done((bf16[2048,128]{1,0:T(8,128)(2,1)S(1)}, bf16[2048,128]{1,0:T(8,128)(2,1)S(1)}, u32[]{:S(2)}, u32[]{:S(2)}) %collective-permute-start.3) | collective-permute-done | bytes 524320 | tf_op jit(solution)/shard_map/ppermute | solution.py:467
  63.3 0.8 copy-done.13
  64.1 5.8 %hidden.1 = (bf16[32,128,128]{2,1,0:T(8,128)(2,1)}, bf16[64,128,128]{2,1,0:T(8,128)(2,1)}) custom-call(s32[3]{0:T(128)} %pad_add_fusion.me_ref, s32[1,64]{1,0:T(1,128)} %send_ref.3, bf16[4096,128]{1,0:T(8,128)(2,1)} %x0.3, bf16[4096,128]{1,0:T(8,128)(2,1)} %copy-done, bf16[2048,128]{1,0:T(8,128)(2,1)} %copy-done.12, bf16[2048,128]{1,0:T(8,128)(2,1)} %copy-done.13, ...), custom_call_target="tpu_custom_call" | custom-call | flops 536870912 | bytes 10485760 | tf_op jit(solution)/shard_map/hidden/pallas_call | solution.py:234
  69.9 2.4 %all-to-all-done.1.got_hbm = bf16[64,128,128]{2,1,0:T(8,128)(2,1)} async-done(((bf16[64,128,128]{2,1,0:T(8,128)(2,1)}), bf16[64,128,128]{2,1,0:T(8,128)(2,1)}, u32[]{:S(2)}, u32[]{:S(2)}) %all-to-all-start.1) | async-done | bytes 2097184 | tf_op jit(solution)/shard_map/all_to_all | solution.py:514
  72.3 8.6 %all-to-all-start = ((bf16[64,128,128]{2,1,0:T(8,128)(2,1)}), bf16[64,128,128]{2,1,0:T(8,128)(2,1)}, u32[]{:S(2)}, u32[]{:S(2)}) async-start(bf16[64,128,128]{2,1,0:T(8,128)(2,1)} %get-tuple-element.27.after), calls=%async_computation | async-start | bytes 4194304 | tf_op jit(solution)/shard_map/all_to_all | solution.py:514
  81.0 9.1 %sum_returned.1 = (f32[512,128]{1,0:T(8,128)}, bf16[4096,128]{1,0:T(8,128)(2,1)}, bf16[4096,128]{1,0:T(8,128)(2,1)}, bf16[2048,128]{1,0:T(8,128)(2,1)}, bf16[204...) custom-call(s32[3]{0:T(128)} %pad_add_fusion.me_ref, s32[1,64]{1,0:T(1,128)} %send_ref.3, ...), custom_call_target="tpu_custom_call" | custom-call | flops 536870912 | bytes 12582912 | tf_op jit(solution)/shard_map/sum_returned/pallas_call | solution.py:315
  90.8 1.6 %collective-permute-start.5 = (bf16[2048,128]{1,0:T(8,128)(2,1)}, bf16[2048,128]{1,0:T(8,128)(2,1)S(1)}, u32[]{:S(2)}, u32[]{:S(2)}) collective-permute-start(bf16[2048,128]{1,0:T(8,128)(2,1)} %get-tuple-element.34), channel_id=1, source_target_pairs={{0,3},{1,0},{2,1},{3,2},{4,7},{5,4},{6,5},{7,6},{8,11},{9,8},{10,9... | collective-permute-start | bytes 1572872 | tf_op jit(solution)/shard_map/ppermute | solution.py:467
  92.3 1.0 add.10
  93.4 1.5 collective-permute-start.7
  94.8 1.8 %collective-permute-start.8 = (f32[128,128]{1,0:T(8,128)S(1)}, f32[128,128]{1,0:T(8,128)S(1)}, u32[]{:S(2)}, u32[]{:S(2)}) collective-permute-start(f32[128,128]{1,0:T(8,128)S(1)} %get-tuple-element.40), channel_id=1, source_target_pairs={{0,24},{4,28},{8,0},{12,4},{16,8},{20,12},{24,16},{28,20},{32,56},... | collective-permute-start | bytes 196616 | tf_op jit(solution)/shard_map/ppermute | solution.py:506
  96.7 1.7 %collective-permute-start.9 = (f32[128,128]{1,0:T(8,128)S(1)}, f32[128,128]{1,0:T(8,128)S(1)}, u32[]{:S(2)}, u32[]{:S(2)}) collective-permute-start(f32[128,128]{1,0:T(8,128)S(1)} %get-tuple-element.39), channel_id=1, source_target_pairs={{0,16},{4,20},{8,24},{12,28},{16,0},{20,4},{24,8},{28,12},{32,48},... | collective-permute-start | bytes 196616 | tf_op jit(solution)/shard_map/ppermute | solution.py:506
  98.4 1.5 collective-permute-done.7.b
  99.8 0.6 collective-permute-done.8.c
  100.4 3.2 %collective-permute-done.9.d = f32[128,128]{1,0:T(8,128)S(1)} collective-permute-done((f32[128,128]{1,0:T(8,128)S(1)}, f32[128,128]{1,0:T(8,128)S(1)}, u32[]{:S(2)}, u32[]{:S(2)}) %collective-permute-start.9) | collective-permute-done | bytes 65568 | tf_op jit(solution)/shard_map/ppermute | solution.py:506
  103.7 1.1 collective-permute-done.4.low
  104.8 1.4 collective-permute-done.5.high
  106.2 1.2 copy-done.4
  107.4 1.2 relay.1
  108.9 1.7 %collective-permute-start.11 = (bf16[4096,128]{1,0:T(8,128)(2,1)S(1)}, bf16[4096,128]{1,0:T(8,128)(2,1)S(1)}, u32[]{:S(2)}, u32[]{:S(2)}) collective-permute-start(bf16[4096,128]{1,0:T(8,128)(2,1)S(1)} %get-tuple-element.37), channel_id=1, source_target_pairs={{0,3},{1,0},{2,1},{3,2},{4,7},{5,4},{6,5},{7,6},{8,11},{9,8},{10,9... | collective-permute-start | bytes 3145736 | tf_op jit(solution)/shard_map/ppermute | solution.py:467
  110.6 1.3 collective-permute-start.12
  111.9 2.4 %collective-permute-start.13 = (bf16[128,128]{1,0:T(8,128)(2,1)S(1)}, bf16[128,128]{1,0:T(8,128)(2,1)S(1)}, u32[]{:S(2)}, u32[]{:S(2)}) collective-permute-start(bf16[128,128]{1,0:T(8,128)(2,1)S(1)} %add_y.1.after.p0), channel_id=1, source_target_pairs={{0,64},{4,68},{8,72},{12,76},{16,80},{20,84},{24,88},{28,92},{32,9... | collective-permute-start | bytes 98312 | tf_op jit(solution)/shard_map/ppermute | solution.py:510
  114.3 0.7 collective-permute-start.14
  115.0 14.3 %collective-permute-done.12.p1 = bf16[128,128]{1,0:T(8,128)(2,1)S(1)} collective-permute-done((bf16[128,128]{1,0:T(8,128)(2,1)S(1)}, bf16[128,128]{1,0:T(8,128)(2,1)S(1)}, u32[]{:S(2)}, u32[]{:S(2)}) %collective-permute-start.12) | collective-permute-done | bytes 32800 | tf_op jit(solution)/shard_map/ppermute | solution.py:510
  129.3 1.8 %collective-permute-done.14.p3 = bf16[128,128]{1,0:T(8,128)(2,1)S(1)} collective-permute-done((bf16[128,128]{1,0:T(8,128)(2,1)S(1)}, bf16[128,128]{1,0:T(8,128)(2,1)S(1)}, u32[]{:S(2)}, u32[]{:S(2)}) %collective-permute-start.14) | collective-permute-done | bytes 32800 | tf_op jit(solution)/shard_map/ppermute | solution.py:510
  131.1 0.6 add_z.1.a
  131.7 3.8 %collective-permute-start.15 = (bf16[128,128]{1,0:T(8,128)(2,1)S(1)}, bf16[128,128]{1,0:T(8,128)(2,1)S(1)}, u32[]{:S(2)}, u32[]{:S(2)}) collective-permute-start(bf16[128,128]{1,0:T(8,128)(2,1)S(1)} %add_z.1.a), channel_id=1, source_target_pairs={{0,128},{4,132},{8,136},{12,140},{16,144},{20,148},{24,152},{28,15... | collective-permute-start | bytes 98312 | tf_op jit(solution)/shard_map/ppermute | solution.py:510
  135.5 7.2 %tiles_fwd.1 = (bf16[32,128,128]{2,1,0:T(8,128)(2,1)}, f32[8,128]{1,0:T(8,128)}) custom-call(s32[1]{0:T(128)S(6)} %copy.12.count_ref, s32[1,176]{1,0:T(1,128)} %rows_ref.3, s32[1,176]{1,0:T(1,128)} %cols_ref.3, bf16[4096,128]{1,0:T(8,128)(2,1)} %copy-done.6, bf16[32,128,128]{2,1,0:T(8,128)(2,1)} %get-tuple-element.26.own_hbm, ...), custom_call_target="tpu_custom_call" | custom-call | flops 738197504 | bytes 31457280 | tf_op jit(solution)/shard_map/tiles_fwd/pallas_call | solution.py:191
  142.8 0.7 copy-done.9
  143.4 1.8 %collective-permute-start.16 = (f32[128,128]{1,0:T(8,128)S(1)}, f32[128,128]{1,0:T(8,128)S(1)}, u32[]{:S(2)}, u32[]{:S(2)}) collective-permute-start(f32[128,128]{1,0:T(8,128)S(1)} %add_pair.1.after.t0), channel_id=1, source_target_pairs={{0,8},{4,12},{8,16},{12,20},{16,24},{20,28},{24,0},{28,4},{32,40},... | collective-permute-start | bytes 196616 | tf_op jit(solution)/shard_map/ppermute | solution.py:506
  145.2 2.8 %collective-permute-start.17 = (f32[128,128]{1,0:T(8,128)S(1)}, f32[128,128]{1,0:T(8,128)S(1)}, u32[]{:S(2)}, u32[]{:S(2)}) collective-permute-start(f32[128,128]{1,0:T(8,128)S(1)} %add_pair.1.after.t0), channel_id=1, source_target_pairs={{0,16},{4,20},{8,24},{12,28},{16,0},{20,4},{24,8},{28,12},{32,48},... | collective-permute-start | bytes 196616 | tf_op jit(solution)/shard_map/ppermute | solution.py:506
  148.0 1.4 collective-permute-start.18
  149.4 1.5 add_parts.1
  151.0 1.2 collective-permute-done.18.t3
  152.3 1.3 finish.1
  (37 shorter events, 1.2 us)
Async XLA Ops:
  8.5 12.7 %copy-start.11 = (bf16[4096,128]{1,0:T(8,128)(2,1)S(1)}, bf16[4096,128]{1,0:T(8,128)(2,1)}, u32[]{:S(2)}) copy-start(bf16[4096,128]{1,0:T(8,128)(2,1)} %x0.3) | copy-start | bytes 3145732
  8.5 39.2 %copy-start.2 = (bf16[64,128,128]{2,1,0:T(8,128)(2,1)S(1)}, bf16[64,128,128]{2,1,0:T(8,128)(2,1)}, u32[]{:S(2)}) copy-start(bf16[64,128,128]{2,1,0:T(8,128)(2,1)} %get-tuple-element.22.after) | copy-start | bytes 6291460
  8.5 63.9 %all-to-all-start.1 = ((bf16[64,128,128]{2,1,0:T(8,128)(2,1)}), bf16[64,128,128]{2,1,0:T(8,128)(2,1)}, u32[]{:S(2)}, u32[]{:S(2)}) async-start(bf16[64,128,128]{2,1,0:T(8,128)(2,1)} %get-tuple-element.22.after), calls=%async_computation.1 | async-start | bytes 4194304 | tf_op jit(solution)/shard_map/all_to_all | solution.py:514
  21.2 29.6 %copy-start.7 = (s32[4096,8]{0,1:T(8,128)S(1)}, s32[4096,8]{0,1:T(8,128)}, u32[]{:S(2)}) copy-start(s32[4096,8]{0,1:T(8,128)} %param.16) | copy-start | bytes 393220
  21.2 25.1 %collective-permute-start = (bf16[4096,128]{1,0:T(8,128)(2,1)S(1)}, bf16[4096,128]{1,0:T(8,128)(2,1)S(1)}, u32[]{:S(2)}, u32[]{:S(2)}) collective-permute-start(bf16[4096,128]{1,0:T(8,128)(2,1)S(1)} %copy-done.11), channel_id=1, source_target_pairs={{0,1},{1,2},{2,3},{3,0},{4,5},{5,6},{6,7},{7,4},{8,9},{9,10},{10,1... | collective-permute-start | bytes 3145736 | tf_op jit(solution)/shard_map/ppermute | solution.py:467
  21.7 26.0 %collective-permute-start.1 = (bf16[4096,128]{1,0:T(8,128)(2,1)S(1)}, bf16[4096,128]{1,0:T(8,128)(2,1)S(1)}, u32[]{:S(2)}, u32[]{:S(2)}) collective-permute-start(bf16[4096,128]{1,0:T(8,128)(2,1)S(1)} %copy-done.11), channel_id=1, source_target_pairs={{0,3},{1,0},{2,1},{3,2},{4,7},{5,4},{6,5},{7,6},{8,11},{9,8},{10,9... | collective-permute-start | bytes 3145736 | tf_op jit(solution)/shard_map/ppermute | solution.py:467
  46.3 1.5 copy-start
  47.7 1.0 copy-start.1
  48.7 12.7 %collective-permute-start.2 = (bf16[2048,128]{1,0:T(8,128)(2,1)S(1)}, bf16[2048,128]{1,0:T(8,128)(2,1)S(1)}, u32[]{:S(2)}, u32[]{:S(2)}) collective-permute-start(bf16[2048,128]{1,0:T(8,128)(2,1)S(1)} %get-tuple-element.23), channel_id=1, source_target_pairs={{0,1},{1,2},{2,3},{3,0},{4,5},{5,6},{6,7},{7,4},{8,9},{9,10},{10,1... | collective-permute-start | bytes 1572872 | tf_op jit(solution)/shard_map/ppermute | solution.py:467
  49.3 14.0 %collective-permute-start.3 = (bf16[2048,128]{1,0:T(8,128)(2,1)S(1)}, bf16[2048,128]{1,0:T(8,128)(2,1)S(1)}, u32[]{:S(2)}, u32[]{:S(2)}) collective-permute-start(bf16[2048,128]{1,0:T(8,128)(2,1)S(1)} %get-tuple-element.24), channel_id=1, source_target_pairs={{0,3},{1,0},{2,1},{3,2},{4,7},{5,4},{6,5},{7,6},{8,11},{9,8},{10,9... | collective-permute-start | bytes 1572872 | tf_op jit(solution)/shard_map/ppermute | solution.py:467
  51.3 1.0 copy-start.6
  52.3 0.6 copy-start.10
  61.4 1.9 %copy-start.12 = (bf16[2048,128]{1,0:T(8,128)(2,1)}, bf16[2048,128]{1,0:T(8,128)(2,1)S(1)}, u32[]{:S(2)}) copy-start(bf16[2048,128]{1,0:T(8,128)(2,1)S(1)} %collective-permute-done.2.x2a) | copy-start | bytes 1572868
  63.3 0.8 copy-start.13
  72.3 63.2 %all-to-all-start = ((bf16[64,128,128]{2,1,0:T(8,128)(2,1)}), bf16[64,128,128]{2,1,0:T(8,128)(2,1)}, u32[]{:S(2)}, u32[]{:S(2)}) async-start(bf16[64,128,128]{2,1,0:T(8,128)(2,1)} %get-tuple-element.27.after), calls=%async_computation | async-start | bytes 4194304 | tf_op jit(solution)/shard_map/all_to_all | solution.py:514
  90.1 16.0 %copy-start.3 = (bf16[4096,128]{1,0:T(8,128)(2,1)S(1)}, bf16[4096,128]{1,0:T(8,128)(2,1)}, u32[]{:S(2)}) copy-start(bf16[4096,128]{1,0:T(8,128)(2,1)} %get-tuple-element.31.p1) | copy-start | bytes 3145732
  90.1 2.2 %collective-permute-start.6 = (f32[512,128]{1,0:T(8,128)}, f32[512,128]{1,0:T(8,128)S(1)}, u32[]{:S(2)}, u32[]{:S(2)}) collective-permute-start(f32[512,128]{1,0:T(8,128)} %get-tuple-element.35), channel_id=1, source_target_pairs={{0,4},{4,0},{8,12},{12,8},{16,20},{20,16},{24,28},{28,24},{32,36},... | collective-permute-start | bytes 786440 | tf_op jit(solution)/shard_map/ppermute | solution.py:506
  90.2 14.6 %collective-permute-start.4 = (bf16[2048,128]{1,0:T(8,128)(2,1)}, bf16[2048,128]{1,0:T(8,128)(2,1)S(1)}, u32[]{:S(2)}, u32[]{:S(2)}) collective-permute-start(bf16[2048,128]{1,0:T(8,128)(2,1)} %get-tuple-element.33), channel_id=1, source_target_pairs={{0,1},{1,2},{2,3},{3,0},{4,5},{5,6},{6,7},{7,4},{8,9},{9,10},{10,1... | collective-permute-start | bytes 1572872 | tf_op jit(solution)/shard_map/ppermute | solution.py:467
  90.8 15.4 %collective-permute-start.5 = (bf16[2048,128]{1,0:T(8,128)(2,1)}, bf16[2048,128]{1,0:T(8,128)(2,1)S(1)}, u32[]{:S(2)}, u32[]{:S(2)}) collective-permute-start(bf16[2048,128]{1,0:T(8,128)(2,1)} %get-tuple-element.34), channel_id=1, source_target_pairs={{0,3},{1,0},{2,1},{3,2},{4,7},{5,4},{6,5},{7,6},{8,11},{9,8},{10,9... | collective-permute-start | bytes 1572872 | tf_op jit(solution)/shard_map/ppermute | solution.py:467
  93.3 37.8 %copy-start.8 = (s32[3]{0:T(128)S(1)}, s32[3]{0:T(128)}, u32[]{:S(2)}) copy-start(s32[3]{0:T(128)} %pad_add_fusion.me_ref) | copy-start | bytes 40
  93.4 6.5 %collective-permute-start.7 = (f32[128,128]{1,0:T(8,128)S(1)}, f32[128,128]{1,0:T(8,128)S(1)}, u32[]{:S(2)}, u32[]{:S(2)}) collective-permute-start(f32[128,128]{1,0:T(8,128)S(1)} %get-tuple-element.41), channel_id=1, source_target_pairs={{0,8},{4,12},{8,16},{12,20},{16,24},{20,28},{24,0},{28,4},{32,40},... | collective-permute-start | bytes 196616 | tf_op jit(solution)/shard_map/ppermute | solution.py:506
  94.8 5.6 %collective-permute-start.8 = (f32[128,128]{1,0:T(8,128)S(1)}, f32[128,128]{1,0:T(8,128)S(1)}, u32[]{:S(2)}, u32[]{:S(2)}) collective-permute-start(f32[128,128]{1,0:T(8,128)S(1)} %get-tuple-element.40), channel_id=1, source_target_pairs={{0,24},{4,28},{8,0},{12,4},{16,8},{20,12},{24,16},{28,20},{32,56},... | collective-permute-start | bytes 196616 | tf_op jit(solution)/shard_map/ppermute | solution.py:506
  96.7 7.0 %collective-permute-start.9 = (f32[128,128]{1,0:T(8,128)S(1)}, f32[128,128]{1,0:T(8,128)S(1)}, u32[]{:S(2)}, u32[]{:S(2)}) collective-permute-start(f32[128,128]{1,0:T(8,128)S(1)} %get-tuple-element.39), channel_id=1, source_target_pairs={{0,16},{4,20},{8,24},{12,28},{16,0},{20,4},{24,8},{28,12},{32,48},... | collective-permute-start | bytes 196616 | tf_op jit(solution)/shard_map/ppermute | solution.py:506
  106.2 1.2 copy-start.4
  108.6 40.8 %collective-permute-start.10 = (bf16[4096,128]{1,0:T(8,128)(2,1)}, bf16[4096,128]{1,0:T(8,128)(2,1)S(1)}, u32[]{:S(2)}, u32[]{:S(2)}) collective-permute-start(bf16[4096,128]{1,0:T(8,128)(2,1)} %get-tuple-element.36), channel_id=1, source_target_pairs={{0,1},{1,2},{2,3},{3,0},{4,5},{5,6},{6,7},{7,4},{8,9},{9,10},{10,1... | collective-permute-start | bytes 3145736 | tf_op jit(solution)/shard_map/ppermute | solution.py:467
  108.9 40.6 %collective-permute-start.11 = (bf16[4096,128]{1,0:T(8,128)(2,1)S(1)}, bf16[4096,128]{1,0:T(8,128)(2,1)S(1)}, u32[]{:S(2)}, u32[]{:S(2)}) collective-permute-start(bf16[4096,128]{1,0:T(8,128)(2,1)S(1)} %get-tuple-element.37), channel_id=1, source_target_pairs={{0,3},{1,0},{2,1},{3,2},{4,7},{5,4},{6,5},{7,6},{8,11},{9,8},{10,9... | collective-permute-start | bytes 3145736 | tf_op jit(solution)/shard_map/ppermute | solution.py:467
  110.6 18.7 %collective-permute-start.12 = (bf16[128,128]{1,0:T(8,128)(2,1)S(1)}, bf16[128,128]{1,0:T(8,128)(2,1)S(1)}, u32[]{:S(2)}, u32[]{:S(2)}) collective-permute-start(bf16[128,128]{1,0:T(8,128)(2,1)S(1)} %add_y.1.after.p0), channel_id=1, source_target_pairs={{0,32},{4,36},{8,40},{12,44},{16,48},{20,52},{24,56},{28,60},{32,0... | collective-permute-start | bytes 98312 | tf_op jit(solution)/shard_map/ppermute | solution.py:510
  111.9 17.3 %collective-permute-start.13 = (bf16[128,128]{1,0:T(8,128)(2,1)S(1)}, bf16[128,128]{1,0:T(8,128)(2,1)S(1)}, u32[]{:S(2)}, u32[]{:S(2)}) collective-permute-start(bf16[128,128]{1,0:T(8,128)(2,1)S(1)} %add_y.1.after.p0), channel_id=1, source_target_pairs={{0,64},{4,68},{8,72},{12,76},{16,80},{20,84},{24,88},{28,92},{32,9... | collective-permute-start | bytes 98312 | tf_op jit(solution)/shard_map/ppermute | solution.py:510
  114.3 16.8 %collective-permute-start.14 = (bf16[128,128]{1,0:T(8,128)(2,1)S(1)}, bf16[128,128]{1,0:T(8,128)(2,1)S(1)}, u32[]{:S(2)}, u32[]{:S(2)}) collective-permute-start(bf16[128,128]{1,0:T(8,128)(2,1)S(1)} %add_y.1.after.p0), channel_id=1, source_target_pairs={{0,96},{4,100},{8,104},{12,108},{16,112},{20,116},{24,120},{28,124... | collective-permute-start | bytes 98312 | tf_op jit(solution)/shard_map/ppermute | solution.py:510
  131.7 11.0 %collective-permute-start.15 = (bf16[128,128]{1,0:T(8,128)(2,1)S(1)}, bf16[128,128]{1,0:T(8,128)(2,1)S(1)}, u32[]{:S(2)}, u32[]{:S(2)}) collective-permute-start(bf16[128,128]{1,0:T(8,128)(2,1)S(1)} %add_z.1.a), channel_id=1, source_target_pairs={{0,128},{4,132},{8,136},{12,140},{16,144},{20,148},{24,152},{28,15... | collective-permute-start | bytes 98312 | tf_op jit(solution)/shard_map/ppermute | solution.py:510
  135.5 13.9 %copy-start.5 = (bf16[4096,128]{1,0:T(8,128)(2,1)S(1)}, bf16[4096,128]{1,0:T(8,128)(2,1)}, u32[]{:S(2)}) copy-start(bf16[4096,128]{1,0:T(8,128)(2,1)} %get-tuple-element.30.p0) | copy-start | bytes 3145732
  142.7 0.7 copy-start.9
  143.4 7.5 %collective-permute-start.16 = (f32[128,128]{1,0:T(8,128)S(1)}, f32[128,128]{1,0:T(8,128)S(1)}, u32[]{:S(2)}, u32[]{:S(2)}) collective-permute-start(f32[128,128]{1,0:T(8,128)S(1)} %add_pair.1.after.t0), channel_id=1, source_target_pairs={{0,8},{4,12},{8,16},{12,20},{16,24},{20,28},{24,0},{28,4},{32,40},... | collective-permute-start | bytes 196616 | tf_op jit(solution)/shard_map/ppermute | solution.py:506
  145.2 5.8 %collective-permute-start.17 = (f32[128,128]{1,0:T(8,128)S(1)}, f32[128,128]{1,0:T(8,128)S(1)}, u32[]{:S(2)}, u32[]{:S(2)}) collective-permute-start(f32[128,128]{1,0:T(8,128)S(1)} %add_pair.1.after.t0), channel_id=1, source_target_pairs={{0,16},{4,20},{8,24},{12,28},{16,0},{20,4},{24,8},{28,12},{32,48},... | collective-permute-start | bytes 196616 | tf_op jit(solution)/shard_map/ppermute | solution.py:506
  148.0 4.3 %collective-permute-start.18 = (f32[128,128]{1,0:T(8,128)S(1)}, f32[128,128]{1,0:T(8,128)S(1)}, u32[]{:S(2)}, u32[]{:S(2)}) collective-permute-start(f32[128,128]{1,0:T(8,128)S(1)} %add_pair.1.after.t0), channel_id=1, source_target_pairs={{0,24},{4,28},{8,0},{12,4},{16,8},{20,12},{24,16},{28,20},{32,56},... | collective-permute-start | bytes 196616 | tf_op jit(solution)/shard_map/ppermute | solution.py:506
